TPU v7x, 512 devices: a whole 4x4x16 slice. The times are simulated.
512 devices in a mesh: pipe: 32 (over z, x_hi), dp: 4 (over y), mp: 4 (over x_lo, core).
Axes of the slice: x: 4 (x_hi: 2, x_lo: 2; x = x_hi * 2 + x_lo), y: 4, z: 16, core: 2. Of those that a mesh axis runs over, the one named last changes fastest.
Arguments:
- act_in: bfloat16 [32, 512, 12288], P('pipe', 'dp', 'mp'), may hold values from -30 to 30
- grad_in: bfloat16 [32, 512, 12288], P('pipe', 'dp', 'mp'), may hold values from -0.8 to 0.8
- stash_far: bfloat16 [32, 512, 12288], P('pipe', 'dp', 'mp'), may hold values from -40 to 40
- up_proj: bfloat16 [32, 12288, 192], P('pipe', 'mp', 'dp'), may hold values from -1 to 1
- down_proj: bfloat16 [32, 192, 12288], P('pipe', 'dp', 'mp'), may hold values from -2 to 2
Outputs:
- act_next: bfloat16 [32, 512, 12288], P('pipe', 'dp', 'mp')
- grad_prev: bfloat16 [32, 512, 12288], P('pipe', 'dp', 'mp')
- up_grad: bfloat16 [32, 12288, 192], P('pipe', 'mp', 'dp')
- down_grad: bfloat16 [32, 192, 12288], P('pipe', 'dp', 'mp')
All inputs are finite; a program needn't handle non-finite values.
Results may differ from a plain program's by a relative error of at most 0.03.
Values may be sent and summed in bfloat16 or wider, within the bound.
No kernel may reach another device: no remote copies, remote signals or barrier semaphores. Data moves between devices by JAX's collectives and lax.ppermute only.
A program may use at most 64 MiB of HBM per device.

v0:
```python
import jax
import jax.numpy as jnp
from jax import lax
from jax.sharding import PartitionSpec as P

D = 12288


epsilon = 1e-05


def shifted(block, axis, distance):
    devices = range(lax.axis_size(axis))
    route = [(i - distance, i) for i in devices if i - distance in devices]
    return lax.ppermute(block, axis, route)


def gated(hidden):
    sigmoid_value = jax.nn.sigmoid(hidden)
    return (hidden * sigmoid_value, sigmoid_value * (1.0 + hidden * (1.0 - sigmoid_value)))


def fetch_back(stored):
    section_count = lax.axis_size("pipe")
    row_count, feature_count = stored.shape
    pieces = stored.reshape(row_count, section_count, feature_count // section_count)
    spread = lax.all_to_all(pieces, "pipe", split_axis=1, concat_axis=1, tiled=True)
    flipped = spread[:, ::-1, :]
    gathered = lax.all_to_all(flipped, "pipe", split_axis=1, concat_axis=1, tiled=True)
    return gathered.reshape(row_count, feature_count)


def shards(act_in, grad_in, stash_far, up_proj, down_proj):
    forward_in = act_in[0]
    cotangent = grad_in[0]
    up_full, down_full = (
        lax.all_gather(up_proj[0], "dp", axis=1, tiled=True),
        lax.all_gather(down_proj[0], "dp", axis=0, tiled=True),
    )
    returned = fetch_back(stash_far[0])

    def partials(inputs):
        projected = jnp.dot(inputs, up_full, preferred_element_type=jnp.float32)
        squares = jnp.sum(jnp.square(inputs.astype(jnp.float32)), axis=1)
        return (projected, squares)

    fwd_proj_part, fwd_squares_part = partials(forward_in)
    back_proj_part, back_squares_part = partials(returned)
    grad_act_part = lax.dot_general(
        cotangent, down_full, (((1,), (1,)), ((), ())), preferred_element_type=jnp.float32
    )
    fwd_proj, fwd_squares = (
        lax.psum(fwd_proj_part.astype(jnp.bfloat16), "mp").astype(jnp.float32),
        lax.psum(fwd_squares_part.astype(jnp.bfloat16), "mp").astype(jnp.float32),
    )
    back_proj, back_squares, grad_act = (
        lax.psum(back_proj_part.astype(jnp.bfloat16), "mp").astype(jnp.float32),
        lax.psum(back_squares_part.astype(jnp.bfloat16), "mp").astype(jnp.float32),
        lax.psum(grad_act_part.astype(jnp.bfloat16), "mp").astype(jnp.float32),
    )
    fwd_scale = lax.rsqrt(fwd_squares / D + epsilon)
    activated = gated(fwd_proj * fwd_scale[:, None])[0].astype(jnp.bfloat16)
    output = (
        forward_in.astype(jnp.float32)
        + jnp.dot(activated, down_full, preferred_element_type=jnp.float32)
    ).astype(jnp.bfloat16)
    act_next = shifted(output, "pipe", 1)
    back_scale = lax.rsqrt(back_squares / D + epsilon)
    back_value, back_slope = gated(back_proj * back_scale[:, None])
    back_act = back_value.astype(jnp.bfloat16)
    grad_hidden = grad_act * back_slope
    grad_proj = (grad_hidden * back_scale[:, None]).astype(jnp.bfloat16)
    grad_scale = jnp.sum(grad_hidden * back_proj, axis=1)
    grad_input = cotangent.astype(jnp.float32) + lax.dot_general(
        grad_proj, up_full, (((1,), (1,)), ((), ())), preferred_element_type=jnp.float32
    )
    grad_input = (
        grad_input + returned.astype(jnp.float32) * (-(back_scale**3) * grad_scale / D)[:, None]
    )
    grad_prev = shifted(grad_input.astype(jnp.bfloat16), "pipe", -1)
    down_grad = lax.psum_scatter(
        lax.dot_general(
            back_act, cotangent, (((0,), (0,)), ((), ())), preferred_element_type=jnp.float32
        ).astype(jnp.bfloat16),
        "dp",
        scatter_dimension=0,
        tiled=True,
    )
    up_term = lax.dot_general(
        returned, grad_proj, (((0,), (0,)), ((), ())), preferred_element_type=jnp.float32
    )
    up_grad = lax.psum_scatter(up_term.astype(jnp.bfloat16), "dp", scatter_dimension=1, tiled=True)
    return (act_next[None], grad_prev[None], up_grad[None], down_grad[None])


def solution(mesh):
    in_specs = (
        P("pipe", "dp", "mp"),
        P("pipe", "dp", "mp"),
        P("pipe", "dp", "mp"),
        P("pipe", "mp", "dp"),
        P("pipe", "dp", "mp"),
    )
    out_specs = (
        P("pipe", "dp", "mp"),
        P("pipe", "dp", "mp"),
        P("pipe", "mp", "dp"),
        P("pipe", "dp", "mp"),
    )
    return jax.shard_map(shards, mesh=mesh, in_specs=in_specs, out_specs=out_specs, check_vma=False)
```

profile of v0, /device:TPU:4, one launch (start us, length us, event | category | flops | bytes accessed | tf_op | source)
XLA Modules:
  0.0 250.7 jit_solution(5362801552524598388)
XLA Ops:
  7.2 2.3 copy.9
  9.5 18.2 %all-to-all-start = ((bf16[128,32,96]{0,2,1:T(8,128)(2,1)}), bf16[128,32,96]{0,2,1:T(8,128)(2,1)S(1)}, u32[]{:S(2)}, u32[]{:S(2)}) async-start(bf16[128,32,96]{0,2,1:T(8,128)(2,1)} %bitcast.5), calls=%async_computation | async-start | bytes 1572864 | tf_op jit(solution)/shard_map/all_to_all | solution.py:27
  27.7 0.0 all-gather.5.cloned.1.call-start
  27.7 0.7 all-gather.5.cloned.1.call-update
  28.4 42.0 %all-to-all-done = bf16[128,32,96]{0,2,1:T(8,128)(2,1)S(1)} async-done(((bf16[128,32,96]{0,2,1:T(8,128)(2,1)}), bf16[128,32,96]{0,2,1:T(8,128)(2,1)S(1)}, u32[]{:S(2)}, u32[]{:S(2)}) %all-to-all-start) | async-done | bytes 786464 | tf_op jit(solution)/shard_map/all_to_all | solution.py:27
  70.4 0.9 rev.3
  71.3 6.5 %all-to-all-start.1 = ((bf16[128,32,96]{0,2,1:T(8,128)(2,1)}), bf16[128,32,96]{0,2,1:T(8,128)(2,1)S(1)}, u32[]{:S(2)}, u32[]{:S(2)}) async-start(bf16[128,32,96]{0,2,1:T(8,128)(2,1)} %rev.3), calls=%async_computation.1 | async-start | bytes 1572864 | tf_op jit(solution)/shard_map/all_to_all | solution.py:29
  77.9 0.0 all-gather.7.cloned.1.call-start
  77.9 0.7 all-gather.7.cloned.1.call-update
  78.6 0.0 all-reduce.3.cloned.1.call-start
  78.7 0.0 copy-done.1
  78.7 0.7 fusion.4
  79.4 2.4 fusion.13
  81.9 31.9 %all-gather.7.cloned.1.call-done = bf16[1,192,3072]{2,1,0:T(8,128)(2,1)} async-done(((bf16[1,48,3072]{2,1,0:T(8,128)(2,1)}), bf16[1,192,3072]{2,1,0:T(8,128)(2,1)}) %all-gather.7.cloned.1.call-update) | async-done | bytes 1179664 | tf_op jit(solution)/shard_map/all_gather | solution.py:38
  113.7 0.0 copy-done.2
  113.8 2.4 fusion.19
  116.1 4.4 %all-to-all-done.1 = bf16[128,32,96]{0,2,1:T(8,128)(2,1)S(1)} async-done(((bf16[128,32,96]{0,2,1:T(8,128)(2,1)}), bf16[128,32,96]{0,2,1:T(8,128)(2,1)S(1)}, u32[]{:S(2)}, u32[]{:S(2)}) %all-to-all-start.1) | async-done | bytes 786464 | tf_op jit(solution)/shard_map/all_to_all | solution.py:29
  120.5 0.9 multiply_reduce_fusion
  121.5 0.0 copy-done
  121.5 1.1 fusion.16
  122.5 0.0 all-reduce.3.cloned.1.call-update
  122.6 0.0 reduce-scatter.3.cloned.1.call-start
  122.6 47.8 %all-reduce.3.cloned.1.call-done = (bf16[128,192]{0,1:T(8,128)(2,1)}, bf16[128]{0:T(256)(128)(2,1)}, bf16[128,192]{0,1:T(8,128)(2,1)}, bf16[128]{0:T(256)(128)(2,1)}, bf16[128,192]{0,1:T(8,128)(2,1)}) async-done(((bf16[128,192]{0,1:T(8,128)(2,1)}, bf16[128]{0:T(256)(128)(2,1)}, bf16[128,192]{0,1:T(8,128)(2,1)}, bf16[128]{0:T(256)(128)(2,1)}, bf16[128,192]{0,1:T(8,128)(2,1)}), (bf16[128,192]{0,1:T(8,128)(2,1)}, ...) | async-done | bytes 147984 | tf_op jit(solution)/shard_map/psum | solution.py:53
  170.4 0.7 add_rsqrt_fusion
  171.1 2.3 fusion.3
  173.4 0.0 reduce-scatter.3.cloned.1.call-update
  173.5 0.0 reduce-scatter.5.cloned.1.call-start
  173.5 2.3 convolution_convert_fusion
  175.8 0.0 reduce-scatter.5.cloned.1.call-update
  175.8 1.2 copy.10
  177.0 0.0 copy-done.7
  177.0 0.0 copy-start.5
  177.0 0.0 copy-start.6
  177.0 0.0 copy-start.3
  177.1 1.8 fusion.2
  178.9 3.4 %collective-permute-start = (bf16[128,3072]{1,0:T(8,128)(2,1)S(1)}, bf16[128,3072]{1,0:T(8,128)(2,1)S(1)}, u32[]{:S(2)}, u32[]{:S(2)}) collective-permute-start(bf16[128,3072]{1,0:T(8,128)(2,1)S(1)} %fusion.2), channel_id=1, source_target_pairs={{0,16},{16,32},{32,48},{48,64},{64,80},{80,96},{96,112},{112,128},... | collective-permute-start | bytes 2359304 | tf_op jit(solution)/shard_map/ppermute | solution.py:15
  182.3 0.0 copy-done.4
  182.3 0.0 copy-done.5
  182.3 0.1 fusion.35
  182.4 0.0 copy-done.6
  182.4 0.0 copy-done.3
  182.4 0.6 fusion.1
  183.0 4.0 %collective-permute-start.1 = (bf16[128,3072]{1,0:T(8,128)(2,1)S(1)}, bf16[128,3072]{1,0:T(8,128)(2,1)S(1)}, u32[]{:S(2)}, u32[]{:S(2)}) collective-permute-start(bf16[128,3072]{1,0:T(8,128)(2,1)S(1)} %fusion.1), channel_id=1, source_target_pairs={{16,0},{32,16},{48,32},{64,48},{80,64},{96,80},{112,96},{128,112},... | collective-permute-start | bytes 2359304 | tf_op jit(solution)/shard_map/ppermute | solution.py:15
  187.0 31.9 %collective-permute-done = bf16[128,3072]{1,0:T(8,128)(2,1)S(1)} collective-permute-done((bf16[128,3072]{1,0:T(8,128)(2,1)S(1)}, bf16[128,3072]{1,0:T(8,128)(2,1)S(1)}, u32[]{:S(2)}, u32[]{:S(2)}) %collective-permute-start) | collective-permute-done | bytes 786464 | tf_op jit(solution)/shard_map/ppermute | solution.py:15
  218.9 0.0 collective-permute-done.1
  218.9 23.4 %reduce-scatter.5.cloned.1.call-done = bf16[48,3072]{1,0:T(8,128)(2,1)} async-done(((bf16[192,3072]{1,0:T(8,128)(2,1)}), bf16[48,3072]{1,0:T(8,128)(2,1)}) %reduce-scatter.5.cloned.1.call-update) | async-done | bytes 294928 | tf_op jit(solution)/shard_map/reduce_scatter | solution.py:81
  242.4 0.9 copy.18
  243.2 0.9 copy.19
  (9 shorter events, 0.0 us)
Async XLA Ops:
  9.5 60.9 %all-to-all-start = ((bf16[128,32,96]{0,2,1:T(8,128)(2,1)}), bf16[128,32,96]{0,2,1:T(8,128)(2,1)S(1)}, u32[]{:S(2)}, u32[]{:S(2)}) async-start(bf16[128,32,96]{0,2,1:T(8,128)(2,1)} %bitcast.5), calls=%async_computation | async-start | bytes 1572864 | tf_op jit(solution)/shard_map/all_to_all | solution.py:27
  27.7 51.8 %all-gather.5.cloned.1.call-start = ((), (), s32[]{:S(2)}) async-start(), calls=%async_computation.6 | async-start | bytes 1474560 | tf_op jit(solution)/shard_map/all_gather | solution.py:37
  71.3 7.4 %copy-start.1 = (bf16[1,128,3072]{2,1,0:T(8,128)(2,1)S(1)}, bf16[1,128,3072]{2,1,0:T(8,128)(2,1)}, u32[]{:S(2)}) copy-start(bf16[1,128,3072]{2,1,0:T(8,128)(2,1)} %param.5) | copy-start | bytes 2359300
  71.3 49.2 %all-to-all-start.1 = ((bf16[128,32,96]{0,2,1:T(8,128)(2,1)}), bf16[128,32,96]{0,2,1:T(8,128)(2,1)S(1)}, u32[]{:S(2)}, u32[]{:S(2)}) async-start(bf16[128,32,96]{0,2,1:T(8,128)(2,1)} %rev.3), calls=%async_computation.1 | async-start | bytes 1572864 | tf_op jit(solution)/shard_map/all_to_all | solution.py:29
  77.9 35.9 %all-gather.7.cloned.1.call-start = ((), (), s32[]{:S(2)}) async-start(), calls=%async_computation.7 | async-start | bytes 1474560 | tf_op jit(solution)/shard_map/all_gather | solution.py:38
  78.6 91.8 %all-reduce.3.cloned.1.call-start = ((), (), s32[]{:S(2)}) async-start(), calls=%async_computation.8 | async-start | bytes 296960 | tf_op jit(solution)/shard_map/psum | solution.py:53
  79.4 34.3 %copy-start.2 = (bf16[1,128,3072]{2,1,0:T(8,128)(2,1)S(1)}, bf16[1,128,3072]{2,1,0:T(8,128)(2,1)}, u32[]{:S(2)}) copy-start(bf16[1,128,3072]{2,1,0:T(8,128)(2,1)} %param.6) | copy-start | bytes 2359300
  81.9 39.6 %copy-start = (bf16[1,3072,192]{1,2,0:T(8,128)(2,1)S(1)}, bf16[1,3072,192]{1,2,0:T(8,128)(2,1)}, u32[]{:S(2)}) copy-start(bf16[1,3072,192]{1,2,0:T(8,128)(2,1)} %all-gather.5.cloned.1.call-done) | copy-start | bytes 3538948
  122.6 96.4 %reduce-scatter.3.cloned.1.call-start = ((), (), s32[]{:S(2)}) async-start(), calls=%async_computation.4 | async-start | bytes 1474560 | tf_op jit(solution)/shard_map/reduce_scatter | solution.py:92
  173.5 68.9 %reduce-scatter.5.cloned.1.call-start = ((), (), s32[]{:S(2)}) async-start(), calls=%async_computation.5 | async-start | bytes 1474560 | tf_op jit(solution)/shard_map/reduce_scatter | solution.py:81
  175.8 1.2 copy-start.7
  177.0 5.3 %copy-start.4 = (bf16[128,192]{0,1:T(8,128)(2,1)S(1)}, bf16[128,192]{0,1:T(8,128)(2,1)}, u32[]{:S(2)}) copy-start(bf16[128,192]{0,1:T(8,128)(2,1)} %get-tuple-element.6) | copy-start | bytes 147460
  177.0 5.3 %copy-start.5 = (bf16[128,192]{0,1:T(8,128)(2,1)S(1)}, bf16[128,192]{0,1:T(8,128)(2,1)}, u32[]{:S(2)}) copy-start(bf16[128,192]{0,1:T(8,128)(2,1)} %get-tuple-element.8) | copy-start | bytes 147460
  177.0 5.4 %copy-start.6 = (bf16[128]{0:T(256)(128)(2,1)S(1)}, bf16[128]{0:T(256)(128)(2,1)}, u32[]{:S(2)}) copy-start(bf16[128]{0:T(256)(128)(2,1)} %get-tuple-element.7) | copy-start | bytes 772
  177.0 5.4 %copy-start.3 = (bf16[128,3072]{1,0:T(8,128)(2,1)S(1)}, bf16[128,3072]{1,0:T(8,128)(2,1)}, u32[]{:S(2)}) copy-start(bf16[128,3072]{1,0:T(8,128)(2,1)} %copy.10) | copy-start | bytes 2359300
  178.9 40.1 %collective-permute-start = (bf16[128,3072]{1,0:T(8,128)(2,1)S(1)}, bf16[128,3072]{1,0:T(8,128)(2,1)S(1)}, u32[]{:S(2)}, u32[]{:S(2)}) collective-permute-start(bf16[128,3072]{1,0:T(8,128)(2,1)S(1)} %fusion.2), channel_id=1, source_target_pairs={{0,16},{16,32},{32,48},{48,64},{64,80},{80,96},{96,112},{112,128},... | collective-permute-start | bytes 2359304 | tf_op jit(solution)/shard_map/ppermute | solution.py:15
  183.0 35.9 %collective-permute-start.1 = (bf16[128,3072]{1,0:T(8,128)(2,1)S(1)}, bf16[128,3072]{1,0:T(8,128)(2,1)S(1)}, u32[]{:S(2)}, u32[]{:S(2)}) collective-permute-start(bf16[128,3072]{1,0:T(8,128)(2,1)S(1)} %fusion.1), channel_id=1, source_target_pairs={{16,0},{32,16},{48,32},{64,48},{80,64},{96,80},{112,96},{128,112},... | collective-permute-start | bytes 2359304 | tf_op jit(solution)/shard_map/ppermute | solution.py:15
Sparse Core Ops, SparseCore 0:
  30.6 32.8 all-gather.4
  80.8 32.8 all-gather.6
  122.7 47.7 all-reduce.2
  174.0 33.1 reduce-scatter.2
  210.7 31.6 reduce-scatter.4
where the time goes:
time: 251 us
  waiting for transfers between devices  183 us (73%)
  starting transfers between devices  32.3 us (13%)
  between operations  13.9 us (6%)
  matrix products  12.9 us (5%)
  local copies, waits for them, and re-layouts  6.17 us (2%)
    psum x1, waiting for transfers between devices, shards(): lax.psum(fwd_proj_part.astype(jnp.bfloat16), 'mp').astype(jnp.float32)  47.8 us
    all_to_all x1, waiting for transfers between devices, fetch_back(): lax.all_to_all(pieces, 'pipe', split_axis=1, concat_axis=1, tiled=True)  42 us
    ppermute x2, waiting for transfers between devices, shifted(): return lax.ppermute(block, axis, route)  31.9 us
    all_gather x1, waiting for transfers between devices, shards(): lax.all_gather(down_proj[0], 'dp', axis=0, tiled=True)  31.9 us
    reduce_scatter x1, waiting for transfers between devices, shards(): lax.psum_scatter(lax.dot_general(back_act, cotangent, (((0,), (0,)), ((),...  23.4 us
    all_to_all x1, starting transfers between devices, fetch_back(): lax.all_to_all(pieces, 'pipe', split_axis=1, concat_axis=1, tiled=True)  18.2 us
    ppermute x2, starting transfers between devices, shifted(): return lax.ppermute(block, axis, route)  7.39 us
    all_to_all x1, starting transfers between devices, fetch_back(): lax.all_to_all(flipped, 'pipe', split_axis=1, concat_axis=1, tiled=True)  6.54 us
  transfers between devices with their start and end apart: 9, of which 6 were waited for; matrix products, arithmetic and copies ran while one was open for 5% of the time, Pallas kernels for 0%

commit v1 on v0

v1 whole, which is shorter than its diff:
```python
import jax
import jax.numpy as jnp
from jax import lax
from jax.sharding import PartitionSpec as P

D = 12288


epsilon = 1e-05


def shifted(block, axis, distance):
    devices = range(lax.axis_size(axis))
    route = [(i - distance, i) for i in devices if i - distance in devices]
    return lax.ppermute(block, axis, route)


def mirrored(block, axis):
    last = lax.axis_size(axis) - 1
    return lax.ppermute(block, axis, [(i, last - i) for i in range(last + 1)])


def spread(block, axis):
    copies = jnp.broadcast_to(block[None], (lax.axis_size(axis),) + block.shape)
    return lax.all_to_all(copies, axis, split_axis=0, concat_axis=0, tiled=True)


def summed(block, axis):
    return jnp.sum(spread(block, axis).astype(jnp.float32), axis=0)


def dot(left, right, left_dim, right_dim):
    return lax.dot_general(
        left, right, (((left_dim,), (right_dim,)), ((), ())), preferred_element_type=jnp.float32
    )


def gated(hidden):
    sigmoid_value = jax.nn.sigmoid(hidden)
    return (hidden * sigmoid_value, sigmoid_value * (1.0 + hidden * (1.0 - sigmoid_value)))


def square_rows(inputs):
    squares = jnp.sum(jnp.square(inputs.astype(jnp.float32)), axis=1)
    return jnp.broadcast_to(squares[None], (16, inputs.shape[0]))


def shards(act_in, grad_in, stash_far, up_proj, down_proj):
    forward_in = act_in[0]
    cotangent = grad_in[0]
    group = lax.axis_size("dp")
    rows, features = forward_in.shape
    returned = mirrored(stash_far[0], "pipe")
    up_full = spread(up_proj[0].T, "dp").reshape(-1, features)
    down_full = spread(down_proj[0], "dp").reshape(-1, features)
    rank = up_full.shape[0]
    cotangent_all = spread(cotangent, "dp")

    first = jnp.concatenate(
        [dot(up_full, forward_in, 1, 1), dot(down_full, cotangent, 1, 1), square_rows(forward_in)]
    )
    first = summed(first.astype(jnp.bfloat16), "mp")
    fwd_proj, grad_act, fwd_squares = first[:rank], first[rank : 2 * rank], first[2 * rank]
    fwd_scale = lax.rsqrt(fwd_squares / D + epsilon)
    activated = gated(fwd_proj * fwd_scale[None])[0].astype(jnp.bfloat16)
    output = forward_in.astype(jnp.float32) + dot(activated, down_full, 0, 0)
    act_next = shifted(output.astype(jnp.bfloat16), "pipe", 1)

    second = jnp.concatenate([dot(up_full, returned, 1, 1), square_rows(returned)])
    second = summed(second.astype(jnp.bfloat16), "mp")
    back_proj, back_squares = second[:rank], second[rank]
    back_scale = lax.rsqrt(back_squares / D + epsilon)
    back_value, back_slope = gated(back_proj * back_scale[None])
    back_act = back_value.astype(jnp.bfloat16)
    grad_hidden = grad_act * back_slope
    grad_proj = (grad_hidden * back_scale[None]).astype(jnp.bfloat16)
    grad_scale = jnp.sum(grad_hidden * back_proj, axis=0)
    pull = -(back_scale**3) * grad_scale / D
    grad_input = cotangent.astype(jnp.float32) + dot(grad_proj, up_full, 0, 0)
    grad_input = grad_input + returned.astype(jnp.float32) * pull[:, None]
    grad_prev = shifted(grad_input.astype(jnp.bfloat16), "pipe", -1)

    up_term = dot(grad_proj, returned, 1, 0).astype(jnp.bfloat16)
    up_terms = lax.all_to_all(
        up_term.reshape(group, -1, features), "dp", split_axis=0, concat_axis=0, tiled=True
    )
    up_grad = jnp.sum(up_terms.astype(jnp.float32), axis=0).astype(jnp.bfloat16)
    own_act = lax.all_to_all(
        back_act.reshape(group, -1, rows), "dp", split_axis=0, concat_axis=0, tiled=True
    )
    down_grad = lax.dot_general(
        own_act, cotangent_all, (((0, 2), (0, 1)), ((), ())), preferred_element_type=jnp.float32
    ).astype(jnp.bfloat16)
    return (act_next[None], grad_prev[None], up_grad.T[None], down_grad[None])


def solution(mesh):
    in_specs = (
        P("pipe", "dp", "mp"),
        P("pipe", "dp", "mp"),
        P("pipe", "dp", "mp"),
        P("pipe", "mp", "dp"),
        P("pipe", "dp", "mp"),
    )
    out_specs = (
        P("pipe", "dp", "mp"),
        P("pipe", "dp", "mp"),
        P("pipe", "mp", "dp"),
        P("pipe", "dp", "mp"),
    )
    return jax.shard_map(shards, mesh=mesh, in_specs=in_specs, out_specs=out_specs, check_vma=False)
```

time: 251 us -> 197 us (0.78)
  the two profiles are of different devices: /device:TPU:4 before, /device:TPU:13 now
where the time goes in v1:
time: 197 us; the launch traced here: 195 us
  waiting for transfers between devices  100 us (51%)
  starting transfers between devices  46.8 us (24%)
  blocking collectives  18.7 us (9%)
  matrix products  11.1 us (6%)
  local copies, waits for them, and re-layouts  10.6 us (5%)
  other arithmetic  7.08 us (4%)
    ppermute x1, waiting for transfers between devices, mirrored(): return lax.ppermute(block, axis, [(i, last - i) for i in range(last + 1)])  57.7 us
    ppermute x2, waiting for transfers between devices, shifted(): return lax.ppermute(block, axis, route)  30.8 us
    all_to_all x5, starting transfers between devices, spread(): return lax.all_to_all(copies, axis, split_axis=0, concat_axis=0, tiled=True)  23.8 us
    all_to_all x1, blocking collectives, shards(): lax.all_to_all(up_term.reshape(group, -1, features), 'dp', split_axis=0,...  18.7 us
    ppermute x1, starting transfers between devices, mirrored(): return lax.ppermute(block, axis, [(i, last - i) for i in range(last + 1)])  11.1 us
    all_to_all x5, waiting for transfers between devices, spread(): return lax.all_to_all(copies, axis, split_axis=0, concat_axis=0, tiled=True)  10.9 us
    dot_general x6, matrix products, dot(): lax.dot_general(left, right, (((left_dim,), (right_dim,)), ((), ())), pre...  7.85 us
    ppermute x2, starting transfers between devices, shifted(): return lax.ppermute(block, axis, route)  7.69 us
  transfers between devices with their start and end apart: 9, of which 7 were waited for; matrix products, arithmetic and copies ran while one was open for 7% of the time, Pallas kernels for 0%

profile of v1, /device:TPU:13, one launch (start us, length us, event | category | flops | bytes accessed | tf_op | source)
XLA Modules:
  0.0 195.5 jit_solution(17330859882210580057)
XLA Ops:
  0.6 2.1 %broadcast_in_dim.24 = bf16[4,48,3072]{2,1,0:T(8,128)(2,1)} broadcast(bf16[48,3072]{1,0:T(8,128)(2,1)} %bitcast.55), dimensions={1,2} | broadcast | bytes 1474560 | tf_op jit(solution)/shard_map/broadcast_in_dim | solution.py:24
  2.7 4.5 %all-to-all-start = ((bf16[4,48,3072]{2,1,0:T(8,128)(2,1)}), bf16[4,48,3072]{2,1,0:T(8,128)(2,1)S(1)}, u32[]{:S(2)}, u32[]{:S(2)}) async-start(bf16[4,48,3072]{2,1,0:T(8,128)(2,1)} %broadcast_in_dim.24), calls=%async_computation | async-start | bytes 2359296 | tf_op jit(solution)/shard_map/all_to_all | solution.py:25
  7.2 11.1 %collective-permute-start.1 = (bf16[128,3072]{1,0:T(8,128)(2,1)}, bf16[128,3072]{1,0:T(8,128)(2,1)S(1)}, u32[]{:S(2)}, u32[]{:S(2)}) collective-permute-start(bf16[128,3072]{1,0:T(8,128)(2,1)} %bitcast.9), channel_id=1, source_target_pairs={{0,496},{16,480},{32,464},{48,448},{64,432},{80,416},{96,400},{112... | collective-permute-start | bytes 2359304 | tf_op jit(solution)/shard_map/ppermute | solution.py:20
  18.3 3.3 %all-to-all-done = bf16[4,48,3072]{2,1,0:T(8,128)(2,1)S(1)} async-done(((bf16[4,48,3072]{2,1,0:T(8,128)(2,1)}), bf16[4,48,3072]{2,1,0:T(8,128)(2,1)S(1)}, u32[]{:S(2)}, u32[]{:S(2)}) %all-to-all-start) | async-done | bytes 1179680 | tf_op jit(solution)/shard_map/all_to_all | solution.py:25
  21.6 1.1 broadcast_in_dim.26
  22.8 4.7 %all-to-all-start.1 = ((bf16[4,48,3072]{2,1,0:T(8,128)(2,1)}), bf16[4,48,3072]{2,1,0:T(8,128)(2,1)S(1)}, u32[]{:S(2)}, u32[]{:S(2)}) async-start(bf16[4,48,3072]{2,1,0:T(8,128)(2,1)} %broadcast_in_dim.26), calls=%async_computation.1 | async-start | bytes 2359296 | tf_op jit(solution)/shard_map/all_to_all | solution.py:25
  27.5 1.4 fusion.3
  28.8 57.7 %collective-permute-done.1 = bf16[128,3072]{1,0:T(8,128)(2,1)S(1)} collective-permute-done((bf16[128,3072]{1,0:T(8,128)(2,1)}, bf16[128,3072]{1,0:T(8,128)(2,1)S(1)}, u32[]{:S(2)}, u32[]{:S(2)}) %collective-permute-start.1) | collective-permute-done | bytes 786464 | tf_op jit(solution)/shard_map/ppermute | solution.py:20
  86.5 0.2 fusion.4
  86.8 0.5 convolution_convert_fusion.1
  87.3 0.6 copy-done
  87.9 0.5 convolution_convert_fusion.3
  88.4 0.0 all-to-all-done.1
  88.4 0.7 broadcast_in_dim.31
  89.1 4.4 %all-to-all-start.3 = ((bf16[4,208,128]{2,1,0:T(8,128)(2,1)}), bf16[4,208,128]{2,1,0:T(8,128)(2,1)S(1)}, u32[]{:S(2)}, u32[]{:S(2)}) async-start(bf16[4,208,128]{2,1,0:T(8,128)(2,1)} %broadcast_in_dim.31), calls=%async_computation.3 | async-start | bytes 425984 | tf_op jit(solution)/shard_map/all_to_all | solution.py:25
  93.5 1.6 convolution_convert_fusion.2
  95.1 2.9 %all-to-all-done.3 = bf16[4,208,128]{2,1,0:T(8,128)(2,1)S(1)} async-done(((bf16[4,208,128]{2,1,0:T(8,128)(2,1)}), bf16[4,208,128]{2,1,0:T(8,128)(2,1)S(1)}, u32[]{:S(2)}, u32[]{:S(2)}) %all-to-all-start.3) | async-done | bytes 213024 | tf_op jit(solution)/shard_map/all_to_all | solution.py:25
  98.0 0.8 broadcast_in_dim.28
  98.9 4.4 %all-to-all-start.2 = ((bf16[4,400,128]{2,1,0:T(8,128)(2,1)}), bf16[4,400,128]{2,1,0:T(8,128)(2,1)S(1)}, u32[]{:S(2)}, u32[]{:S(2)}) async-start(bf16[4,400,128]{2,1,0:T(8,128)(2,1)} %broadcast_in_dim.28), calls=%async_computation.2 | async-start | bytes 819200 | tf_op jit(solution)/shard_map/all_to_all | solution.py:25
  103.2 1.0 convert_reduce_fusion.1
  104.2 0.0 copy-start.6
  104.2 0.6 copy-done.6
  104.9 0.5 fusion.14
  105.4 4.6 %all-to-all-done.2 = bf16[4,400,128]{2,1,0:T(8,128)(2,1)S(1)} async-done(((bf16[4,400,128]{2,1,0:T(8,128)(2,1)}), bf16[4,400,128]{2,1,0:T(8,128)(2,1)S(1)}, u32[]{:S(2)}, u32[]{:S(2)}) %all-to-all-start.2) | async-done | bytes 409632 | tf_op jit(solution)/shard_map/all_to_all | solution.py:25
  110.0 0.1 convert_reduce_fusion
  110.1 0.0 copy-start.5
  110.1 0.7 copy-done.5
  110.7 1.6 multiply_reduce_fusion
  112.3 4.2 %all-to-all-start.5 = ((bf16[4,48,128]{2,1,0:T(8,128)(2,1)}), bf16[4,48,128]{2,1,0:T(8,128)(2,1)S(1)}, u32[]{:S(2)}, u32[]{:S(2)}) async-start(bf16[4,48,128]{2,1,0:T(8,128)(2,1)} %bitcast.15), calls=%async_computation.5 | async-start | bytes 98304 | tf_op jit(solution)/shard_map/all_to_all | solution.py:88
  116.5 2.1 %convolution_convert_fusion = bf16[192,3072]{1,0:T(8,128)(2,1)} fusion(bf16[128,3072]{1,0:T(8,128)(2,1)S(1)} %collective-permute-done.1, f32[192,128]{1,0:T(8,128)S(1)} %get-tuple-element.5, f32[128]{0:T(128)} %fusion.14), kind=kOutput, calls=%fused_computation | convolution fusion | flops 151633920 | bytes 2064896 | tf_op jit(solution)/shard_map/dot_general | solution.py:33
  118.7 1.1 all-to-all-done.5
  119.8 18.7 %all_to_all.35 = bf16[4,48,3072]{2,1,0:T(8,128)(2,1)} all-to-all(bf16[4,48,3072]{2,1,0:T(8,128)(2,1)} %bitcast.52), channel_id=1, replica_groups=mesh['pipe'=32,'dp'=4,'mp'=4] {'dp'}, dimensions={0} | all-to-all | bytes 2359296 | tf_op jit(solution)/shard_map/all_to_all | solution.py:84
  138.4 2.1 %broadcast_in_dim.68 = bf16[4,128,3072]{2,1,0:T(8,128)(2,1)} broadcast(bf16[128,3072]{1,0:T(8,128)(2,1)S(1)} %bitcast.51), dimensions={1,2} | broadcast | bytes 3932160 | tf_op jit(solution)/shard_map/broadcast_in_dim | solution.py:24
  140.5 5.9 %all-to-all-start.6 = ((bf16[4,128,3072]{2,1,0:T(8,128)(2,1)}), bf16[4,128,3072]{2,1,0:T(8,128)(2,1)}, u32[]{:S(2)}, u32[]{:S(2)}) async-start(bf16[4,128,3072]{2,1,0:T(8,128)(2,1)} %broadcast_in_dim.68), calls=%async_computation.6 | async-start | bytes 6291456 | tf_op jit(solution)/shard_map/all_to_all | solution.py:25
  146.4 0.7 fusion.18
  147.1 1.8 fusion.6
  148.9 4.6 %collective-permute-start.2 = (bf16[128,3072]{1,0:T(8,128)(2,1)S(1)}, bf16[128,3072]{1,0:T(8,128)(2,1)S(1)}, u32[]{:S(2)}, u32[]{:S(2)}) collective-permute-start(bf16[128,3072]{1,0:T(8,128)(2,1)S(1)} %fusion.6), channel_id=1, source_target_pairs={{16,0},{32,16},{48,32},{64,48},{80,64},{96,80},{112,96},{128,112},... | collective-permute-start | bytes 2359304 | tf_op jit(solution)/shard_map/ppermute | solution.py:15
  153.5 0.7 fusion.17
  154.2 0.0 copy-done.1
  154.2 1.4 fusion
  155.7 3.0 %collective-permute-start = (bf16[128,3072]{1,0:T(8,128)(2,1)S(1)}, bf16[128,3072]{1,0:T(8,128)(2,1)S(1)}, u32[]{:S(2)}, u32[]{:S(2)}) collective-permute-start(bf16[128,3072]{1,0:T(8,128)(2,1)S(1)} %fusion), channel_id=1, source_target_pairs={{0,16},{16,32},{32,48},{48,64},{64,80},{80,96},{96,112},{112,128},... | collective-permute-start | bytes 2359304 | tf_op jit(solution)/shard_map/ppermute | solution.py:15
  158.7 10.1 %collective-permute-done.2 = bf16[128,3072]{1,0:T(8,128)(2,1)S(1)} collective-permute-done((bf16[128,3072]{1,0:T(8,128)(2,1)S(1)}, bf16[128,3072]{1,0:T(8,128)(2,1)S(1)}, u32[]{:S(2)}, u32[]{:S(2)}) %collective-permute-start.2) | collective-permute-done | bytes 786464 | tf_op jit(solution)/shard_map/ppermute | solution.py:15
  168.8 20.7 %collective-permute-done = bf16[128,3072]{1,0:T(8,128)(2,1)S(1)} collective-permute-done((bf16[128,3072]{1,0:T(8,128)(2,1)S(1)}, bf16[128,3072]{1,0:T(8,128)(2,1)S(1)}, u32[]{:S(2)}, u32[]{:S(2)}) %collective-permute-start) | collective-permute-done | bytes 786464 | tf_op jit(solution)/shard_map/ppermute | solution.py:15
  189.5 1.0 reduce_sum.62
  190.5 0.0 all-to-all-done.6
  190.5 3.3 %fusion.2 = bf16[1,48,3072]{2,1,0:T(8,128)(2,1)} fusion(bf16[4,48,128]{2,1,0:T(8,128)(2,1)S(1)} %all-to-all-done.5, bf16[4,128,3072]{2,1,0:T(8,128)(2,1)} %all-to-all-done.6), kind=kOutput, calls=%fused_computation.6 | convolution fusion | flops 151142400 | bytes 3489792 | tf_op jit(solution)/shard_map/dot_general | solution.py:91
  193.7 0.9 copy.11
  194.6 0.9 copy.12
  (16 shorter events, 0.0 us)
Async XLA Ops:
  2.7 18.9 %copy-start.7 = (bf16[1,48,3072]{2,1,0:T(8,128)(2,1)S(1)}, bf16[1,48,3072]{2,1,0:T(8,128)(2,1)}, u32[]{:S(2)}) copy-start(bf16[1,48,3072]{2,1,0:T(8,128)(2,1)} %param.9) | copy-start | bytes 884740
  2.7 18.9 %all-to-all-start = ((bf16[4,48,3072]{2,1,0:T(8,128)(2,1)}), bf16[4,48,3072]{2,1,0:T(8,128)(2,1)S(1)}, u32[]{:S(2)}, u32[]{:S(2)}) async-start(bf16[4,48,3072]{2,1,0:T(8,128)(2,1)} %broadcast_in_dim.24), calls=%async_computation | async-start | bytes 2359296 | tf_op jit(solution)/shard_map/all_to_all | solution.py:25
  7.2 79.3 %collective-permute-start.1 = (bf16[128,3072]{1,0:T(8,128)(2,1)}, bf16[128,3072]{1,0:T(8,128)(2,1)S(1)}, u32[]{:S(2)}, u32[]{:S(2)}) collective-permute-start(bf16[128,3072]{1,0:T(8,128)(2,1)} %bitcast.9), channel_id=1, source_target_pairs={{0,496},{16,480},{32,464},{48,448},{64,432},{80,416},{96,400},{112... | collective-permute-start | bytes 2359304 | tf_op jit(solution)/shard_map/ppermute | solution.py:20
  22.8 65.6 %all-to-all-start.1 = ((bf16[4,48,3072]{2,1,0:T(8,128)(2,1)}), bf16[4,48,3072]{2,1,0:T(8,128)(2,1)S(1)}, u32[]{:S(2)}, u32[]{:S(2)}) async-start(bf16[4,48,3072]{2,1,0:T(8,128)(2,1)} %broadcast_in_dim.26), calls=%async_computation.1 | async-start | bytes 2359296 | tf_op jit(solution)/shard_map/all_to_all | solution.py:25
  86.8 1.1 copy-start
  89.1 8.9 %all-to-all-start.3 = ((bf16[4,208,128]{2,1,0:T(8,128)(2,1)}), bf16[4,208,128]{2,1,0:T(8,128)(2,1)S(1)}, u32[]{:S(2)}, u32[]{:S(2)}) async-start(bf16[4,208,128]{2,1,0:T(8,128)(2,1)} %broadcast_in_dim.31), calls=%async_computation.3 | async-start | bytes 425984 | tf_op jit(solution)/shard_map/all_to_all | solution.py:25
  98.0 0.8 copy-start.4
  98.9 11.1 %all-to-all-start.2 = ((bf16[4,400,128]{2,1,0:T(8,128)(2,1)}), bf16[4,400,128]{2,1,0:T(8,128)(2,1)S(1)}, u32[]{:S(2)}, u32[]{:S(2)}) async-start(bf16[4,400,128]{2,1,0:T(8,128)(2,1)} %broadcast_in_dim.28), calls=%async_computation.2 | async-start | bytes 819200 | tf_op jit(solution)/shard_map/all_to_all | solution.py:25
  104.2 0.6 copy-start.6
  110.1 0.7 copy-start.5
  112.3 7.4 %all-to-all-start.5 = ((bf16[4,48,128]{2,1,0:T(8,128)(2,1)}), bf16[4,48,128]{2,1,0:T(8,128)(2,1)S(1)}, u32[]{:S(2)}, u32[]{:S(2)}) async-start(bf16[4,48,128]{2,1,0:T(8,128)(2,1)} %bitcast.15), calls=%async_computation.5 | async-start | bytes 98304 | tf_op jit(solution)/shard_map/all_to_all | solution.py:88
  119.8 18.7 %copy-start.2 = (bf16[1,128,3072]{2,1,0:T(8,128)(2,1)S(1)}, bf16[1,128,3072]{2,1,0:T(8,128)(2,1)}, u32[]{:S(2)}) copy-start(bf16[1,128,3072]{2,1,0:T(8,128)(2,1)} %param.6) | copy-start | bytes 2359300
  140.5 6.6 %copy-start.8 = (f32[128]{0:T(128)S(1)}, f32[128]{0:T(128)}, u32[]{:S(2)}) copy-start(f32[128]{0:T(128)} %fusion.14) | copy-start | bytes 1540
  140.5 50.0 %all-to-all-start.6 = ((bf16[4,128,3072]{2,1,0:T(8,128)(2,1)}), bf16[4,128,3072]{2,1,0:T(8,128)(2,1)}, u32[]{:S(2)}, u32[]{:S(2)}) async-start(bf16[4,128,3072]{2,1,0:T(8,128)(2,1)} %broadcast_in_dim.68), calls=%async_computation.6 | async-start | bytes 6291456 | tf_op jit(solution)/shard_map/all_to_all | solution.py:25
  147.1 7.1 %copy-start.1 = (bf16[1,128,3072]{2,1,0:T(8,128)(2,1)S(1)}, bf16[1,128,3072]{2,1,0:T(8,128)(2,1)}, u32[]{:S(2)}) copy-start(bf16[1,128,3072]{2,1,0:T(8,128)(2,1)} %param.5) | copy-start | bytes 2359300
  148.9 19.9 %collective-permute-start.2 = (bf16[128,3072]{1,0:T(8,128)(2,1)S(1)}, bf16[128,3072]{1,0:T(8,128)(2,1)S(1)}, u32[]{:S(2)}, u32[]{:S(2)}) collective-permute-start(bf16[128,3072]{1,0:T(8,128)(2,1)S(1)} %fusion.6), channel_id=1, source_target_pairs={{16,0},{32,16},{48,32},{64,48},{80,64},{96,80},{112,96},{128,112},... | collective-permute-start | bytes 2359304 | tf_op jit(solution)/shard_map/ppermute | solution.py:15
  154.2 35.3 %copy-start.3 = (bf16[4,48,3072]{2,1,0:T(8,128)(2,1)S(1)}, bf16[4,48,3072]{2,1,0:T(8,128)(2,1)}, u32[]{:S(2)}) copy-start(bf16[4,48,3072]{2,1,0:T(8,128)(2,1)} %all_to_all.35) | copy-start | bytes 3538948
  155.7 33.9 %collective-permute-start = (bf16[128,3072]{1,0:T(8,128)(2,1)S(1)}, bf16[128,3072]{1,0:T(8,128)(2,1)S(1)}, u32[]{:S(2)}, u32[]{:S(2)}) collective-permute-start(bf16[128,3072]{1,0:T(8,128)(2,1)S(1)} %fusion), channel_id=1, source_target_pairs={{0,16},{16,32},{32,48},{48,64},{64,80},{80,96},{96,112},{112,128},... | collective-permute-start | bytes 2359304 | tf_op jit(solution)/shard_map/ppermute | solution.py:15

commit v2 on v1

v2 whole, which is shorter than its diff:
```python
import jax
import jax.numpy as jnp
from jax import lax
from jax.sharding import PartitionSpec as P

D = 12288


epsilon = 1e-05


def shifted(block, axis, distance):
    devices = range(lax.axis_size(axis))
    route = [(i - distance, i) for i in devices if i - distance in devices]
    return lax.ppermute(block, axis, route)


def near_sections(count):
    planes = count // 2
    return [i for i in range(count) if min((2 * (i // 2) + 1) % planes, -(2 * (i // 2) + 1) % planes) <= 3]


def spread(block, axis):
    copies = jnp.broadcast_to(block[None], (lax.axis_size(axis),) + block.shape)
    return lax.all_to_all(copies, axis, split_axis=0, concat_axis=0, tiled=True)


def summed(block, axis):
    return jnp.sum(spread(block, axis).astype(jnp.float32), axis=0)


def from_next(block, axis, distance):
    size = lax.axis_size(axis)
    return lax.ppermute(block, axis, [((i + distance) % size, i) for i in range(size)])


def ring(block, axis):
    return [block] + [from_next(block, axis, k) for k in range(1, lax.axis_size(axis))]


def dot(left, right, left_dim, right_dim):
    return lax.dot_general(
        left, right, (((left_dim,), (right_dim,)), ((), ())), preferred_element_type=jnp.float32
    )


def gated(hidden):
    sigmoid_value = jax.nn.sigmoid(hidden)
    return (hidden * sigmoid_value, sigmoid_value * (1.0 + hidden * (1.0 - sigmoid_value)))


def square_rows(inputs):
    squares = jnp.sum(jnp.square(inputs.astype(jnp.float32)), axis=1)
    return jnp.broadcast_to(squares[None], (16, inputs.shape[0]))


def staged(axis, step, *args):
    shapes = jax.eval_shape(step, *args)
    empty = lambda *_: jax.tree.map(lambda leaf: jnp.zeros(leaf.shape, leaf.dtype), shapes)
    return lax.cond(lax.axis_index(axis) < lax.axis_size(axis), step, empty, *args)


def forward(forward_in, cotangent, up_full, down_full):
    rank = up_full.shape[0]
    first = jnp.concatenate(
        [dot(up_full, forward_in, 1, 1), dot(down_full, cotangent, 1, 1), square_rows(forward_in)]
    )
    first = sum(part.astype(jnp.float32) for part in ring(first.astype(jnp.bfloat16), "mp"))
    fwd_proj, grad_act, fwd_squares = first[:rank], first[rank : 2 * rank], first[2 * rank]
    fwd_scale = lax.rsqrt(fwd_squares / D + epsilon)
    activated = gated(fwd_proj * fwd_scale[None])[0].astype(jnp.bfloat16)
    output = forward_in.astype(jnp.float32) + dot(activated, down_full, 0, 0)
    output = output.astype(jnp.bfloat16)
    middle = lax.axis_size("pipe") // 2
    act_next = lax.ppermute(output, "pipe", [(i - 1, i) for i in range(1, 2 * middle) if i != middle])
    return act_next, output, grad_act


def forward(forward_in, cotangent, up_full, down_full):
    rank = up_full.shape[0]
    first = jnp.concatenate(
        [dot(up_full, forward_in, 1, 1), dot(down_full, cotangent, 1, 1), square_rows(forward_in)]
    )
    first = sum(part.astype(jnp.float32) for part in ring(first.astype(jnp.bfloat16), "mp"))
    fwd_proj, grad_act, fwd_squares = first[:rank], first[rank : 2 * rank], first[2 * rank]
    fwd_scale = lax.rsqrt(fwd_squares / D + epsilon)
    activated = gated(fwd_proj * fwd_scale[None])[0].astype(jnp.bfloat16)
    output = forward_in.astype(jnp.float32) + dot(activated, down_full, 0, 0)
    output = output.astype(jnp.bfloat16)
    middle = lax.axis_size("pipe") // 2
    act_next = lax.ppermute(output, "pipe", [(i - 1, i) for i in range(1, 2 * middle) if i != middle])
    return act_next, output, grad_act


def gathered(up_proj, down_proj):
    own_rank = down_proj.shape[0]
    weights = ring(jnp.concatenate([up_proj, down_proj]), "dp")
    return (
        jnp.concatenate([w[:own_rank] for w in weights]),
        jnp.concatenate([w[own_rank:] for w in weights]),
    )


def ahead(forward_in, cotangent, up_proj, down_proj, stash):
    own_rank, features = down_proj.shape
    near = near_sections(lax.axis_size("pipe"))
    last = lax.axis_size("pipe") - 1
    crossed = lax.ppermute(stash, "pipe", [(i, i ^ 1) for i in near])
    weights = spread(jnp.concatenate([up_proj, down_proj]), "dp")
    weights, cotangent_sent, crossed = lax.optimization_barrier((weights, cotangent, crossed))
    returned = lax.ppermute(crossed, "pipe", [(i ^ 1, last - i) for i in near])
    cotangents = spread(cotangent_sent, "dp")
    up_full = weights[:, :own_rank].reshape(-1, features)
    down_full = weights[:, own_rank:].reshape(-1, features)
    act_next, output, grad_act = staged("mp", forward, forward_in, cotangent, up_full, down_full)
    return act_next, output, grad_act, up_full, cotangents, returned


def backward(returned, cotangent, up_full, grad_act):
    rank = up_full.shape[0]
    second = jnp.concatenate([dot(up_full, returned, 1, 1), square_rows(returned)])
    second = summed(second.astype(jnp.bfloat16), "mp")
    back_proj, back_squares = second[:rank], second[rank]
    back_scale = lax.rsqrt(back_squares / D + epsilon)
    back_value, back_slope = gated(back_proj * back_scale[None])
    back_act = back_value.astype(jnp.bfloat16)
    grad_hidden = grad_act * back_slope
    grad_proj = (grad_hidden * back_scale[None]).astype(jnp.bfloat16)
    grad_scale = jnp.sum(grad_hidden * back_proj, axis=0)
    pull = -(back_scale**3) * grad_scale / D
    grad_input = cotangent.astype(jnp.float32) + dot(grad_proj, up_full, 0, 0)
    grad_input = grad_input + returned.astype(jnp.float32) * pull[:, None]
    up_terms = dot(grad_proj, returned, 1, 0).astype(jnp.bfloat16)
    terms = jnp.concatenate([up_terms, back_act], 1)
    return grad_input.astype(jnp.bfloat16), terms.reshape(lax.axis_size("dp"), -1, terms.shape[1])


def shards(act_in, grad_in, stash_far, up_proj, down_proj):
    forward_in = act_in[0]
    cotangent = grad_in[0]
    rows, features = cotangent.shape
    group = lax.axis_size("dp")
    sections = lax.axis_size("pipe")
    far = [i for i in range(sections) if i not in near_sections(sections)]
    returned = lax.ppermute(stash_far[0], "pipe", [(i, sections - 1 - i) for i in far])
    act_next, output, grad_act, up_full, cotangents, returned_near = staged(
        "dp", ahead, forward_in, cotangent, up_proj[0].T, down_proj[0], stash_far[0]
    )
    middle = sections // 2
    act_middle = lax.ppermute(output, "pipe", [(middle - 1, middle)])
    returned = returned + returned_near
    grad_input, terms = staged("dp", backward, returned, cotangent, up_full, grad_act)
    terms = lax.all_to_all(terms, "dp", split_axis=0, concat_axis=0, tiled=True)
    grad_prev = shifted(grad_input, "pipe", -1)
    up_grad = jnp.sum(terms[:, :, :features].astype(jnp.float32), axis=0)
    down_grad = lax.dot_general(
        terms[:, :, features:], cotangents, (((0, 2), (0, 1)), ((), ())), preferred_element_type=jnp.float32
    )
    return (
        (act_next + act_middle)[None],
        grad_prev[None],
        up_grad.astype(jnp.bfloat16).T[None],
        down_grad.astype(jnp.bfloat16)[None],
    )


def solution(mesh):
    in_specs = (
        P("pipe", "dp", "mp"),
        P("pipe", "dp", "mp"),
        P("pipe", "dp", "mp"),
        P("pipe", "mp", "dp"),
        P("pipe", "dp", "mp"),
    )
    out_specs = (
        P("pipe", "dp", "mp"),
        P("pipe", "dp", "mp"),
        P("pipe", "mp", "dp"),
        P("pipe", "dp", "mp"),
    )
    return jax.shard_map(shards, mesh=mesh, in_specs=in_specs, out_specs=out_specs, check_vma=False)
```

time: 197 us -> 149 us (0.76)
  the two profiles are of different devices: /device:TPU:13 before, /device:TPU:136 now
where the time goes in v2:
time: 149 us
  waiting for transfers between devices  67.2 us (45%)
  starting transfers between devices  46 us (31%)
  matrix products  10.9 us (7%)
  other arithmetic  8.51 us (6%)
  blocking collectives  7.88 us (5%)
  local copies, waits for them, and re-layouts  7.16 us (5%)
    all_to_all x2, waiting for transfers between devices, spread(): return lax.all_to_all(copies, axis, split_axis=0, concat_axis=0, tiled=True)  25.8 us
    ppermute x1, waiting for transfers between devices, forward(): lax.ppermute(output, 'pipe', [(i - 1, i) for i in range(1, 2 * middle) if...  19.8 us
    ppermute x1, waiting for transfers between devices, shifted(): return lax.ppermute(block, axis, route)  17.7 us
    ppermute x1, starting transfers between devices, shards(): lax.ppermute(stash_far[0], 'pipe', [(i, sections - 1 - i) for i in far])  12.9 us
    all_to_all x2, starting transfers between devices, spread(): return lax.all_to_all(copies, axis, split_axis=0, concat_axis=0, tiled=True)  11.1 us
    all_to_all x1, blocking collectives, spread(): return lax.all_to_all(copies, axis, split_axis=0, concat_axis=0, tiled=True)  7.88 us
    dot_general x6, matrix products, dot(): lax.dot_general(left, right, (((left_dim,), (right_dim,)), ((), ())), pre...  7.63 us
    ppermute x3, starting transfers between devices, from_next(): lax.ppermute(block, axis, [((i + distance) % size, i) for i in range(size)])  6.55 us
  transfers between devices with their start and end apart: 12, of which 5 were waited for; matrix products, arithmetic and copies ran while one was open for 14% of the time, Pallas kernels for 0%

profile of v2, /device:TPU:136, one launch (start us, length us, event | category | flops | bytes accessed | tf_op | source)
XLA Modules:
  0.0 148.5 jit_solution(17366391869823509553)
XLA Ops:
  0.6 12.9 %collective-permute-start.7 = (bf16[128,3072]{1,0:T(8,128)(2,1)}, bf16[128,3072]{1,0:T(8,128)(2,1)}, u32[]{:S(2)}, u32[]{:S(2)}) collective-permute-start(bf16[128,3072]{1,0:T(8,128)(2,1)} %bitcast.53), channel_id=1, source_target_pairs={{64,432},{80,416},{96,400},{112,384},{128,368},{144,352},{160,336}... | collective-permute-start | bytes 2359304 | tf_op jit(solution)/shard_map/ppermute | solution.py:145
  13.6 85.3 %conditional.3 = (bf16[128,3072]{1,0:T(8,128)(2,1)}, bf16[128,3072]{1,0:T(8,128)(2,1)}, f32[192,128]{1,0:T(8,128)}, bf16[192,3072]{1,0:T(8,128)(2,1)}, bf16[4,12...) conditional(s32[]{:T(128)} %convert_element_type.62, () %tuple.33, (bf16[1,48,3072]{2,1,0:T(8,128)(2,1)}, ...), branch_computations={%region_0.0_spmd, %region_1.0_spmd} | conditional | flops 457642112 | bytes 58087948 | solution.py:60
  13.6 1.1 pad_maximum_fusion.1
  14.7 1.7 %broadcast_in_dim.8 = bf16[4,96,3072]{2,1,0:T(8,128)(2,1)} broadcast(bf16[96,3072]{1,0:T(8,128)(2,1)S(1)} %pad_maximum_fusion.1), dimensions={1,2} | broadcast | bytes 2949120 | tf_op jit(solution)/shard_map/cond/branch_1_fun/broadcast_in_dim | solution.py:24
  16.4 5.0 %all-to-all-start = ((bf16[4,96,3072]{2,1,0:T(8,128)(2,1)}), bf16[4,96,3072]{2,1,0:T(8,128)(2,1)S(1)}, u32[]{:S(2)}, u32[]{:S(2)}) async-start(bf16[4,96,3072]{2,1,0:T(8,128)(2,1)} %broadcast_in_dim.8), calls=%async_computation | async-start | bytes 4718592 | tf_op jit(solution)/shard_map/cond/branch_1_fun/all_to_all | solution.py:25
  21.4 1.6 %collective-permute-start.4 = (bf16[128,3072]{1,0:T(8,128)(2,1)}, bf16[128,3072]{1,0:T(8,128)(2,1)}, u32[]{:S(2)}, u32[]{:S(2)}) collective-permute-start(bf16[128,3072]{1,0:T(8,128)(2,1)} %get-tuple-element.42), channel_id=1, source_target_pairs={{0,16},{16,0},{32,48},{48,32},{192,208},{208,192},{224,240},{240,2... | collective-permute-start | bytes 2359304 | tf_op jit(solution)/shard_map/cond/branch_1_fun/ppermute | solution.py:108
  23.0 0.0 collective-permute-done.4
  23.0 25.8 %all-to-all-done = bf16[4,96,3072]{2,1,0:T(8,128)(2,1)S(1)} async-done(((bf16[4,96,3072]{2,1,0:T(8,128)(2,1)}), bf16[4,96,3072]{2,1,0:T(8,128)(2,1)S(1)}, u32[]{:S(2)}, u32[]{:S(2)}) %all-to-all-start) | async-done | bytes 2359328 | tf_op jit(solution)/shard_map/cond/branch_1_fun/all_to_all | solution.py:25
  48.8 2.1 %broadcast_in_dim.11 = bf16[4,128,3072]{2,1,0:T(8,128)(2,1)} broadcast(bf16[128,3072]{1,0:T(8,128)(2,1)S(1)} %copy-done.1), dimensions={1,2} | broadcast | bytes 3932160 | tf_op jit(solution)/shard_map/cond/branch_1_fun/broadcast_in_dim | solution.py:24
  50.9 6.1 %all-to-all-start.1 = ((bf16[4,128,3072]{2,1,0:T(8,128)(2,1)}), bf16[4,128,3072]{2,1,0:T(8,128)(2,1)}, u32[]{:S(2)}, u32[]{:S(2)}) async-start(bf16[4,128,3072]{2,1,0:T(8,128)(2,1)} %broadcast_in_dim.11), calls=%async_computation.1 | async-start | bytes 6291456 | tf_op jit(solution)/shard_map/cond/branch_1_fun/all_to_all | solution.py:25
  57.0 1.7 %collective-permute-start.5 = (bf16[128,3072]{1,0:T(8,128)(2,1)}, bf16[128,3072]{1,0:T(8,128)(2,1)}, u32[]{:S(2)}, u32[]{:S(2)}) collective-permute-start(bf16[128,3072]{1,0:T(8,128)(2,1)} %collective-permute-done.4), channel_id=1, source_target_pairs={{16,496},{0,480},{48,464},{32,448},{208,304},{192,288},{240,272},{... | collective-permute-start | bytes 2359304 | tf_op jit(solution)/shard_map/cond/branch_1_fun/ppermute | solution.py:111
  58.7 1.1 slice.23
  59.8 0.3 copy-done.2
  60.1 38.8 %conditional = (bf16[128,3072]{1,0:T(8,128)(2,1)}, bf16[128,3072]{1,0:T(8,128)(2,1)}, f32[192,128]{1,0:T(8,128)}) conditional(s32[]{:T(128)} %convert_element_type.52, () %tuple.21, (bf16[1,128,3072]{2,1,0:T(8,128)(2,1)S(1)}, bf16[192,3072]{1,0:T(8,128)(2,1)}, bf16[4,96,3072]{2,1,0:T(8,128)(2,1)S(1)}, bf16[128,3072]{1,0:T(8,128)(2,1)S(1)}) %tuple.52), branch_computations={%region_2.0_spmd, %region_3.0_spmd} | conditional | flops 456462464 | bytes 15423672 | solution.py:60
  60.1 0.2 fusion.1
  60.3 1.7 %convolution_convert_fusion.1 = bf16[192,128]{1,0:T(8,128)(2,1)S(1)} fusion(bf16[192,3072]{1,0:T(8,128)(2,1)} %get-tuple-element.35, bf16[1,128,3072]{2,1,0:T(8,128)(2,1)S(1)} %get-tuple-element.34), kind=kOutput, calls=%fused_computation.5 | convolution fusion | flops 151019520 | bytes 2015232 | tf_op jit(solution)/shard_map/cond/branch_1_fun/cond/branch_1_fun/dot_general | solution.py:42
  62.1 0.1 slice.19
  62.2 0.5 convolution_convert_fusion
  62.7 1.9 %collective-permute-start = (bf16[400,128]{1,0:T(8,128)(2,1)S(1)}, bf16[400,128]{1,0:T(8,128)(2,1)S(1)}, u32[]{:S(2)}, u32[]{:S(2)}) collective-permute-start(bf16[400,128]{1,0:T(8,128)(2,1)S(1)} %pad_maximum_fusion), channel_id=1, source_target_pairs={{1,0},{2,1},{3,2},{0,3},{5,4},{6,5},{7,6},{4,7},{9,8},{10,9},{11,1... | collective-permute-start | bytes 307208 | tf_op jit(solution)/shard_map/cond/branch_1_fun/cond/branch_1_fun/ppermute | solution.py:34
  64.6 2.5 %collective-permute-start.1 = (bf16[400,128]{1,0:T(8,128)(2,1)S(1)}, bf16[400,128]{1,0:T(8,128)(2,1)S(1)}, u32[]{:S(2)}, u32[]{:S(2)}) collective-permute-start(bf16[400,128]{1,0:T(8,128)(2,1)S(1)} %pad_maximum_fusion), channel_id=1, source_target_pairs={{2,0},{3,1},{0,2},{1,3},{6,4},{7,5},{4,6},{5,7},{10,8},{11,9},{8,1... | collective-permute-start | bytes 307208 | tf_op jit(solution)/shard_map/cond/branch_1_fun/cond/branch_1_fun/ppermute | solution.py:34
  67.1 2.1 %collective-permute-start.2 = (bf16[400,128]{1,0:T(8,128)(2,1)S(1)}, bf16[400,128]{1,0:T(8,128)(2,1)S(1)}, u32[]{:S(2)}, u32[]{:S(2)}) collective-permute-start(bf16[400,128]{1,0:T(8,128)(2,1)S(1)} %pad_maximum_fusion), channel_id=1, source_target_pairs={{3,0},{0,1},{1,2},{2,3},{7,4},{4,5},{5,6},{6,7},{11,8},{8,9},{9,10... | collective-permute-start | bytes 307208 | tf_op jit(solution)/shard_map/cond/branch_1_fun/cond/branch_1_fun/ppermute | solution.py:34
  69.3 2.5 %collective-permute-done.1 = bf16[400,128]{1,0:T(8,128)(2,1)S(1)} collective-permute-done((bf16[400,128]{1,0:T(8,128)(2,1)S(1)}, bf16[400,128]{1,0:T(8,128)(2,1)S(1)}, u32[]{:S(2)}, u32[]{:S(2)}) %collective-permute-start.1) | collective-permute-done | bytes 102432 | tf_op jit(solution)/shard_map/cond/branch_1_fun/cond/branch_1_fun/ppermute | solution.py:34
  71.8 1.3 collective-permute-done.2
  73.1 0.1 convert_add_fusion
  73.2 1.3 fusion
  74.5 3.9 %collective-permute-start.3 = (bf16[128,3072]{1,0:T(8,128)(2,1)}, bf16[128,3072]{1,0:T(8,128)(2,1)}, u32[]{:S(2)}, u32[]{:S(2)}) collective-permute-start(bf16[128,3072]{1,0:T(8,128)(2,1)} %fusion), channel_id=1, source_target_pairs={{0,16},{16,32},{32,48},{48,64},{64,80},{80,96},{96,112},{112,128},... | collective-permute-start | bytes 2359304 | tf_op jit(solution)/shard_map/cond/branch_1_fun/cond/branch_1_fun/ppermute | solution.py:91
  78.4 0.6 slice.32
  79.0 19.8 %collective-permute-done.3 = bf16[128,3072]{1,0:T(8,128)(2,1)} collective-permute-done((bf16[128,3072]{1,0:T(8,128)(2,1)}, bf16[128,3072]{1,0:T(8,128)(2,1)}, u32[]{:S(2)}, u32[]{:S(2)}) %collective-permute-start.3) | collective-permute-done | bytes 786464 | tf_op jit(solution)/shard_map/cond/branch_1_fun/cond/branch_1_fun/ppermute | solution.py:91
  98.9 1.6 %collective-permute-start.6 = (bf16[128,3072]{1,0:T(8,128)(2,1)}, bf16[128,3072]{1,0:T(8,128)(2,1)}, u32[]{:S(2)}, u32[]{:S(2)}) collective-permute-start(bf16[128,3072]{1,0:T(8,128)(2,1)} %get-tuple-element.67), channel_id=1, source_target_pairs={{240,256},{241,257},{242,258},{243,259},{244,260},{245,261},{246,2... | collective-permute-start | bytes 2359304 | tf_op jit(solution)/shard_map/ppermute | solution.py:150
  100.5 0.0 collective-permute-done.7
  100.5 16.3 %conditional.4 = (bf16[128,3072]{1,0:T(8,128)(2,1)S(1)}, bf16[4,48,3200]{2,1,0:T(8,128)(2,1)}) conditional(s32[]{:T(128)} %convert_element_type.62, () %tuple.35, (bf16[128,3072]{1,0:T(8,128)(2,1)}, bf16[128,3072]{1,0:T(8,128)(2,1)}, bf16[128,3072]{1,0:T(8,128)(2,1)}, bf16[192,3072]{1,0:T(8,128)(2,1)}, f32[192,128]{1,0:T(8,128)}) %tuple.51), branch_computations={%region_5.0_spmd, %region_6.0_spmd} | conditional | flops 461880192 | bytes 17151532 | solution.py:60
  100.5 1.7 %fusion.11 = (bf16[128]{0:T(256)(128)(2,1)S(1)}, bf16[128,3072]{1,0:T(8,128)(2,1)S(1)}) fusion(bf16[128,3072]{1,0:T(8,128)(2,1)} %get-tuple-element.51, bf16[128,3072]{1,0:T(8,128)(2,1)} %get-tuple-element.52), kind=kLoop, calls=%fused_computation.25 | loop fusion | flops 2752384 | bytes 2359552 | tf_op jit(solution)/shard_map/cond/branch_1_fun/reduce_sum | solution.py:53
  102.2 1.8 %fusion.12 = bf16[192,128]{1,0:T(8,128)(2,1)S(1)} fusion(bf16[128,3072]{1,0:T(8,128)(2,1)S(1)} %get-tuple-element.81, bf16[192,3072]{1,0:T(8,128)(2,1)} %get-tuple-element.53), kind=kOutput, calls=%fused_computation.28 | convolution fusion | flops 151019520 | bytes 2015232 | tf_op jit(solution)/shard_map/cond/branch_1_fun/dot_general | solution.py:42
  104.1 7.9 %all_to_all.17 = bf16[4,208,128]{2,1,0:T(8,128)(2,1)S(1)} all-to-all(bf16[4,208,128]{2,1,0:T(8,128)(2,1)S(1)} %broadcast_in_dim.26), channel_id=1, replica_groups=mesh['pipe'=32,'dp'=4,'mp'=4] {'mp'}, dimensions={0} | all-to-all | bytes 425984 | tf_op jit(solution)/shard_map/cond/branch_1_fun/all_to_all | solution.py:25
  112.0 1.0 multiply_reduce_fusion
  113.0 0.5 convolution_convert_fusion.2
  113.4 0.0 copy-start.3
  113.4 1.1 pad_maximum_fusion.2
  114.6 0.3 copy-done.3
  114.9 1.9 %fusion.10 = bf16[128,3072]{1,0:T(8,128)(2,1)S(1)} fusion(bf16[192,3072]{1,0:T(8,128)(2,1)} %get-tuple-element.53, bf16[128,3072]{1,0:T(8,128)(2,1)S(1)} %get-tuple-element.81, bf16[128,3072]{1,0:T(8,128)(2,1)S(1)} %copy-done.3, f32[128]{0:T(128)S(1)} %fusion.18, f32[192,128]{1,0:T(8,128)S(1)} %get-tuple-element.79, f32[128]{0:T(128)S(1)} %fusion.17), kind=kOutput, calls=%fused_computation.22 | convolution fusion | flops 153403392 | bytes 3638272 | tf_op jit(solution)/shard_map/cond/branch_1_fun/dot_general | solution.py:42
  116.7 4.8 %all-to-all-start.3 = ((bf16[4,48,3200]{2,1,0:T(8,128)(2,1)}), bf16[4,48,3200]{2,1,0:T(8,128)(2,1)S(1)}, u32[]{:S(2)}, u32[]{:S(2)}) async-start(bf16[4,48,3200]{2,1,0:T(8,128)(2,1)} %get-tuple-element.72), calls=%async_computation.3 | async-start | bytes 2457600 | tf_op jit(solution)/shard_map/all_to_all | solution.py:153
  121.6 1.9 %collective-permute-start.8 = (bf16[128,3072]{1,0:T(8,128)(2,1)S(1)}, bf16[128,3072]{1,0:T(8,128)(2,1)S(1)}, u32[]{:S(2)}, u32[]{:S(2)}) collective-permute-start(bf16[128,3072]{1,0:T(8,128)(2,1)S(1)} %get-tuple-element.71), channel_id=1, source_target_pairs={{16,0},{32,16},{48,32},{64,48},{80,64},{96,80},{112,96},{128,112},... | collective-permute-start | bytes 2359304 | tf_op jit(solution)/shard_map/ppermute | solution.py:15
  123.5 2.3 %add_bitcast_fusion = bf16[1,128,3072]{2,1,0:T(8,128)(2,1)} fusion(bf16[128,3072]{1,0:T(8,128)(2,1)} %get-tuple-element.66, bf16[128,3072]{1,0:T(8,128)(2,1)} %collective-permute-done.6), kind=kLoop, calls=%fused_computation.49 | loop fusion | flops 393216 | bytes 2359296 | tf_op jit(solution)/shard_map/broadcast_in_dim | solution.py:160
  125.8 17.7 %collective-permute-done.8 = bf16[128,3072]{1,0:T(8,128)(2,1)S(1)} collective-permute-done((bf16[128,3072]{1,0:T(8,128)(2,1)S(1)}, bf16[128,3072]{1,0:T(8,128)(2,1)S(1)}, u32[]{:S(2)}, u32[]{:S(2)}) %collective-permute-start.8) | collective-permute-done | bytes 786464 | tf_op jit(solution)/shard_map/ppermute | solution.py:15
  143.5 0.0 all-to-all-done.3
  143.5 0.9 slice_reduce_fusion
  144.4 3.3 %fusion.20 = bf16[1,48,3072]{2,1,0:T(8,128)(2,1)} fusion(bf16[4,128,3072]{2,1,0:T(8,128)(2,1)} %get-tuple-element.73, bf16[4,48,3200]{2,1,0:T(8,128)(2,1)S(1)} %all-to-all-done.3), kind=kOutput, calls=%fused_computation.47 | convolution fusion | flops 151142400 | bytes 3489792 | tf_op jit(solution)/shard_map/dot_general | solution.py:156
  147.6 0.9 copy.34
  (18 shorter events, 0.1 us)
Async XLA Ops:
  0.6 99.8 %collective-permute-start.7 = (bf16[128,3072]{1,0:T(8,128)(2,1)}, bf16[128,3072]{1,0:T(8,128)(2,1)}, u32[]{:S(2)}, u32[]{:S(2)}) collective-permute-start(bf16[128,3072]{1,0:T(8,128)(2,1)} %bitcast.53), channel_id=1, source_target_pairs={{64,432},{80,416},{96,400},{112,384},{128,368},{144,352},{160,336}... | collective-permute-start | bytes 2359304 | tf_op jit(solution)/shard_map/ppermute | solution.py:145
  16.4 32.4 %copy-start.1 = (bf16[128,3072]{1,0:T(8,128)(2,1)S(1)}, bf16[128,3072]{1,0:T(8,128)(2,1)}, u32[]{:S(2)}) copy-start(bf16[128,3072]{1,0:T(8,128)(2,1)} %get-tuple-element.47) | copy-start | bytes 2359300 | tf_op jit(solution)/shard_map/cond
  16.4 32.4 %all-to-all-start = ((bf16[4,96,3072]{2,1,0:T(8,128)(2,1)}), bf16[4,96,3072]{2,1,0:T(8,128)(2,1)S(1)}, u32[]{:S(2)}, u32[]{:S(2)}) async-start(bf16[4,96,3072]{2,1,0:T(8,128)(2,1)} %broadcast_in_dim.8), calls=%async_computation | async-start | bytes 4718592 | tf_op jit(solution)/shard_map/cond/branch_1_fun/all_to_all | solution.py:25
  21.4 1.6 %collective-permute-start.4 = (bf16[128,3072]{1,0:T(8,128)(2,1)}, bf16[128,3072]{1,0:T(8,128)(2,1)}, u32[]{:S(2)}, u32[]{:S(2)}) collective-permute-start(bf16[128,3072]{1,0:T(8,128)(2,1)} %get-tuple-element.42), channel_id=1, source_target_pairs={{0,16},{16,0},{32,48},{48,32},{192,208},{208,192},{224,240},{240,2... | collective-permute-start | bytes 2359304 | tf_op jit(solution)/shard_map/cond/branch_1_fun/ppermute | solution.py:108
  50.9 48.0 %all-to-all-start.1 = ((bf16[4,128,3072]{2,1,0:T(8,128)(2,1)}), bf16[4,128,3072]{2,1,0:T(8,128)(2,1)}, u32[]{:S(2)}, u32[]{:S(2)}) async-start(bf16[4,128,3072]{2,1,0:T(8,128)(2,1)} %broadcast_in_dim.11), calls=%async_computation.1 | async-start | bytes 6291456 | tf_op jit(solution)/shard_map/cond/branch_1_fun/all_to_all | solution.py:25
  57.0 2.8 %copy-start = (bf16[1,128,3072]{2,1,0:T(8,128)(2,1)S(1)}, bf16[1,128,3072]{2,1,0:T(8,128)(2,1)}, u32[]{:S(2)}) copy-start(bf16[1,128,3072]{2,1,0:T(8,128)(2,1)} %get-tuple-element.77) | copy-start | bytes 2359300 | tf_op jit(solution)/shard_map/cond
  57.0 41.9 %collective-permute-start.5 = (bf16[128,3072]{1,0:T(8,128)(2,1)}, bf16[128,3072]{1,0:T(8,128)(2,1)}, u32[]{:S(2)}, u32[]{:S(2)}) collective-permute-start(bf16[128,3072]{1,0:T(8,128)(2,1)} %collective-permute-done.4), channel_id=1, source_target_pairs={{16,496},{0,480},{48,464},{32,448},{208,304},{192,288},{240,272},{... | collective-permute-start | bytes 2359304 | tf_op jit(solution)/shard_map/cond/branch_1_fun/ppermute | solution.py:111
  58.7 1.4 copy-start.2
  62.7 6.6 %collective-permute-start = (bf16[400,128]{1,0:T(8,128)(2,1)S(1)}, bf16[400,128]{1,0:T(8,128)(2,1)S(1)}, u32[]{:S(2)}, u32[]{:S(2)}) collective-permute-start(bf16[400,128]{1,0:T(8,128)(2,1)S(1)} %pad_maximum_fusion), channel_id=1, source_target_pairs={{1,0},{2,1},{3,2},{0,3},{5,4},{6,5},{7,6},{4,7},{9,8},{10,9},{11,1... | collective-permute-start | bytes 307208 | tf_op jit(solution)/shard_map/cond/branch_1_fun/cond/branch_1_fun/ppermute | solution.py:34
  64.6 7.2 %collective-permute-start.1 = (bf16[400,128]{1,0:T(8,128)(2,1)S(1)}, bf16[400,128]{1,0:T(8,128)(2,1)S(1)}, u32[]{:S(2)}, u32[]{:S(2)}) collective-permute-start(bf16[400,128]{1,0:T(8,128)(2,1)S(1)} %pad_maximum_fusion), channel_id=1, source_target_pairs={{2,0},{3,1},{0,2},{1,3},{6,4},{7,5},{4,6},{5,7},{10,8},{11,9},{8,1... | collective-permute-start | bytes 307208 | tf_op jit(solution)/shard_map/cond/branch_1_fun/cond/branch_1_fun/ppermute | solution.py:34
  67.1 6.0 %collective-permute-start.2 = (bf16[400,128]{1,0:T(8,128)(2,1)S(1)}, bf16[400,128]{1,0:T(8,128)(2,1)S(1)}, u32[]{:S(2)}, u32[]{:S(2)}) collective-permute-start(bf16[400,128]{1,0:T(8,128)(2,1)S(1)} %pad_maximum_fusion), channel_id=1, source_target_pairs={{3,0},{0,1},{1,2},{2,3},{7,4},{4,5},{5,6},{6,7},{11,8},{8,9},{9,10... | collective-permute-start | bytes 307208 | tf_op jit(solution)/shard_map/cond/branch_1_fun/cond/branch_1_fun/ppermute | solution.py:34
  74.5 24.4 %collective-permute-start.3 = (bf16[128,3072]{1,0:T(8,128)(2,1)}, bf16[128,3072]{1,0:T(8,128)(2,1)}, u32[]{:S(2)}, u32[]{:S(2)}) collective-permute-start(bf16[128,3072]{1,0:T(8,128)(2,1)} %fusion), channel_id=1, source_target_pairs={{0,16},{16,32},{32,48},{48,64},{64,80},{80,96},{96,112},{112,128},... | collective-permute-start | bytes 2359304 | tf_op jit(solution)/shard_map/cond/branch_1_fun/cond/branch_1_fun/ppermute | solution.py:91
  98.9 24.6 %collective-permute-start.6 = (bf16[128,3072]{1,0:T(8,128)(2,1)}, bf16[128,3072]{1,0:T(8,128)(2,1)}, u32[]{:S(2)}, u32[]{:S(2)}) collective-permute-start(bf16[128,3072]{1,0:T(8,128)(2,1)} %get-tuple-element.67), channel_id=1, source_target_pairs={{240,256},{241,257},{242,258},{243,259},{244,260},{245,261},{246,2... | collective-permute-start | bytes 2359304 | tf_op jit(solution)/shard_map/ppermute | solution.py:150
  113.4 1.4 copy-start.3
  116.7 26.8 %all-to-all-start.3 = ((bf16[4,48,3200]{2,1,0:T(8,128)(2,1)}), bf16[4,48,3200]{2,1,0:T(8,128)(2,1)S(1)}, u32[]{:S(2)}, u32[]{:S(2)}) async-start(bf16[4,48,3200]{2,1,0:T(8,128)(2,1)} %get-tuple-element.72), calls=%async_computation.3 | async-start | bytes 2457600 | tf_op jit(solution)/shard_map/all_to_all | solution.py:153
  121.6 21.9 %collective-permute-start.8 = (bf16[128,3072]{1,0:T(8,128)(2,1)S(1)}, bf16[128,3072]{1,0:T(8,128)(2,1)S(1)}, u32[]{:S(2)}, u32[]{:S(2)}) collective-permute-start(bf16[128,3072]{1,0:T(8,128)(2,1)S(1)} %get-tuple-element.71), channel_id=1, source_target_pairs={{16,0},{32,16},{48,32},{64,48},{80,64},{96,80},{112,96},{128,112},... | collective-permute-start | bytes 2359304 | tf_op jit(solution)/shard_map/ppermute | solution.py:15

commit v3 on v1

v3 whole, which is shorter than its diff:
```python
import functools

import jax
import jax.numpy as jnp
from jax import lax
from jax.experimental import pallas as pl
from jax.experimental.pallas import tpu as pltpu
from jax.sharding import PartitionSpec as P

D = 12288


epsilon = 1e-05


TILE = 1024


EXTRA = 16


def shifted(block, axis, distance):
    devices = range(lax.axis_size(axis))
    route = [(i - distance, i) for i in devices if i - distance in devices]
    return lax.ppermute(block, axis, route)


def near_sections(count):
    planes = count // 2
    return [i for i in range(count) if min((2 * (i // 2) + 1) % planes, -(2 * (i // 2) + 1) % planes) <= 3]


def spread(block, axis):
    copies = jnp.broadcast_to(block[None], (lax.axis_size(axis),) + block.shape)
    return lax.all_to_all(copies, axis, split_axis=0, concat_axis=0, tiled=True)


def summed(block, axis):
    size, distance = lax.axis_size(axis), 1
    while distance < size:
        block = block + lax.ppermute(block, axis, [(i, i ^ distance) for i in range(size)])
        distance *= 2
    return block


def staged(axis, step, *args):
    shapes = jax.eval_shape(step, *args)
    empty = lambda *_: jax.tree.map(lambda leaf: jnp.zeros(leaf.shape, leaf.dtype), shapes)
    return lax.cond(lax.axis_index(axis) < lax.axis_size(axis), step, empty, *args)


def dot(left, right, left_dim, right_dim):
    return lax.dot_general(
        left, right, (((left_dim,), (right_dim,)), ((), ())), preferred_element_type=jnp.float32
    )


def gated(hidden):
    sigmoid_value = jax.nn.sigmoid(hidden)
    return (hidden * sigmoid_value, sigmoid_value * (1.0 + hidden * (1.0 - sigmoid_value)))


def call(kernel, name, args, out_shape, scratch, flops):
    in_vmem = pl.BlockSpec(memory_space=pltpu.VMEM)
    return pl.pallas_call(
        kernel,
        in_specs=[in_vmem] * len(args),
        out_specs=jax.tree.map(lambda _: in_vmem, out_shape),
        out_shape=out_shape,
        scratch_shapes=scratch,
        name=name,
        compiler_params=pltpu.CompilerParams(vmem_limit_bytes=24 * 2**20),
        cost_estimate=pl.CostEstimate(flops=flops, bytes_accessed=5 * 2**20, transcendentals=0),
    )(*args)


def struct(*shape, dtype=jnp.bfloat16):
    return jax.ShapeDtypeStruct(shape, dtype)


def tiles(features):
    return [pl.ds(start, TILE) for start in range(0, features, TILE)]


def up_rows(weights_ref, tile):
    group, own_rank, _ = weights_ref.shape
    own_rank //= 2
    return weights_ref[:, :own_rank, tile].reshape(group * own_rank, TILE)


def down_rows(weights_ref, tile):
    group, own_rank, _ = weights_ref.shape
    own_rank //= 2
    return weights_ref[:, own_rank:, tile].reshape(group * own_rank, TILE)


def squares_of(inputs):
    wide = inputs.astype(jnp.float32)
    return sum(jnp.square(wide[:, i : i + 128]) for i in range(0, wide.shape[1], 128))


def row_sums(squares):
    return jnp.broadcast_to(jnp.sum(squares.T, axis=0, keepdims=True), (EXTRA, squares.shape[0]))


def first_kernel(weights_ref, input_ref, cotangent_ref, out_ref):
    rank = (out_ref.shape[0] - EXTRA) // 2
    product = squares = grad_act = 0.0
    for tile in tiles(input_ref.shape[1]):
        inputs = input_ref[:, tile]
        product += dot(up_rows(weights_ref, tile), inputs, 1, 1)
        grad_act += dot(down_rows(weights_ref, tile), cotangent_ref[:, tile], 1, 1)
        squares += squares_of(inputs)
    out_ref[:rank, :] = product.astype(out_ref.dtype)
    out_ref[rank : 2 * rank, :] = grad_act.astype(out_ref.dtype)
    out_ref[2 * rank :, :] = row_sums(squares).astype(out_ref.dtype)


def first_products(weights, inputs, cotangent):
    group, own_rank, features = weights.shape
    rank, rows = group * own_rank // 2, inputs.shape[0]
    return call(
        first_kernel, "first_products", (weights, inputs, cotangent),
        struct(2 * rank + EXTRA, rows, dtype=jnp.float32), [], 4 * rank * rows * features,
    )


def second_kernel(up_ref, *refs):
    *input_refs, out_ref, sum_ref = refs
    rank = up_ref.shape[0]
    product = squares = 0.0
    for tile in tiles(up_ref.shape[1]):
        inputs = sum(ref[:, tile] for ref in input_refs)
        sum_ref[:, tile] = inputs
        product += dot(up_ref[:, tile], inputs, 1, 1)
        squares += squares_of(inputs)
    out_ref[:rank, :] = product.astype(out_ref.dtype)
    out_ref[rank:, :] = row_sums(squares).astype(out_ref.dtype)


def second_products(up_full, inputs):
    rank, features = up_full.shape
    rows = inputs[0].shape[0]
    return call(
        second_kernel, "second_products", (up_full, *inputs),
        [struct(rank + EXTRA, rows), struct(rows, features)], [], 2 * rank * rows * features,
    )


def output_kernel(parts_ref, weights_ref, input_ref, out_ref, grad_act_ref, up_ref):
    rank = grad_act_ref.shape[0]
    scale = lax.rsqrt(parts_ref[2 * rank : 2 * rank + 1, :] / D + epsilon)
    act = gated(parts_ref[:rank, :] * scale)[0].astype(jnp.bfloat16)
    grad_act_ref[...] = parts_ref[rank : 2 * rank, :]
    for tile in tiles(input_ref.shape[1]):
        out = input_ref[:, tile].astype(jnp.float32) + dot(act, down_rows(weights_ref, tile), 0, 0)
        out_ref[:, tile] = out.astype(out_ref.dtype)
        up_ref[:, tile] = up_rows(weights_ref, tile)


def forward_output(parts, weights, inputs):
    group, own_rank, features = weights.shape
    rank, rows = group * own_rank // 2, inputs.shape[0]
    return call(
        output_kernel, "forward_output", (parts, weights, inputs),
        [struct(*inputs.shape), struct(rank, rows, dtype=jnp.float32), struct(rank, features)],
        [], 2 * rank * rows * features,
    )


def input_kernel(parts_ref, grad_act_ref, up_ref, returned_ref, cotangent_ref, grad_ref, terms_ref):
    group, own_rank, _ = terms_ref.shape
    rank, rows = grad_act_ref.shape
    features = up_ref.shape[1]
    parts = jnp.sum(parts_ref[...].astype(jnp.float32), axis=0)
    back_proj = parts[:rank]
    scale = lax.rsqrt(parts[rank:] / D + epsilon)
    value, slope = gated(back_proj * scale[:1])
    grad_hidden = grad_act_ref[...] * slope
    proj = (grad_hidden * scale[:1]).astype(jnp.bfloat16)
    grad_scale = jnp.sum(grad_hidden * back_proj, axis=0, keepdims=True)
    pull = (-(scale * scale * scale) * grad_scale / D).T[:, :1]
    terms_ref[:, :, features:] = value.astype(terms_ref.dtype).reshape(group, own_rank, rows)
    for tile in tiles(features):
        returned = returned_ref[:, tile]
        grad = cotangent_ref[:, tile].astype(jnp.float32) + dot(proj, up_ref[:, tile], 0, 0)
        grad_ref[:, tile] = (grad + returned.astype(jnp.float32) * pull).astype(grad_ref.dtype)
        term = dot(proj, returned, 1, 0).astype(terms_ref.dtype)
        terms_ref[:, :, tile] = term.reshape(group, own_rank, TILE)


def input_gradient(parts, grad_act, up_full, returned, cotangent):
    rank, features = up_full.shape
    rows, group = returned.shape[0], lax.axis_size("dp")
    return call(
        input_kernel, "input_gradient", (parts, grad_act, up_full, returned, cotangent),
        [struct(rows, features), struct(group, rank // group, features + rows)], [], 4 * rank * rows * features,
    )


def weight_kernel(terms_ref, cotangents_ref, up_ref, down_ref):
    group, rows, features = cotangents_ref.shape
    acts = [terms_ref[k, :, features:] for k in range(group)]
    for tile in tiles(features):
        up_ref[:, tile] = jnp.sum(terms_ref[:, :, tile].astype(jnp.float32), axis=0).astype(up_ref.dtype)
        down = sum(dot(acts[k], cotangents_ref[k, :, tile], 1, 0) for k in range(group))
        down_ref[:, tile] = down.astype(down_ref.dtype)


def weight_gradients(terms, cotangents):
    group, rows, features = cotangents.shape
    share = (terms.shape[1], features)
    return call(
        weight_kernel, "weight_gradients", (terms, cotangents),
        [struct(*share)] * 2, [], 2 * group * rows * share[0] * features,
    )


def forward(weights, forward_in, cotangent):
    parts = summed(first_products(weights, forward_in, cotangent), "mp")
    output, grad_act, up_full = forward_output(parts, weights, forward_in)
    count = lax.axis_size("pipe")
    act_next = lax.ppermute(output, "pipe", [(i - 1, i) for i in range(1, count) if i != count // 2])
    return act_next, output, grad_act, up_full


def beside(weights, copies, forward_in, cotangent):
    cotangents = lax.all_to_all(copies, "dp", split_axis=0, concat_axis=0, tiled=True)
    return *staged("mp", forward, weights, forward_in, cotangent), cotangents


def ahead(forward_in, cotangent, up_proj, down_proj, stash):
    count, group = lax.axis_size("pipe"), lax.axis_size("dp")
    near = near_sections(count)
    copies = [jnp.broadcast_to(w[None], (group,) + w.shape) for w in (up_proj, down_proj)]
    weights = lax.all_to_all(jnp.concatenate(copies, 1), "dp", split_axis=0, concat_axis=0, tiled=True)
    crossed = lax.ppermute(stash, "pipe", [(i, i ^ 1) for i in near])
    copies = jnp.broadcast_to(cotangent[None], (group,) + cotangent.shape)
    copies, crossed = lax.optimization_barrier((copies, crossed))
    returned_far = lax.ppermute(stash, "pipe", [(i, count - 1 - i) for i in range(count // 2) if i not in near])
    returned_near = lax.ppermute(crossed, "pipe", [(i ^ 1, count - 1 - i) for i in near])
    act_next, output, grad_act, up_full, cotangents = staged("mp", beside, weights, copies, forward_in, cotangent)
    return act_next, output, grad_act, up_full, cotangents, returned_far, returned_near


def backward(returned, cotangent, up_full, grad_act):
    parts, returned = second_products(up_full, returned)
    return input_gradient(spread(parts, "mp"), grad_act, up_full, returned, cotangent)


def last_terms(terms, cotangents, act_next, output):
    middle = lax.axis_size("pipe") // 2
    act_middle = lax.ppermute(output, "pipe", [(middle - 1, middle)])
    terms = lax.all_to_all(terms, "dp", split_axis=0, concat_axis=0, tiled=True)
    return *weight_gradients(terms, cotangents), act_next + act_middle


def shards(act_in, grad_in, stash_far, up_proj, down_proj):
    cotangent = grad_in[0]
    count = lax.axis_size("pipe")
    near = near_sections(count)
    returned = lax.ppermute(
        stash_far[0], "pipe", [(i, count - 1 - i) for i in range(count // 2, count) if i not in near]
    )
    act_next, output, grad_act, up_full, cotangents, *returned_later = staged(
        "dp", ahead, act_in[0], cotangent, up_proj[0].T, down_proj[0], stash_far[0]
    )
    grad_input, terms = staged("dp", backward, [returned, *returned_later], cotangent, up_full, grad_act)
    grad_prev = shifted(grad_input, "pipe", -1)
    up_grad, down_grad, act_next = staged("dp", last_terms, terms, cotangents, act_next, output)
    return act_next[None], grad_prev[None], up_grad.T[None], down_grad[None]


def solution(mesh):
    in_specs = (
        P("pipe", "dp", "mp"),
        P("pipe", "dp", "mp"),
        P("pipe", "dp", "mp"),
        P("pipe", "mp", "dp"),
        P("pipe", "dp", "mp"),
    )
    out_specs = (
        P("pipe", "dp", "mp"),
        P("pipe", "dp", "mp"),
        P("pipe", "mp", "dp"),
        P("pipe", "dp", "mp"),
    )
    return jax.shard_map(shards, mesh=mesh, in_specs=in_specs, out_specs=out_specs, check_vma=False)
```

time: 197 us -> 146 us (0.74)
  the two profiles are of different devices: /device:TPU:13 before, /device:TPU:264 now
where the time goes in v3:
time: 146 us; the launch traced here: 145 us
  waiting for transfers between devices  72.8 us (50%)
  starting transfers between devices  42.3 us (29%)
  Pallas kernels  12.7 us (9%)
  blocking collectives  8.07 us (6%)
  local copies, waits for them, and re-layouts  4.23 us (3%)
  other arithmetic  3.95 us (3%)
    ppermute x1, waiting for transfers between devices, last_terms(): act_middle = lax.ppermute(output, 'pipe', [(middle - 1, middle)])  18.7 us
    ppermute x1, waiting for transfers between devices, ahead(): crossed = lax.ppermute(stash, 'pipe', [(i, i ^ 1) for i in near])  15.9 us
    ppermute x1, waiting for transfers between devices, forward(): lax.ppermute(output, 'pipe', [(i - 1, i) for i in range(1, count) if i !=...  15.8 us
    pallas_call x5, Pallas kernels, call(): pl.pallas_call(kernel, in_specs=[in_vmem] * len(args), out_specs=jax.tree...  12.7 us
    ppermute x1, waiting for transfers between devices, ahead(): lax.ppermute(crossed, 'pipe', [(i ^ 1, count - 1 - i) for i in near])  8.92 us
    all_to_all x1, blocking collectives, spread(): return lax.all_to_all(copies, axis, split_axis=0, concat_axis=0, tiled=True)  8.07 us
    ppermute x2, waiting for transfers between devices, summed(): lax.ppermute(block, axis, [(i, i ^ distance) for i in range(size)])  7.03 us
    all_to_all x1, starting transfers between devices, beside(): lax.all_to_all(copies, 'dp', split_axis=0, concat_axis=0, tiled=True)  6.07 us
  transfers between devices with their start and end apart: 12, of which 8 were waited for; matrix products, arithmetic and copies ran while one was open for 5% of the time, Pallas kernels for 5%

profile of v3, /device:TPU:264, one launch (start us, length us, event | category | flops | bytes accessed | tf_op | source)
XLA Modules:
  0.0 144.8 jit_solution(3739556438251590689)
XLA Ops:
  0.6 1.6 %collective-permute-start.7 = (bf16[128,3072]{1,0:T(8,128)(2,1)}, bf16[128,3072]{1,0:T(8,128)(2,1)}, u32[]{:S(2)}, u32[]{:S(2)}) collective-permute-start(bf16[128,3072]{1,0:T(8,128)(2,1)} %bitcast.24), channel_id=1, source_target_pairs={{320,176},{336,160},{352,144},{368,128},{384,112},{400,96},{416,80... | collective-permute-start | bytes 2359304 | tf_op jit(solution)/shard_map/ppermute | solution.py:262
  2.3 88.4 %conditional.5 = (bf16[128,3072]{1,0:T(8,128)(2,1)}, bf16[128,3072]{1,0:T(8,128)(2,1)}, f32[192,128]{1,0:T(8,128)}, bf16[192,3072]{1,0:T(8,128)(2,1)}, bf16[4,12...) conditional(s32[]{:T(128)} %convert_element_type.11, () %tuple.54, ...), branch_computations={%region_0.0_spmd, %region_1.0_spmd} | conditional | flops 457805824 | bytes 61522560 | solution.py:49
  2.3 0.0 copy-start.3
  2.3 1.1 broadcast_in_dim.30
  3.4 0.0 copy-done.3
  3.4 0.1 broadcast_in_dim.36
  3.5 1.6 %pad_maximum_fusion = bf16[4,96,3072]{2,1,0:T(8,128)(2,1)} fusion(bf16[4,48,3072]{2,1,0:T(8,128)(2,1)S(1)} %broadcast_in_dim.36, bf16[4,48,3072]{2,1,0:T(8,128)(2,1)S(1)} %broadcast_in_dim.30), kind=kLoop, calls=%fused_computation | loop fusion | flops 4718592 | bytes 4718592 | tf_op jit(solution)/shard_map/cond/branch_1_fun/concatenate | solution.py:236
  5.1 0.0 copy-start
  5.1 5.0 %all-to-all-start.2 = ((bf16[4,96,3072]{2,1,0:T(8,128)(2,1)}), bf16[4,96,3072]{2,1,0:T(8,128)(2,1)S(1)}, u32[]{:S(2)}, u32[]{:S(2)}) async-start(bf16[4,96,3072]{2,1,0:T(8,128)(2,1)} %pad_maximum_fusion), calls=%async_computation.2 | async-start | bytes 4718592 | tf_op jit(solution)/shard_map/cond/branch_1_fun/all_to_all | solution.py:236
  10.2 4.9 %collective-permute-start.3 = (bf16[128,3072]{1,0:T(8,128)(2,1)}, bf16[128,3072]{1,0:T(8,128)(2,1)}, u32[]{:S(2)}, u32[]{:S(2)}) collective-permute-start(bf16[128,3072]{1,0:T(8,128)(2,1)} %get-tuple-element.70), channel_id=1, source_target_pairs={{0,16},{16,0},{32,48},{48,32},{192,208},{208,192},{224,240},{240,2... | collective-permute-start | bytes 2359304 | tf_op jit(solution)/shard_map/cond/branch_1_fun/ppermute | solution.py:237
  15.1 1.6 %collective-permute-start.4 = (bf16[128,3072]{1,0:T(8,128)(2,1)}, bf16[128,3072]{1,0:T(8,128)(2,1)}, u32[]{:S(2)}, u32[]{:S(2)}) collective-permute-start(bf16[128,3072]{1,0:T(8,128)(2,1)} %get-tuple-element.70), channel_id=1, source_target_pairs={{64,432},{80,416},{96,400},{112,384},{128,368},{144,352},{160,336}... | collective-permute-start | bytes 2359304 | tf_op jit(solution)/shard_map/cond/branch_1_fun/ppermute | solution.py:240
  16.7 15.9 %collective-permute-done.3 = bf16[128,3072]{1,0:T(8,128)(2,1)} collective-permute-done((bf16[128,3072]{1,0:T(8,128)(2,1)}, bf16[128,3072]{1,0:T(8,128)(2,1)}, u32[]{:S(2)}, u32[]{:S(2)}) %collective-permute-start.3) | collective-permute-done | bytes 786464 | tf_op jit(solution)/shard_map/cond/branch_1_fun/ppermute | solution.py:237
  32.6 0.0 copy-done
  32.6 2.1 %broadcast_in_dim.38 = bf16[4,128,3072]{2,1,0:T(8,128)(2,1)} broadcast(bf16[128,3072]{1,0:T(8,128)(2,1)S(1)} %copy-done), dimensions={1,2} | broadcast | bytes 3932160 | tf_op jit(solution)/shard_map/cond/branch_1_fun/broadcast_in_dim | solution.py:238
  34.7 2.0 %collective-permute-start.5 = (bf16[128,3072]{1,0:T(8,128)(2,1)}, bf16[128,3072]{1,0:T(8,128)(2,1)}, u32[]{:S(2)}, u32[]{:S(2)}) collective-permute-start(bf16[128,3072]{1,0:T(8,128)(2,1)} %collective-permute-done.3), channel_id=1, source_target_pairs={{16,496},{0,480},{48,464},{32,448},{208,304},{192,288},{240,272},{... | collective-permute-start | bytes 2359304 | tf_op jit(solution)/shard_map/cond/branch_1_fun/ppermute | solution.py:241
  36.7 1.2 all-to-all-done.2
  37.8 43.9 %conditional.1 = (bf16[128,3072]{1,0:T(8,128)(2,1)}, bf16[128,3072]{1,0:T(8,128)(2,1)}, f32[192,128]{1,0:T(8,128)}, bf16[192,3072]{1,0:T(8,128)(2,1)}, bf16[4,128,3072]{2,1,0:T(8,128)(2,1)}) conditional(s32[]{:T(128)} %convert_element_type.6, () %tuple.37, (bf16[1,128,3072]{2,1,0:T(8,128)(2,1)}, bf16[4,96,3072]{2,1,0:T(8,128)(2,1)S(1)}, ...), branch_computations={%region_2.0_spmd, %region_3.0_spmd} | conditional | flops 453087232 | bytes 29081910 | solution.py:49
  37.8 6.1 %all-to-all-start = ((bf16[4,128,3072]{2,1,0:T(8,128)(2,1)}), bf16[4,128,3072]{2,1,0:T(8,128)(2,1)}, u32[]{:S(2)}, u32[]{:S(2)}) async-start(bf16[4,128,3072]{2,1,0:T(8,128)(2,1)} %get-tuple-element.64), calls=%async_computation | async-start | bytes 6291456 | tf_op jit(solution)/shard_map/cond/branch_1_fun/cond/branch_1_fun/all_to_all | solution.py:228
  43.9 37.8 %conditional = (bf16[128,3072]{1,0:T(8,128)(2,1)}, bf16[128,3072]{1,0:T(8,128)(2,1)}, f32[192,128]{1,0:T(8,128)}, bf16[192,3072]{1,0:T(8,128)(2,1)}) conditional(s32[]{:T(128)} %convert_element_type.2, () %tuple.34, (bf16[1,128,3072]{2,1,0:T(8,128)(2,1)}, bf16[4,96,3072]{2,1,0:T(8,128)(2,1)S(1)}, bf16[128,3072]{1,0:T(8,128)(2,1)S(1)}) %tuple.35), branch_computations={%region_4.0_spmd, %region_5.0_spmd} | conditional | flops 453087232 | bytes 19644596 | solution.py:49
  43.9 1.9 %first_products.1 = f32[400,128]{1,0:T(8,128)S(1)} custom-call(bf16[4,96,3072]{2,1,0:T(8,128)(2,1)S(1)} %get-tuple-element.51.weights_ref, bf16[128,3072]{1,0:T(8,128)(2,1)} %bitcast.17, bf16[128,3072]{1,0:T(8,128)(2,1)S(1)} %get-tuple-element.53.cotangent_ref), custom_call_target="tpu_custom_call" | custom-call | flops 301989888 | bytes 5242880 | tf_op jit(solution)/shard_map/cond/branch_1_fun/cond/branch_1_fun/cond/branch_1_fun/first_products/pallas_call | solution.py:65
  45.8 0.0 copy-start.2
  45.8 2.1 %collective-permute-start = (f32[400,128]{1,0:T(8,128)S(1)}, f32[400,128]{1,0:T(8,128)S(1)}, u32[]{:S(2)}, u32[]{:S(2)}) collective-permute-start(f32[400,128]{1,0:T(8,128)S(1)} %first_products.1), channel_id=1, source_target_pairs={{0,1},{1,0},{2,3},{3,2},{4,5},{5,4},{6,7},{7,6},{8,9},{9,8},{10,11... | collective-permute-start | bytes 614408 | tf_op jit(solution)/shard_map/cond/branch_1_fun/cond/branch_1_fun/cond/branch_1_fun/ppermute | solution.py:41
  47.9 1.4 collective-permute-done
  49.4 3.4 %collective-permute-start.1 = (f32[400,128]{1,0:T(8,128)S(1)}, f32[400,128]{1,0:T(8,128)S(1)}, u32[]{:S(2)}, u32[]{:S(2)}) collective-permute-start(f32[400,128]{1,0:T(8,128)S(1)} %add.6), channel_id=1, source_target_pairs={{0,2},{1,3},{2,0},{3,1},{4,6},{5,7},{6,4},{7,5},{8,10},{9,11},{10,... | collective-permute-start | bytes 614408 | tf_op jit(solution)/shard_map/cond/branch_1_fun/cond/branch_1_fun/cond/branch_1_fun/ppermute | solution.py:41
  52.8 5.6 %collective-permute-done.1 = f32[400,128]{1,0:T(8,128)S(1)} collective-permute-done((f32[400,128]{1,0:T(8,128)S(1)}, f32[400,128]{1,0:T(8,128)S(1)}, u32[]{:S(2)}, u32[]{:S(2)}) %collective-permute-start.1) | collective-permute-done | bytes 204832 | tf_op jit(solution)/shard_map/cond/branch_1_fun/cond/branch_1_fun/cond/branch_1_fun/ppermute | solution.py:41
  58.4 0.0 copy-done.2
  58.4 1.7 %forward_output.1 = (bf16[128,3072]{1,0:T(8,128)(2,1)}, f32[192,128]{1,0:T(8,128)}, bf16[192,3072]{1,0:T(8,128)(2,1)}) custom-call(f32[400,128]{1,0:T(8,128)S(1)} %add.7.parts_ref, bf16[4,96,3072]{2,1,0:T(8,128)(2,1)S(1)} %get-tuple-element.51.weights_ref, bf16[128,3072]{1,0:T(8,128)(2,1)S(1)} %bitcast.18), custom_call_target="tpu_custom_call" | custom-call | flops 150994944 | bytes 5242880 | tf_op jit(solution)/shard_map/cond/branch_1_fun/cond/branch_1_fun/cond/branch_1_fun/forward_output/pallas_call | solution.py:65
  60.1 5.8 %collective-permute-start.2 = (bf16[128,3072]{1,0:T(8,128)(2,1)}, bf16[128,3072]{1,0:T(8,128)(2,1)}, u32[]{:S(2)}, u32[]{:S(2)}) collective-permute-start(bf16[128,3072]{1,0:T(8,128)(2,1)} %get-tuple-element.129), channel_id=1, source_target_pairs={{0,16},{16,32},{32,48},{48,64},{64,80},{80,96},{96,112},{112,128},... | collective-permute-start | bytes 2359304 | tf_op jit(solution)/shard_map/cond/branch_1_fun/cond/branch_1_fun/cond/branch_1_fun/ppermute | solution.py:223
  65.9 15.8 %collective-permute-done.2 = bf16[128,3072]{1,0:T(8,128)(2,1)} collective-permute-done((bf16[128,3072]{1,0:T(8,128)(2,1)}, bf16[128,3072]{1,0:T(8,128)(2,1)}, u32[]{:S(2)}, u32[]{:S(2)}) %collective-permute-start.2) | collective-permute-done | bytes 786464 | tf_op jit(solution)/shard_map/cond/branch_1_fun/cond/branch_1_fun/cond/branch_1_fun/ppermute | solution.py:223
  81.7 0.0 all-to-all-done
  81.7 0.0 collective-permute-done.4
  81.7 8.9 %collective-permute-done.5 = bf16[128,3072]{1,0:T(8,128)(2,1)} collective-permute-done((bf16[128,3072]{1,0:T(8,128)(2,1)}, bf16[128,3072]{1,0:T(8,128)(2,1)}, u32[]{:S(2)}, u32[]{:S(2)}) %collective-permute-start.5) | collective-permute-done | bytes 786464 | tf_op jit(solution)/shard_map/cond/branch_1_fun/ppermute | solution.py:241
  90.6 0.0 collective-permute-done.7
  90.6 13.9 %conditional.6 = ((bf16[128,3072]{1,0:T(8,128)(2,1)S(1)}, bf16[4,48,3200]{2,1,0:T(8,128)(2,1)})) conditional(s32[]{:T(128)} %convert_element_type.11, () %tuple.53, (bf16[192,3072]{1,0:T(8,128)(2,1)}, bf16[128,3072]{1,0:T(8,128)(2,1)}, bf16[128,3072]{1,0:T(8,128)(2,1)}, bf16[128,3072]{1,0:T(8,128)(2,1)}, f32[192,128]{1,0:T(8,128)}, ...), branch_computations={%region_6.0_spmd, %region_7.0_spmd} | conditional | flops 452984832 | bytes 14323748 | solution.py:49
  90.7 2.6 %second_products.1 = (bf16[208,128]{1,0:T(8,128)(2,1)S(1)}, bf16[128,3072]{1,0:T(8,128)(2,1)S(1)}) custom-call(bf16[192,3072]{1,0:T(8,128)(2,1)} %get-tuple-element.78.up_ref, bf16[128,3072]{1,0:T(8,128)(2,1)} %get-tuple-element.79.refs_0_, bf16[128,3072]{1,0:T(8,128)(2,1)} %get-tuple-element.80.refs_1_, bf16[128,3072]{1,0:T(8,128)(2,1)} %get-tuple-element.81.refs_2_), custom_call_target="tpu_custom_call" | custom-call | flops 150994944 | bytes 5242880 | tf_op jit(solution)/shard_map/cond/branch_1_fun/second_products/pallas_call | solution.py:65
  93.2 8.1 %all_to_all.16.parts_ref = bf16[4,208,128]{2,1,0:T(8,128)(2,1)S(1)} all-to-all(bf16[4,208,128]{2,1,0:T(8,128)(2,1)S(1)} %broadcast_in_dim.39), channel_id=1, replica_groups=mesh['pipe'=32,'dp'=4,'mp'=4] {'mp'}, dimensions={0} | all-to-all | bytes 425984 | tf_op jit(solution)/shard_map/cond/branch_1_fun/all_to_all | solution.py:35
  101.3 0.0 copy-done.1
  101.3 3.3 %input_gradient.1 = (bf16[128,3072]{1,0:T(8,128)(2,1)S(1)}, bf16[4,48,3200]{2,1,0:T(8,128)(2,1)}) custom-call(bf16[4,208,128]{2,1,0:T(8,128)(2,1)S(1)} %all_to_all.16.parts_ref, f32[192,128]{1,0:T(8,128)} %get-tuple-element.83.grad_act_ref, bf16[192,3072]{1,0:T(8,128)(2,1)} %get-tuple-element.78.up_ref, ...), custom_call_target="tpu_custom_call" | custom-call | flops 301989888 | bytes 5242880 | tf_op jit(solution)/shard_map/cond/branch_1_fun/input_gradient/pallas_call | solution.py:65
  104.6 3.7 %collective-permute-start.8 = (bf16[128,3072]{1,0:T(8,128)(2,1)S(1)}, bf16[128,3072]{1,0:T(8,128)(2,1)S(1)}, u32[]{:S(2)}, u32[]{:S(2)}) collective-permute-start(bf16[128,3072]{1,0:T(8,128)(2,1)S(1)} %get-tuple-element.117), channel_id=1, source_target_pairs={{16,0},{32,16},{48,32},{64,48},{80,64},{96,80},{112,96},{128,112},... | collective-permute-start | bytes 2359304 | tf_op jit(solution)/shard_map/ppermute | solution.py:25
  108.3 30.4 %conditional.7 = (bf16[48,3072]{1,0:T(8,128)(2,1)}, bf16[1,48,3072]{2,1,0:T(8,128)(2,1)}, bf16[1,128,3072]{2,1,0:T(8,128)(2,1)}) conditional(s32[]{:T(128)} %convert_element_type.11, () %tuple.52, (bf16[4,48,3200]{2,1,0:T(8,128)(2,1)}, bf16[4,128,3072]{2,1,0:T(8,128)(2,1)}, bf16[128,3072]{1,0:T(8,128)(2,1)}, bf16[128,3072]{1,0:T(8,128)(2,1)}) %tuple.57), branch_computations={%region_8.0_spmd, %region_9.0_spmd} | conditional | flops 151388160 | bytes 14434400 | solution.py:49
  108.3 1.3 collective-permute-start.6
  109.6 4.8 %all-to-all-start.3 = ((bf16[4,48,3200]{2,1,0:T(8,128)(2,1)}), bf16[4,48,3200]{2,1,0:T(8,128)(2,1)S(1)}, u32[]{:S(2)}, u32[]{:S(2)}) async-start(bf16[4,48,3200]{2,1,0:T(8,128)(2,1)} %get-tuple-element.86), calls=%async_computation.3 | async-start | bytes 2457600 | tf_op jit(solution)/shard_map/cond/branch_1_fun/all_to_all | solution.py:254
  114.4 18.7 %collective-permute-done.6 = bf16[128,3072]{1,0:T(8,128)(2,1)} collective-permute-done((bf16[128,3072]{1,0:T(8,128)(2,1)}, bf16[128,3072]{1,0:T(8,128)(2,1)}, u32[]{:S(2)}, u32[]{:S(2)}) %collective-permute-start.6) | collective-permute-done | bytes 786464 | tf_op jit(solution)/shard_map/cond/branch_1_fun/ppermute | solution.py:253
  133.1 2.3 %add_bitcast_fusion = bf16[1,128,3072]{2,1,0:T(8,128)(2,1)} fusion(bf16[128,3072]{1,0:T(8,128)(2,1)} %get-tuple-element.90, bf16[128,3072]{1,0:T(8,128)(2,1)} %collective-permute-done.6), kind=kLoop, calls=%fused_computation.1 | loop fusion | flops 393216 | bytes 2359296 | tf_op jit(solution)/shard_map/broadcast_in_dim | solution.py:271
  135.4 0.0 all-to-all-done.3.terms_ref
  135.4 3.3 %weight_gradients.1 = (bf16[48,3072]{1,0:T(8,128)(2,1)}, bf16[48,3072]{1,0:T(8,128)(2,1)}) custom-call(bf16[4,48,3200]{2,1,0:T(8,128)(2,1)S(1)} %all-to-all-done.3.terms_ref, bf16[4,128,3072]{2,1,0:T(8,128)(2,1)} %get-tuple-element.87.cotangents_ref), custom_call_target="tpu_custom_call" | custom-call | flops 150994944 | bytes 5242880 | tf_op jit(solution)/shard_map/cond/branch_1_fun/weight_gradients/pallas_call | solution.py:65
  138.7 5.3 %collective-permute-done.8 = bf16[128,3072]{1,0:T(8,128)(2,1)S(1)} collective-permute-done((bf16[128,3072]{1,0:T(8,128)(2,1)S(1)}, bf16[128,3072]{1,0:T(8,128)(2,1)S(1)}, u32[]{:S(2)}, u32[]{:S(2)}) %collective-permute-start.8) | collective-permute-done | bytes 786464 | tf_op jit(solution)/shard_map/ppermute | solution.py:25
  143.9 0.9 copy.54
  (4 shorter events, 0.1 us)
Async XLA Ops:
  0.6 90.0 %collective-permute-start.7 = (bf16[128,3072]{1,0:T(8,128)(2,1)}, bf16[128,3072]{1,0:T(8,128)(2,1)}, u32[]{:S(2)}, u32[]{:S(2)}) collective-permute-start(bf16[128,3072]{1,0:T(8,128)(2,1)} %bitcast.24), channel_id=1, source_target_pairs={{320,176},{336,160},{352,144},{368,128},{384,112},{400,96},{416,80... | collective-permute-start | bytes 2359304 | tf_op jit(solution)/shard_map/ppermute | solution.py:262
  2.3 1.1 copy-start.3
  5.1 27.5 %copy-start = (bf16[128,3072]{1,0:T(8,128)(2,1)S(1)}, bf16[128,3072]{1,0:T(8,128)(2,1)}, u32[]{:S(2)}) copy-start(bf16[128,3072]{1,0:T(8,128)(2,1)} %get-tuple-element.68) | copy-start | bytes 2359300 | tf_op jit(solution)/shard_map/cond
  5.1 32.7 %all-to-all-start.2 = ((bf16[4,96,3072]{2,1,0:T(8,128)(2,1)}), bf16[4,96,3072]{2,1,0:T(8,128)(2,1)S(1)}, u32[]{:S(2)}, u32[]{:S(2)}) async-start(bf16[4,96,3072]{2,1,0:T(8,128)(2,1)} %pad_maximum_fusion), calls=%async_computation.2 | async-start | bytes 4718592 | tf_op jit(solution)/shard_map/cond/branch_1_fun/all_to_all | solution.py:236
  10.2 22.4 %collective-permute-start.3 = (bf16[128,3072]{1,0:T(8,128)(2,1)}, bf16[128,3072]{1,0:T(8,128)(2,1)}, u32[]{:S(2)}, u32[]{:S(2)}) collective-permute-start(bf16[128,3072]{1,0:T(8,128)(2,1)} %get-tuple-element.70), channel_id=1, source_target_pairs={{0,16},{16,0},{32,48},{48,32},{192,208},{208,192},{224,240},{240,2... | collective-permute-start | bytes 2359304 | tf_op jit(solution)/shard_map/cond/branch_1_fun/ppermute | solution.py:237
  15.1 66.6 %collective-permute-start.4 = (bf16[128,3072]{1,0:T(8,128)(2,1)}, bf16[128,3072]{1,0:T(8,128)(2,1)}, u32[]{:S(2)}, u32[]{:S(2)}) collective-permute-start(bf16[128,3072]{1,0:T(8,128)(2,1)} %get-tuple-element.70), channel_id=1, source_target_pairs={{64,432},{80,416},{96,400},{112,384},{128,368},{144,352},{160,336}... | collective-permute-start | bytes 2359304 | tf_op jit(solution)/shard_map/cond/branch_1_fun/ppermute | solution.py:240
  34.7 56.0 %collective-permute-start.5 = (bf16[128,3072]{1,0:T(8,128)(2,1)}, bf16[128,3072]{1,0:T(8,128)(2,1)}, u32[]{:S(2)}, u32[]{:S(2)}) collective-permute-start(bf16[128,3072]{1,0:T(8,128)(2,1)} %collective-permute-done.3), channel_id=1, source_target_pairs={{16,496},{0,480},{48,464},{32,448},{208,304},{192,288},{240,272},{... | collective-permute-start | bytes 2359304 | tf_op jit(solution)/shard_map/cond/branch_1_fun/ppermute | solution.py:241
  37.8 43.9 %all-to-all-start = ((bf16[4,128,3072]{2,1,0:T(8,128)(2,1)}), bf16[4,128,3072]{2,1,0:T(8,128)(2,1)}, u32[]{:S(2)}, u32[]{:S(2)}) async-start(bf16[4,128,3072]{2,1,0:T(8,128)(2,1)} %get-tuple-element.64), calls=%async_computation | async-start | bytes 6291456 | tf_op jit(solution)/shard_map/cond/branch_1_fun/cond/branch_1_fun/all_to_all | solution.py:228
  45.8 12.6 %copy-start.2 = (bf16[1,128,3072]{2,1,0:T(8,128)(2,1)S(1)}, bf16[1,128,3072]{2,1,0:T(8,128)(2,1)}, u32[]{:S(2)}) copy-start(bf16[1,128,3072]{2,1,0:T(8,128)(2,1)} %get-tuple-element.52) | copy-start | bytes 2359300 | tf_op jit(solution)/shard_map/cond/branch_1_fun/cond/branch_1_fun/cond
  45.8 3.5 %collective-permute-start = (f32[400,128]{1,0:T(8,128)S(1)}, f32[400,128]{1,0:T(8,128)S(1)}, u32[]{:S(2)}, u32[]{:S(2)}) collective-permute-start(f32[400,128]{1,0:T(8,128)S(1)} %first_products.1), channel_id=1, source_target_pairs={{0,1},{1,0},{2,3},{3,2},{4,5},{5,4},{6,7},{7,6},{8,9},{9,8},{10,11... | collective-permute-start | bytes 614408 | tf_op jit(solution)/shard_map/cond/branch_1_fun/cond/branch_1_fun/cond/branch_1_fun/ppermute | solution.py:41
  49.4 9.0 %collective-permute-start.1 = (f32[400,128]{1,0:T(8,128)S(1)}, f32[400,128]{1,0:T(8,128)S(1)}, u32[]{:S(2)}, u32[]{:S(2)}) collective-permute-start(f32[400,128]{1,0:T(8,128)S(1)} %add.6), channel_id=1, source_target_pairs={{0,2},{1,3},{2,0},{3,1},{4,6},{5,7},{6,4},{7,5},{8,10},{9,11},{10,... | collective-permute-start | bytes 614408 | tf_op jit(solution)/shard_map/cond/branch_1_fun/cond/branch_1_fun/cond/branch_1_fun/ppermute | solution.py:41
  60.1 21.6 %collective-permute-start.2 = (bf16[128,3072]{1,0:T(8,128)(2,1)}, bf16[128,3072]{1,0:T(8,128)(2,1)}, u32[]{:S(2)}, u32[]{:S(2)}) collective-permute-start(bf16[128,3072]{1,0:T(8,128)(2,1)} %get-tuple-element.129), channel_id=1, source_target_pairs={{0,16},{16,32},{32,48},{48,64},{64,80},{80,96},{96,112},{112,128},... | collective-permute-start | bytes 2359304 | tf_op jit(solution)/shard_map/cond/branch_1_fun/cond/branch_1_fun/cond/branch_1_fun/ppermute | solution.py:223
  90.7 10.7 %copy-start.1 = (bf16[128,3072]{1,0:T(8,128)(2,1)S(1)}, bf16[128,3072]{1,0:T(8,128)(2,1)}, u32[]{:S(2)}) copy-start(bf16[128,3072]{1,0:T(8,128)(2,1)} %get-tuple-element.85.cotangent_ref) | copy-start | bytes 2359300 | tf_op jit(solution)/shard_map/cond
  104.6 39.4 %collective-permute-start.8 = (bf16[128,3072]{1,0:T(8,128)(2,1)S(1)}, bf16[128,3072]{1,0:T(8,128)(2,1)S(1)}, u32[]{:S(2)}, u32[]{:S(2)}) collective-permute-start(bf16[128,3072]{1,0:T(8,128)(2,1)S(1)} %get-tuple-element.117), channel_id=1, source_target_pairs={{16,0},{32,16},{48,32},{64,48},{80,64},{96,80},{112,96},{128,112},... | collective-permute-start | bytes 2359304 | tf_op jit(solution)/shard_map/ppermute | solution.py:25
  108.3 24.8 %collective-permute-start.6 = (bf16[128,3072]{1,0:T(8,128)(2,1)}, bf16[128,3072]{1,0:T(8,128)(2,1)}, u32[]{:S(2)}, u32[]{:S(2)}) collective-permute-start(bf16[128,3072]{1,0:T(8,128)(2,1)} %get-tuple-element.91), channel_id=1, source_target_pairs={{240,256},{241,257},{242,258},{243,259},{244,260},{245,261},{246,2... | collective-permute-start | bytes 2359304 | tf_op jit(solution)/shard_map/cond/branch_1_fun/ppermute | solution.py:253
  109.6 25.8 %all-to-all-start.3 = ((bf16[4,48,3200]{2,1,0:T(8,128)(2,1)}), bf16[4,48,3200]{2,1,0:T(8,128)(2,1)S(1)}, u32[]{:S(2)}, u32[]{:S(2)}) async-start(bf16[4,48,3200]{2,1,0:T(8,128)(2,1)} %get-tuple-element.86), calls=%async_computation.3 | async-start | bytes 2457600 | tf_op jit(solution)/shard_map/cond/branch_1_fun/all_to_all | solution.py:254

commit v4 on v3

--- a/solution.py
+++ b/solution.py
@@ -25,9 +25,14 @@
     return lax.ppermute(block, axis, route)
 
 
-def near_sections(count):
-    planes = count // 2
-    return [i for i in range(count) if min((2 * (i // 2) + 1) % planes, -(2 * (i // 2) + 1) % planes) <= 3]
+def stash_routes(count):
+    planes, middle = count // 2, count // 2
+    near = [i for i in range(count) if min((2 * (i // 2) + 1) % planes, -(2 * (i // 2) + 1) % planes) <= 3]
+    below = [middle - 2, middle - 1]
+    first = [i for i in range(middle, count) if i not in near] + below
+    second = [i for i in range(middle) if i not in near]
+    crossing = [i for i in near if i not in below]
+    return [[(i, count - 1 - i) for i in sources] for sources in (first, second, crossing)]
 
 
 def spread(block, axis):
@@ -60,11 +65,12 @@
     return (hidden * sigmoid_value, sigmoid_value * (1.0 + hidden * (1.0 - sigmoid_value)))
 
 
-def call(kernel, name, args, out_shape, scratch, flops):
+def call(kernel, name, args, out_shape, scratch, flops, fetched=()):
     in_vmem = pl.BlockSpec(memory_space=pltpu.VMEM)
+    anywhere = pl.BlockSpec(memory_space=pl.ANY)
     return pl.pallas_call(
         kernel,
-        in_specs=[in_vmem] * len(args),
+        in_specs=[anywhere if i in fetched else in_vmem for i in range(len(args))],
         out_specs=jax.tree.map(lambda _: in_vmem, out_shape),
         out_shape=out_shape,
         scratch_shapes=scratch,
@@ -125,13 +131,32 @@
     )
 
 
-def second_kernel(up_ref, *refs):
-    *input_refs, out_ref, sum_ref = refs
-    rank = up_ref.shape[0]
+def second_kernel(up_hbm, first_ref, second_ref, crossed_ref, out_ref, returned_ref, up_ref, done):
+    rank, features = up_ref.shape
+    section = lax.axis_index("pipe")
+    kind = 0
+    for k, routes in enumerate(stash_routes(lax.axis_size("pipe"))):
+        kind += k * sum((section == target).astype(jnp.int32) for _, target in routes)
+
+    def up_copy(k, tile):
+        return pltpu.make_async_copy(up_hbm.at[:, tile], up_ref.at[:, tile], done.at[0, k])
+
+    def returned_copy(ref, k, tile):
+        return pltpu.make_async_copy(ref.at[:, tile], returned_ref.at[:, tile], done.at[1, k])
+
+    for k, tile in enumerate(tiles(features)):
+        up_copy(k, tile).start()
+        for i, ref in enumerate((first_ref, second_ref, crossed_ref)):
+
+            @pl.when(kind == i)
+            def _(ref=ref, k=k, tile=tile):
+                returned_copy(ref, k, tile).start()
+
     product = squares = 0.0
-    for tile in tiles(up_ref.shape[1]):
-        inputs = sum(ref[:, tile] for ref in input_refs)
-        sum_ref[:, tile] = inputs
+    for k, tile in enumerate(tiles(features)):
+        up_copy(k, tile).wait()
+        returned_copy(first_ref, k, tile).wait()
+        inputs = returned_ref[:, tile]
         product += dot(up_ref[:, tile], inputs, 1, 1)
         squares += squares_of(inputs)
     out_ref[:rank, :] = product.astype(out_ref.dtype)
@@ -143,7 +168,9 @@
     rows = inputs[0].shape[0]
     return call(
         second_kernel, "second_products", (up_full, *inputs),
-        [struct(rank + EXTRA, rows), struct(rows, features)], [], 2 * rank * rows * features,
+        [struct(rank + EXTRA, rows), struct(rows, features)],
+        [pltpu.VMEM(up_full.shape, jnp.bfloat16), pltpu.SemaphoreType.DMA((2, features // TILE))],
+        2 * rank * rows * features, (0, 1, 2, 3),
     )
 
 
@@ -219,9 +246,7 @@
 def forward(weights, forward_in, cotangent):
     parts = summed(first_products(weights, forward_in, cotangent), "mp")
     output, grad_act, up_full = forward_output(parts, weights, forward_in)
-    count = lax.axis_size("pipe")
-    act_next = lax.ppermute(output, "pipe", [(i - 1, i) for i in range(1, count) if i != count // 2])
-    return act_next, output, grad_act, up_full
+    return shifted(output, "pipe", 1), grad_act, up_full
 
 
 def beside(weights, copies, forward_in, cotangent):
@@ -230,17 +255,17 @@
 
 
 def ahead(forward_in, cotangent, up_proj, down_proj, stash):
-    count, group = lax.axis_size("pipe"), lax.axis_size("dp")
-    near = near_sections(count)
+    group = lax.axis_size("dp")
+    _, second, crossing = stash_routes(lax.axis_size("pipe"))
     copies = [jnp.broadcast_to(w[None], (group,) + w.shape) for w in (up_proj, down_proj)]
     weights = lax.all_to_all(jnp.concatenate(copies, 1), "dp", split_axis=0, concat_axis=0, tiled=True)
-    crossed = lax.ppermute(stash, "pipe", [(i, i ^ 1) for i in near])
+    crossed = lax.ppermute(stash, "pipe", [(i, i ^ 1) for i, _ in crossing])
     copies = jnp.broadcast_to(cotangent[None], (group,) + cotangent.shape)
     copies, crossed = lax.optimization_barrier((copies, crossed))
-    returned_far = lax.ppermute(stash, "pipe", [(i, count - 1 - i) for i in range(count // 2) if i not in near])
-    returned_near = lax.ppermute(crossed, "pipe", [(i ^ 1, count - 1 - i) for i in near])
-    act_next, output, grad_act, up_full, cotangents = staged("mp", beside, weights, copies, forward_in, cotangent)
-    return act_next, output, grad_act, up_full, cotangents, returned_far, returned_near
+    returned_second = lax.ppermute(stash, "pipe", second)
+    returned_crossed = lax.ppermute(crossed, "pipe", [(i ^ 1, target) for i, target in crossing])
+    act_next, grad_act, up_full, cotangents = staged("mp", beside, weights, copies, forward_in, cotangent)
+    return act_next, grad_act, up_full, cotangents, returned_second, returned_crossed
 
 
 def backward(returned, cotangent, up_full, grad_act):
@@ -248,26 +273,29 @@
     return input_gradient(spread(parts, "mp"), grad_act, up_full, returned, cotangent)
 
 
-def last_terms(terms, cotangents, act_next, output):
-    middle = lax.axis_size("pipe") // 2
-    act_middle = lax.ppermute(output, "pipe", [(middle - 1, middle)])
+def hold_kernel(source_ref, out_ref):
+    out_ref[...] = source_ref[...]
+
+
+def held(block):
+    return call(hold_kernel, "held", (block,), struct(*block.shape), [], 0)
+
+
+def last_terms(terms, cotangents, act_next):
     terms = lax.all_to_all(terms, "dp", split_axis=0, concat_axis=0, tiled=True)
-    return *weight_gradients(terms, cotangents), act_next + act_middle
+    return *weight_gradients(terms, cotangents), held(act_next)
 
 
 def shards(act_in, grad_in, stash_far, up_proj, down_proj):
     cotangent = grad_in[0]
-    count = lax.axis_size("pipe")
-    near = near_sections(count)
-    returned = lax.ppermute(
-        stash_far[0], "pipe", [(i, count - 1 - i) for i in range(count // 2, count) if i not in near]
-    )
-    act_next, output, grad_act, up_full, cotangents, *returned_later = staged(
+    first = stash_routes(lax.axis_size("pipe"))[0]
+    returned = lax.ppermute(stash_far[0], "pipe", first)
+    act_next, grad_act, up_full, cotangents, *returned_later = staged(
         "dp", ahead, act_in[0], cotangent, up_proj[0].T, down_proj[0], stash_far[0]
     )
     grad_input, terms = staged("dp", backward, [returned, *returned_later], cotangent, up_full, grad_act)
     grad_prev = shifted(grad_input, "pipe", -1)
-    up_grad, down_grad, act_next = staged("dp", last_terms, terms, cotangents, act_next, output)
+    up_grad, down_grad, act_next = staged("dp", last_terms, terms, cotangents, act_next)
     return act_next[None], grad_prev[None], up_grad.T[None], down_grad[None]
 
 

time: 146 us -> 138 us (0.945)
  the two profiles are of different devices: /device:TPU:264 before, /device:TPU:32 now
where the time goes in v4:
time: 138 us; the launch traced here: 137 us
  waiting for transfers between devices  56.1 us (41%)
  starting transfers between devices  52.4 us (38%)
  Pallas kernels  14.2 us (10%)
  blocking collectives  8.06 us (6%)
  local copies, waits for them, and re-layouts  4.2 us (3%)
  other arithmetic  1.63 us (1%)
    ppermute x2, waiting for transfers between devices, shifted(): return lax.ppermute(block, axis, route)  18.3 us
    ppermute x1, waiting for transfers between devices, ahead(): crossed = lax.ppermute(stash, 'pipe', [(i, i ^ 1) for i, _ in crossing])  16.2 us
    all_to_all x1, waiting for transfers between devices, last_terms(): terms = lax.all_to_all(terms, 'dp', split_axis=0, concat_axis=0, tiled=True)  14.5 us
    pallas_call x6, Pallas kernels, call(): pl.pallas_call(kernel, in_specs=[anywhere if i in fetched else in_vmem fo...  14.2 us
    ppermute x2, starting transfers between devices, shifted(): return lax.ppermute(block, axis, route)  13.6 us
    ppermute x1, starting transfers between devices, ahead(): lax.ppermute(crossed, 'pipe', [(i ^ 1, target) for i, target in crossing])  11.4 us
    all_to_all x1, blocking collectives, spread(): return lax.all_to_all(copies, axis, split_axis=0, concat_axis=0, tiled=True)  8.06 us
    ppermute x2, waiting for transfers between devices, summed(): lax.ppermute(block, axis, [(i, i ^ distance) for i in range(size)])  7.02 us
  transfers between devices with their start and end apart: 11, of which 5 were waited for; matrix products, arithmetic and copies ran while one was open for 4% of the time, Pallas kernels for 6%

profile of v4, /device:TPU:32, one launch (start us, length us, event | category | flops | bytes accessed | tf_op | source)
XLA Modules:
  0.0 137.3 jit_solution(9396624912144211049)
XLA Ops:
  0.6 1.6 %collective-permute-start.6 = (bf16[128,3072]{1,0:T(8,128)(2,1)}, bf16[128,3072]{1,0:T(8,128)(2,1)}, u32[]{:S(2)}, u32[]{:S(2)}) collective-permute-start(bf16[128,3072]{1,0:T(8,128)(2,1)} %bitcast.23), channel_id=1, source_target_pairs={{320,176},{336,160},{352,144},{368,128},{384,112},{400,96},{416,80... | collective-permute-start | bytes 2359304 | tf_op jit(solution)/shard_map/ppermute | solution.py:292
  2.3 87.5 %conditional.5 = (bf16[128,3072]{1,0:T(8,128)(2,1)}, f32[192,128]{1,0:T(8,128)}, bf16[192,3072]{1,0:T(8,128)(2,1)}, bf16[4,128,3072]{2,1,0:T(8,128)(2,1)}, bf16[...) conditional(s32[]{:T(128)} %convert_element_type.11, () %tuple.54, (bf16[1,128,3072]{2,1,0:T(8,128)(2,1)}, ...), branch_computations={%region_0.0_spmd, %region_1.0_spmd} | conditional | flops 457805824 | bytes 61522536 | solution.py:54
  2.3 0.0 copy-start.3
  2.3 1.1 broadcast_in_dim.30
  3.4 0.0 copy-done.3
  3.4 0.1 broadcast_in_dim.36
  3.5 1.6 %pad_maximum_fusion = bf16[4,96,3072]{2,1,0:T(8,128)(2,1)} fusion(bf16[4,48,3072]{2,1,0:T(8,128)(2,1)S(1)} %broadcast_in_dim.36, bf16[4,48,3072]{2,1,0:T(8,128)(2,1)S(1)} %broadcast_in_dim.30), kind=kLoop, calls=%fused_computation | loop fusion | flops 4718592 | bytes 4718592 | tf_op jit(solution)/shard_map/cond/branch_1_fun/concatenate | solution.py:261
  5.1 0.0 copy-start
  5.1 4.6 %all-to-all-start.3 = ((bf16[4,96,3072]{2,1,0:T(8,128)(2,1)}), bf16[4,96,3072]{2,1,0:T(8,128)(2,1)S(1)}, u32[]{:S(2)}, u32[]{:S(2)}) async-start(bf16[4,96,3072]{2,1,0:T(8,128)(2,1)} %pad_maximum_fusion), calls=%async_computation.3 | async-start | bytes 4718592 | tf_op jit(solution)/shard_map/cond/branch_1_fun/all_to_all | solution.py:261
  9.7 4.9 %collective-permute-start.3 = (bf16[128,3072]{1,0:T(8,128)(2,1)}, bf16[128,3072]{1,0:T(8,128)(2,1)}, u32[]{:S(2)}, u32[]{:S(2)}) collective-permute-start(bf16[128,3072]{1,0:T(8,128)(2,1)} %get-tuple-element.67), channel_id=1, source_target_pairs={{0,16},{16,0},{32,48},{48,32},{192,208},{208,192},{256,272},{272,2... | collective-permute-start | bytes 2359304 | tf_op jit(solution)/shard_map/cond/branch_1_fun/ppermute | solution.py:262
  14.7 1.6 %collective-permute-start.4 = (bf16[128,3072]{1,0:T(8,128)(2,1)}, bf16[128,3072]{1,0:T(8,128)(2,1)}, u32[]{:S(2)}, u32[]{:S(2)}) collective-permute-start(bf16[128,3072]{1,0:T(8,128)(2,1)} %get-tuple-element.67), channel_id=1, source_target_pairs={{64,432},{80,416},{96,400},{112,384},{128,368},{144,352},{160,336}... | collective-permute-start | bytes 2359304 | tf_op jit(solution)/shard_map/cond/branch_1_fun/ppermute | solution.py:265
  16.2 16.2 %collective-permute-done.3 = bf16[128,3072]{1,0:T(8,128)(2,1)} collective-permute-done((bf16[128,3072]{1,0:T(8,128)(2,1)}, bf16[128,3072]{1,0:T(8,128)(2,1)}, u32[]{:S(2)}, u32[]{:S(2)}) %collective-permute-start.3) | collective-permute-done | bytes 786464 | tf_op jit(solution)/shard_map/cond/branch_1_fun/ppermute | solution.py:262
  32.4 0.0 copy-done
  32.4 2.0 %broadcast_in_dim.38 = bf16[4,128,3072]{2,1,0:T(8,128)(2,1)} broadcast(bf16[128,3072]{1,0:T(8,128)(2,1)S(1)} %copy-done), dimensions={1,2} | broadcast | bytes 3932160 | tf_op jit(solution)/shard_map/cond/branch_1_fun/broadcast_in_dim | solution.py:263
  34.5 11.4 %collective-permute-start.5 = (bf16[128,3072]{1,0:T(8,128)(2,1)}, bf16[128,3072]{1,0:T(8,128)(2,1)}, u32[]{:S(2)}, u32[]{:S(2)}) collective-permute-start(bf16[128,3072]{1,0:T(8,128)(2,1)} %collective-permute-done.3), channel_id=1, source_target_pairs={{16,496},{0,480},{48,464},{32,448},{208,304},{192,288},{272,240},{... | collective-permute-start | bytes 2359304 | tf_op jit(solution)/shard_map/cond/branch_1_fun/ppermute | solution.py:266
  45.8 0.0 all-to-all-done.3
  45.9 43.9 %conditional.1 = (bf16[128,3072]{1,0:T(8,128)(2,1)}, f32[192,128]{1,0:T(8,128)}, bf16[192,3072]{1,0:T(8,128)(2,1)}, bf16[4,128,3072]{2,1,0:T(8,128)(2,1)}) conditional(s32[]{:T(128)} %convert_element_type.6, () %tuple.37, (bf16[1,128,3072]{2,1,0:T(8,128)(2,1)}, bf16[4,96,3072]{2,1,0:T(8,128)(2,1)S(1)}, bf16[128,3072]{1,0:T(8,128)(2,1)S(1)}, ...), branch_computations={%region_2.0_spmd, %region_3.0_spmd} | conditional | flops 453087232 | bytes 29081894 | solution.py:54
  45.9 4.7 %all-to-all-start = ((bf16[4,128,3072]{2,1,0:T(8,128)(2,1)}), bf16[4,128,3072]{2,1,0:T(8,128)(2,1)}, u32[]{:S(2)}, u32[]{:S(2)}) async-start(bf16[4,128,3072]{2,1,0:T(8,128)(2,1)} %get-tuple-element.61), calls=%async_computation | async-start | bytes 6291456 | tf_op jit(solution)/shard_map/cond/branch_1_fun/cond/branch_1_fun/all_to_all | solution.py:253
  50.5 39.2 %conditional = (bf16[128,3072]{1,0:T(8,128)(2,1)}, f32[192,128]{1,0:T(8,128)}, bf16[192,3072]{1,0:T(8,128)(2,1)}) conditional(s32[]{:T(128)} %convert_element_type.2, () %tuple.34, (bf16[1,128,3072]{2,1,0:T(8,128)(2,1)}, bf16[4,96,3072]{2,1,0:T(8,128)(2,1)S(1)}, bf16[128,3072]{1,0:T(8,128)(2,1)S(1)}) %tuple.35), branch_computations={%region_4.0_spmd, %region_5.0_spmd} | conditional | flops 453087232 | bytes 19644588 | solution.py:54
  50.5 1.9 %first_products.1 = f32[400,128]{1,0:T(8,128)S(1)} custom-call(bf16[4,96,3072]{2,1,0:T(8,128)(2,1)S(1)} %get-tuple-element.49.weights_ref, bf16[128,3072]{1,0:T(8,128)(2,1)} %bitcast.16, bf16[128,3072]{1,0:T(8,128)(2,1)S(1)} %get-tuple-element.51.cotangent_ref), custom_call_target="tpu_custom_call" | custom-call | flops 301989888 | bytes 5242880 | tf_op jit(solution)/shard_map/cond/branch_1_fun/cond/branch_1_fun/cond/branch_1_fun/first_products/pallas_call | solution.py:71
  52.5 0.0 copy-start.2
  52.5 2.1 %collective-permute-start = (f32[400,128]{1,0:T(8,128)S(1)}, f32[400,128]{1,0:T(8,128)S(1)}, u32[]{:S(2)}, u32[]{:S(2)}) collective-permute-start(f32[400,128]{1,0:T(8,128)S(1)} %first_products.1), channel_id=1, source_target_pairs={{0,1},{1,0},{2,3},{3,2},{4,5},{5,4},{6,7},{7,6},{8,9},{9,8},{10,11... | collective-permute-start | bytes 614408 | tf_op jit(solution)/shard_map/cond/branch_1_fun/cond/branch_1_fun/cond/branch_1_fun/ppermute | solution.py:46
  54.5 1.4 %collective-permute-done = f32[400,128]{1,0:T(8,128)S(1)} collective-permute-done((f32[400,128]{1,0:T(8,128)S(1)}, f32[400,128]{1,0:T(8,128)S(1)}, u32[]{:S(2)}, u32[]{:S(2)}) %collective-permute-start) | collective-permute-done | bytes 204832 | tf_op jit(solution)/shard_map/cond/branch_1_fun/cond/branch_1_fun/cond/branch_1_fun/ppermute | solution.py:46
  56.0 3.4 %collective-permute-start.1 = (f32[400,128]{1,0:T(8,128)S(1)}, f32[400,128]{1,0:T(8,128)S(1)}, u32[]{:S(2)}, u32[]{:S(2)}) collective-permute-start(f32[400,128]{1,0:T(8,128)S(1)} %add.4), channel_id=1, source_target_pairs={{0,2},{1,3},{2,0},{3,1},{4,6},{5,7},{6,4},{7,5},{8,10},{9,11},{10,... | collective-permute-start | bytes 614408 | tf_op jit(solution)/shard_map/cond/branch_1_fun/cond/branch_1_fun/cond/branch_1_fun/ppermute | solution.py:46
  59.4 5.6 %collective-permute-done.1 = f32[400,128]{1,0:T(8,128)S(1)} collective-permute-done((f32[400,128]{1,0:T(8,128)S(1)}, f32[400,128]{1,0:T(8,128)S(1)}, u32[]{:S(2)}, u32[]{:S(2)}) %collective-permute-start.1) | collective-permute-done | bytes 204832 | tf_op jit(solution)/shard_map/cond/branch_1_fun/cond/branch_1_fun/cond/branch_1_fun/ppermute | solution.py:46
  65.0 0.0 copy-done.2
  65.0 1.4 %forward_output.1 = (bf16[128,3072]{1,0:T(8,128)(2,1)S(1)}, f32[192,128]{1,0:T(8,128)}, bf16[192,3072]{1,0:T(8,128)(2,1)}) custom-call(f32[400,128]{1,0:T(8,128)S(1)} %add.5.parts_ref, bf16[4,96,3072]{2,1,0:T(8,128)(2,1)S(1)} %get-tuple-element.49.weights_ref, bf16[128,3072]{1,0:T(8,128)(2,1)S(1)} %bitcast.17), custom_call_target="tpu_custom_call" | custom-call | flops 150994944 | bytes 5242880 | tf_op jit(solution)/shard_map/cond/branch_1_fun/cond/branch_1_fun/cond/branch_1_fun/forward_output/pallas_call | solution.py:71
  66.5 4.9 %collective-permute-start.2 = (bf16[128,3072]{1,0:T(8,128)(2,1)S(1)}, bf16[128,3072]{1,0:T(8,128)(2,1)}, u32[]{:S(2)}, u32[]{:S(2)}) collective-permute-start(bf16[128,3072]{1,0:T(8,128)(2,1)S(1)} %get-tuple-element.52), channel_id=1, source_target_pairs={{0,16},{16,32},{32,48},{48,64},{64,80},{80,96},{96,112},{112,128},... | collective-permute-start | bytes 2359304 | tf_op jit(solution)/shard_map/cond/branch_1_fun/cond/branch_1_fun/cond/branch_1_fun/ppermute | solution.py:25
  71.4 18.3 %collective-permute-done.2 = bf16[128,3072]{1,0:T(8,128)(2,1)} collective-permute-done((bf16[128,3072]{1,0:T(8,128)(2,1)S(1)}, bf16[128,3072]{1,0:T(8,128)(2,1)}, u32[]{:S(2)}, u32[]{:S(2)}) %collective-permute-start.2) | collective-permute-done | bytes 786464 | tf_op jit(solution)/shard_map/cond/branch_1_fun/cond/branch_1_fun/cond/branch_1_fun/ppermute | solution.py:25
  89.7 0.0 all-to-all-done
  89.7 0.0 collective-permute-done.4
  89.7 0.0 collective-permute-done.5
  89.8 0.0 collective-permute-done.6
  89.8 13.6 %conditional.6 = ((bf16[128,3072]{1,0:T(8,128)(2,1)S(1)}, bf16[4,48,3200]{2,1,0:T(8,128)(2,1)})) conditional(s32[]{:T(128)} %convert_element_type.11, () %tuple.53, (bf16[192,3072]{1,0:T(8,128)(2,1)}, bf16[128,3072]{1,0:T(8,128)(2,1)}, bf16[128,3072]{1,0:T(8,128)(2,1)}, bf16[128,3072]{1,0:T(8,128)(2,1)}, f32[192,128]{1,0:T(8,128)}, ...), branch_computations={%region_6.0_spmd, %region_7.0_spmd} | conditional | flops 452984832 | bytes 14323748 | solution.py:54
  89.8 0.0 copy-start.1
  89.8 2.2 %second_products.1 = (bf16[208,128]{1,0:T(8,128)(2,1)S(1)}, bf16[128,3072]{1,0:T(8,128)(2,1)S(1)}) custom-call(bf16[192,3072]{1,0:T(8,128)(2,1)} %get-tuple-element.74.up_hbm.up_ref, bf16[128,3072]{1,0:T(8,128)(2,1)} %get-tuple-element.75.first_ref, bf16[128,3072]{1,0:T(8,128)(2,1)} %get-tuple-element.76.second_ref, ...), custom_call_target="tpu_custom_call" | custom-call | flops 150994944 | bytes 5242880 | tf_op jit(solution)/shard_map/cond/branch_1_fun/second_products/pallas_call | solution.py:71
  92.0 8.1 %all_to_all.16.parts_ref = bf16[4,208,128]{2,1,0:T(8,128)(2,1)S(1)} all-to-all(bf16[4,208,128]{2,1,0:T(8,128)(2,1)S(1)} %broadcast_in_dim.39), channel_id=1, replica_groups=mesh['pipe'=32,'dp'=4,'mp'=4] {'mp'}, dimensions={0} | all-to-all | bytes 425984 | tf_op jit(solution)/shard_map/cond/branch_1_fun/all_to_all | solution.py:40
  100.1 0.0 copy-done.1
  100.1 3.3 %input_gradient.1 = (bf16[128,3072]{1,0:T(8,128)(2,1)S(1)}, bf16[4,48,3200]{2,1,0:T(8,128)(2,1)}) custom-call(bf16[4,208,128]{2,1,0:T(8,128)(2,1)S(1)} %all_to_all.16.parts_ref, f32[192,128]{1,0:T(8,128)} %get-tuple-element.79.grad_act_ref, bf16[192,3072]{1,0:T(8,128)(2,1)} %get-tuple-element.74.up_hbm.up_ref, ...), custom_call_target="tpu_custom_call" | custom-call | flops 301989888 | bytes 5242880 | tf_op jit(solution)/shard_map/cond/branch_1_fun/input_gradient/pallas_call | solution.py:71
  103.3 8.7 %collective-permute-start.7 = (bf16[128,3072]{1,0:T(8,128)(2,1)S(1)}, bf16[128,3072]{1,0:T(8,128)(2,1)S(1)}, u32[]{:S(2)}, u32[]{:S(2)}) collective-permute-start(bf16[128,3072]{1,0:T(8,128)(2,1)S(1)} %get-tuple-element.110), channel_id=1, source_target_pairs={{16,0},{32,16},{48,32},{64,48},{80,64},{96,80},{112,96},{128,112},... | collective-permute-start | bytes 2359304 | tf_op jit(solution)/shard_map/ppermute | solution.py:25
  112.0 24.4 %conditional.7 = (bf16[48,3072]{1,0:T(8,128)(2,1)}, bf16[1,48,3072]{2,1,0:T(8,128)(2,1)}, bf16[1,128,3072]{2,1,0:T(8,128)(2,1)}) conditional(s32[]{:T(128)} %convert_element_type.11, () %tuple.52, (bf16[4,48,3200]{2,1,0:T(8,128)(2,1)}, bf16[4,128,3072]{2,1,0:T(8,128)(2,1)}, bf16[128,3072]{1,0:T(8,128)(2,1)}) %tuple.57), branch_computations={%region_8.0_spmd, %region_9.0_spmd} | conditional | flops 150994944 | bytes 14172216 | solution.py:54
  112.0 4.5 %all-to-all-start.2 = ((bf16[4,48,3200]{2,1,0:T(8,128)(2,1)}), bf16[4,48,3200]{2,1,0:T(8,128)(2,1)S(1)}, u32[]{:S(2)}, u32[]{:S(2)}) async-start(bf16[4,48,3200]{2,1,0:T(8,128)(2,1)} %get-tuple-element.82), calls=%async_computation.2 | async-start | bytes 2457600 | tf_op jit(solution)/shard_map/cond/branch_1_fun/all_to_all | solution.py:285
  116.6 2.1 %held.1 = bf16[128,3072]{1,0:T(8,128)(2,1)} custom-call(bf16[128,3072]{1,0:T(8,128)(2,1)} %get-tuple-element.86.source_ref), custom_call_target="tpu_custom_call" | custom-call | bytes 5242880 | tf_op jit(solution)/shard_map/cond/branch_1_fun/held/pallas_call | solution.py:71
  118.6 14.5 %all-to-all-done.2.terms_ref = bf16[4,48,3200]{2,1,0:T(8,128)(2,1)S(1)} async-done(((bf16[4,48,3200]{2,1,0:T(8,128)(2,1)}), bf16[4,48,3200]{2,1,0:T(8,128)(2,1)S(1)}, u32[]{:S(2)}, u32[]{:S(2)}) %all-to-all-start.2) | async-done | bytes 1228832 | tf_op jit(solution)/shard_map/cond/branch_1_fun/all_to_all | solution.py:285
  133.2 3.3 %weight_gradients.1 = (bf16[48,3072]{1,0:T(8,128)(2,1)}, bf16[48,3072]{1,0:T(8,128)(2,1)}) custom-call(bf16[4,48,3200]{2,1,0:T(8,128)(2,1)S(1)} %all-to-all-done.2.terms_ref, bf16[4,128,3072]{2,1,0:T(8,128)(2,1)} %get-tuple-element.83.cotangents_ref), custom_call_target="tpu_custom_call" | custom-call | flops 150994944 | bytes 5242880 | tf_op jit(solution)/shard_map/cond/branch_1_fun/weight_gradients/pallas_call | solution.py:71
  136.4 0.0 collective-permute-done.7
  136.4 0.9 copy.48
  (3 shorter events, 0.1 us)
Async XLA Ops:
  0.6 89.1 %collective-permute-start.6 = (bf16[128,3072]{1,0:T(8,128)(2,1)}, bf16[128,3072]{1,0:T(8,128)(2,1)}, u32[]{:S(2)}, u32[]{:S(2)}) collective-permute-start(bf16[128,3072]{1,0:T(8,128)(2,1)} %bitcast.23), channel_id=1, source_target_pairs={{320,176},{336,160},{352,144},{368,128},{384,112},{400,96},{416,80... | collective-permute-start | bytes 2359304 | tf_op jit(solution)/shard_map/ppermute | solution.py:292
  2.3 1.1 copy-start.3
  5.1 27.3 %copy-start = (bf16[128,3072]{1,0:T(8,128)(2,1)S(1)}, bf16[128,3072]{1,0:T(8,128)(2,1)}, u32[]{:S(2)}) copy-start(bf16[128,3072]{1,0:T(8,128)(2,1)} %get-tuple-element.65) | copy-start | bytes 2359300 | tf_op jit(solution)/shard_map/cond
  5.1 40.7 %all-to-all-start.3 = ((bf16[4,96,3072]{2,1,0:T(8,128)(2,1)}), bf16[4,96,3072]{2,1,0:T(8,128)(2,1)S(1)}, u32[]{:S(2)}, u32[]{:S(2)}) async-start(bf16[4,96,3072]{2,1,0:T(8,128)(2,1)} %pad_maximum_fusion), calls=%async_computation.3 | async-start | bytes 4718592 | tf_op jit(solution)/shard_map/cond/branch_1_fun/all_to_all | solution.py:261
  9.7 22.7 %collective-permute-start.3 = (bf16[128,3072]{1,0:T(8,128)(2,1)}, bf16[128,3072]{1,0:T(8,128)(2,1)}, u32[]{:S(2)}, u32[]{:S(2)}) collective-permute-start(bf16[128,3072]{1,0:T(8,128)(2,1)} %get-tuple-element.67), channel_id=1, source_target_pairs={{0,16},{16,0},{32,48},{48,32},{192,208},{208,192},{256,272},{272,2... | collective-permute-start | bytes 2359304 | tf_op jit(solution)/shard_map/cond/branch_1_fun/ppermute | solution.py:262
  14.7 75.1 %collective-permute-start.4 = (bf16[128,3072]{1,0:T(8,128)(2,1)}, bf16[128,3072]{1,0:T(8,128)(2,1)}, u32[]{:S(2)}, u32[]{:S(2)}) collective-permute-start(bf16[128,3072]{1,0:T(8,128)(2,1)} %get-tuple-element.67), channel_id=1, source_target_pairs={{64,432},{80,416},{96,400},{112,384},{128,368},{144,352},{160,336}... | collective-permute-start | bytes 2359304 | tf_op jit(solution)/shard_map/cond/branch_1_fun/ppermute | solution.py:265
  34.5 55.3 %collective-permute-start.5 = (bf16[128,3072]{1,0:T(8,128)(2,1)}, bf16[128,3072]{1,0:T(8,128)(2,1)}, u32[]{:S(2)}, u32[]{:S(2)}) collective-permute-start(bf16[128,3072]{1,0:T(8,128)(2,1)} %collective-permute-done.3), channel_id=1, source_target_pairs={{16,496},{0,480},{48,464},{32,448},{208,304},{192,288},{272,240},{... | collective-permute-start | bytes 2359304 | tf_op jit(solution)/shard_map/cond/branch_1_fun/ppermute | solution.py:266
  45.9 43.9 %all-to-all-start = ((bf16[4,128,3072]{2,1,0:T(8,128)(2,1)}), bf16[4,128,3072]{2,1,0:T(8,128)(2,1)}, u32[]{:S(2)}, u32[]{:S(2)}) async-start(bf16[4,128,3072]{2,1,0:T(8,128)(2,1)} %get-tuple-element.61), calls=%async_computation | async-start | bytes 6291456 | tf_op jit(solution)/shard_map/cond/branch_1_fun/cond/branch_1_fun/all_to_all | solution.py:253
  52.5 12.6 %copy-start.2 = (bf16[1,128,3072]{2,1,0:T(8,128)(2,1)S(1)}, bf16[1,128,3072]{2,1,0:T(8,128)(2,1)}, u32[]{:S(2)}) copy-start(bf16[1,128,3072]{2,1,0:T(8,128)(2,1)} %get-tuple-element.50) | copy-start | bytes 2359300 | tf_op jit(solution)/shard_map/cond/branch_1_fun/cond/branch_1_fun/cond
  52.5 3.5 %collective-permute-start = (f32[400,128]{1,0:T(8,128)S(1)}, f32[400,128]{1,0:T(8,128)S(1)}, u32[]{:S(2)}, u32[]{:S(2)}) collective-permute-start(f32[400,128]{1,0:T(8,128)S(1)} %first_products.1), channel_id=1, source_target_pairs={{0,1},{1,0},{2,3},{3,2},{4,5},{5,4},{6,7},{7,6},{8,9},{9,8},{10,11... | collective-permute-start | bytes 614408 | tf_op jit(solution)/shard_map/cond/branch_1_fun/cond/branch_1_fun/cond/branch_1_fun/ppermute | solution.py:46
  56.0 9.0 %collective-permute-start.1 = (f32[400,128]{1,0:T(8,128)S(1)}, f32[400,128]{1,0:T(8,128)S(1)}, u32[]{:S(2)}, u32[]{:S(2)}) collective-permute-start(f32[400,128]{1,0:T(8,128)S(1)} %add.4), channel_id=1, source_target_pairs={{0,2},{1,3},{2,0},{3,1},{4,6},{5,7},{6,4},{7,5},{8,10},{9,11},{10,... | collective-permute-start | bytes 614408 | tf_op jit(solution)/shard_map/cond/branch_1_fun/cond/branch_1_fun/cond/branch_1_fun/ppermute | solution.py:46
  66.5 23.3 %collective-permute-start.2 = (bf16[128,3072]{1,0:T(8,128)(2,1)S(1)}, bf16[128,3072]{1,0:T(8,128)(2,1)}, u32[]{:S(2)}, u32[]{:S(2)}) collective-permute-start(bf16[128,3072]{1,0:T(8,128)(2,1)S(1)} %get-tuple-element.52), channel_id=1, source_target_pairs={{0,16},{16,32},{32,48},{48,64},{64,80},{80,96},{96,112},{112,128},... | collective-permute-start | bytes 2359304 | tf_op jit(solution)/shard_map/cond/branch_1_fun/cond/branch_1_fun/cond/branch_1_fun/ppermute | solution.py:25
  89.8 10.3 %copy-start.1 = (bf16[128,3072]{1,0:T(8,128)(2,1)S(1)}, bf16[128,3072]{1,0:T(8,128)(2,1)}, u32[]{:S(2)}) copy-start(bf16[128,3072]{1,0:T(8,128)(2,1)} %get-tuple-element.81.cotangent_ref) | copy-start | bytes 2359300 | tf_op jit(solution)/shard_map/cond
  103.3 33.1 %collective-permute-start.7 = (bf16[128,3072]{1,0:T(8,128)(2,1)S(1)}, bf16[128,3072]{1,0:T(8,128)(2,1)S(1)}, u32[]{:S(2)}, u32[]{:S(2)}) collective-permute-start(bf16[128,3072]{1,0:T(8,128)(2,1)S(1)} %get-tuple-element.110), channel_id=1, source_target_pairs={{16,0},{32,16},{48,32},{64,48},{80,64},{96,80},{112,96},{128,112},... | collective-permute-start | bytes 2359304 | tf_op jit(solution)/shard_map/ppermute | solution.py:25
  112.0 21.1 %all-to-all-start.2 = ((bf16[4,48,3200]{2,1,0:T(8,128)(2,1)}), bf16[4,48,3200]{2,1,0:T(8,128)(2,1)S(1)}, u32[]{:S(2)}, u32[]{:S(2)}) async-start(bf16[4,48,3200]{2,1,0:T(8,128)(2,1)} %get-tuple-element.82), calls=%async_computation.2 | async-start | bytes 2457600 | tf_op jit(solution)/shard_map/cond/branch_1_fun/all_to_all | solution.py:285

commit v5 on v4

--- a/solution.py
+++ b/solution.py
@@ -29,8 +29,9 @@
     planes, middle = count // 2, count // 2
     near = [i for i in range(count) if min((2 * (i // 2) + 1) % planes, -(2 * (i // 2) + 1) % planes) <= 3]
     below = [middle - 2, middle - 1]
-    first = [i for i in range(middle, count) if i not in near] + below
-    second = [i for i in range(middle) if i not in near]
+    wrapping = list(range(count // 4 - 2, count // 4 + 2))
+    first = [i for i in range(middle, count) if i not in near] + below + wrapping
+    second = [i for i in range(middle) if i not in near + wrapping]
     crossing = [i for i in near if i not in below]
     return [[(i, count - 1 - i) for i in sources] for sources in (first, second, crossing)]
 
@@ -43,7 +44,9 @@
 def summed(block, axis):
     size, distance = lax.axis_size(axis), 1
     while distance < size:
-        block = block + lax.ppermute(block, axis, [(i, i ^ distance) for i in range(size)])
+        block = block.astype(jnp.bfloat16) if 2 * distance == size else block
+        far = lax.ppermute(block, axis, [(i, i ^ distance) for i in range(size)])
+        block = block.astype(jnp.float32) + far.astype(jnp.float32)
         distance *= 2
     return block
 

time: 138 us -> 137 us (level)
  the two profiles are of different devices: /device:TPU:32 before, /device:TPU:288 now
where the time goes in v5:
time: 137 us; the launch traced here: 136 us
  waiting for transfers between devices  56.7 us (41%)
  starting transfers between devices  50.8 us (37%)
  Pallas kernels  14.2 us (10%)
  blocking collectives  8.07 us (6%)
  local copies, waits for them, and re-layouts  4.2 us (3%)
  other arithmetic  1.64 us (1%)
    ppermute x2, starting transfers between devices, shifted(): return lax.ppermute(block, axis, route)  21.2 us
    ppermute x2, waiting for transfers between devices, shifted(): return lax.ppermute(block, axis, route)  18.7 us
    ppermute x1, waiting for transfers between devices, ahead(): crossed = lax.ppermute(stash, 'pipe', [(i, i ^ 1) for i, _ in crossing])  16.2 us
    all_to_all x1, waiting for transfers between devices, last_terms(): terms = lax.all_to_all(terms, 'dp', split_axis=0, concat_axis=0, tiled=True)  14.5 us
    pallas_call x6, Pallas kernels, call(): pl.pallas_call(kernel, in_specs=[anywhere if i in fetched else in_vmem fo...  14.2 us
    all_to_all x1, blocking collectives, spread(): return lax.all_to_all(copies, axis, split_axis=0, concat_axis=0, tiled=True)  8.07 us
    ppermute x2, starting transfers between devices, summed(): far = lax.ppermute(block, axis, [(i, i ^ distance) for i in range(size)])  5.45 us
    ppermute x1, starting transfers between devices, ahead(): crossed = lax.ppermute(stash, 'pipe', [(i, i ^ 1) for i, _ in crossing])  4.92 us
  transfers between devices with their start and end apart: 11, of which 6 were waited for; matrix products, arithmetic and copies ran while one was open for 4% of the time, Pallas kernels for 6%

profile of v5, /device:TPU:288, one launch (start us, length us, event | category | flops | bytes accessed | tf_op | source)
XLA Modules:
  0.0 136.3 jit_solution(7481561691200697973)
XLA Ops:
  0.6 1.6 %collective-permute-start.6 = (bf16[128,3072]{1,0:T(8,128)(2,1)}, bf16[128,3072]{1,0:T(8,128)(2,1)}, u32[]{:S(2)}, u32[]{:S(2)}) collective-permute-start(bf16[128,3072]{1,0:T(8,128)(2,1)} %bitcast.23), channel_id=1, source_target_pairs={{320,176},{336,160},{352,144},{368,128},{384,112},{400,96},{416,80... | collective-permute-start | bytes 2359304 | tf_op jit(solution)/shard_map/ppermute | solution.py:295
  2.3 78.6 %conditional.5 = (bf16[128,3072]{1,0:T(8,128)(2,1)}, f32[192,128]{1,0:T(8,128)}, bf16[192,3072]{1,0:T(8,128)(2,1)}, bf16[4,128,3072]{2,1,0:T(8,128)(2,1)}, bf16[...) conditional(s32[]{:T(128)} %convert_element_type.20, () %tuple.54, (bf16[1,128,3072]{2,1,0:T(8,128)(2,1)}, ...), branch_computations={%region_0.0_spmd, %region_1.0_spmd} | conditional | flops 457959424 | bytes 60805736 | solution.py:57
  2.3 0.0 copy-start.3
  2.3 1.1 broadcast_in_dim.30
  3.4 0.0 copy-done.3
  3.4 0.1 broadcast_in_dim.36
  3.5 1.6 %pad_maximum_fusion = bf16[4,96,3072]{2,1,0:T(8,128)(2,1)} fusion(bf16[4,48,3072]{2,1,0:T(8,128)(2,1)S(1)} %broadcast_in_dim.36, bf16[4,48,3072]{2,1,0:T(8,128)(2,1)S(1)} %broadcast_in_dim.30), kind=kLoop, calls=%fused_computation.2 | loop fusion | flops 4718592 | bytes 4718592 | tf_op jit(solution)/shard_map/cond/branch_1_fun/concatenate | solution.py:264
  5.1 0.0 copy-start
  5.1 4.6 %all-to-all-start.3 = ((bf16[4,96,3072]{2,1,0:T(8,128)(2,1)}), bf16[4,96,3072]{2,1,0:T(8,128)(2,1)S(1)}, u32[]{:S(2)}, u32[]{:S(2)}) async-start(bf16[4,96,3072]{2,1,0:T(8,128)(2,1)} %pad_maximum_fusion), calls=%async_computation.3 | async-start | bytes 4718592 | tf_op jit(solution)/shard_map/cond/branch_1_fun/all_to_all | solution.py:264
  9.7 4.9 %collective-permute-start.3 = (bf16[128,3072]{1,0:T(8,128)(2,1)}, bf16[128,3072]{1,0:T(8,128)(2,1)}, u32[]{:S(2)}, u32[]{:S(2)}) collective-permute-start(bf16[128,3072]{1,0:T(8,128)(2,1)} %get-tuple-element.67), channel_id=1, source_target_pairs={{0,16},{16,0},{32,48},{48,32},{192,208},{208,192},{256,272},{272,2... | collective-permute-start | bytes 2359304 | tf_op jit(solution)/shard_map/cond/branch_1_fun/ppermute | solution.py:265
  14.7 1.6 %collective-permute-start.4 = (bf16[128,3072]{1,0:T(8,128)(2,1)}, bf16[128,3072]{1,0:T(8,128)(2,1)}, u32[]{:S(2)}, u32[]{:S(2)}) collective-permute-start(bf16[128,3072]{1,0:T(8,128)(2,1)} %get-tuple-element.67), channel_id=1, source_target_pairs={{64,432},{80,416},{160,336},{176,320},{65,433},{81,417},{161,337},... | collective-permute-start | bytes 2359304 | tf_op jit(solution)/shard_map/cond/branch_1_fun/ppermute | solution.py:268
  16.2 16.2 %collective-permute-done.3 = bf16[128,3072]{1,0:T(8,128)(2,1)} collective-permute-done((bf16[128,3072]{1,0:T(8,128)(2,1)}, bf16[128,3072]{1,0:T(8,128)(2,1)}, u32[]{:S(2)}, u32[]{:S(2)}) %collective-permute-start.3) | collective-permute-done | bytes 786464 | tf_op jit(solution)/shard_map/cond/branch_1_fun/ppermute | solution.py:265
  32.4 0.0 copy-done
  32.4 2.0 %broadcast_in_dim.38 = bf16[4,128,3072]{2,1,0:T(8,128)(2,1)} broadcast(bf16[128,3072]{1,0:T(8,128)(2,1)S(1)} %copy-done), dimensions={1,2} | broadcast | bytes 3932160 | tf_op jit(solution)/shard_map/cond/branch_1_fun/broadcast_in_dim | solution.py:266
  34.5 2.0 %collective-permute-start.5 = (bf16[128,3072]{1,0:T(8,128)(2,1)}, bf16[128,3072]{1,0:T(8,128)(2,1)}, u32[]{:S(2)}, u32[]{:S(2)}) collective-permute-start(bf16[128,3072]{1,0:T(8,128)(2,1)} %collective-permute-done.3), channel_id=1, source_target_pairs={{16,496},{0,480},{48,464},{32,448},{208,304},{192,288},{272,240},{... | collective-permute-start | bytes 2359304 | tf_op jit(solution)/shard_map/cond/branch_1_fun/ppermute | solution.py:269
  36.5 2.4 %all-to-all-done.3 = bf16[4,96,3072]{2,1,0:T(8,128)(2,1)S(1)} async-done(((bf16[4,96,3072]{2,1,0:T(8,128)(2,1)}), bf16[4,96,3072]{2,1,0:T(8,128)(2,1)S(1)}, u32[]{:S(2)}, u32[]{:S(2)}) %all-to-all-start.3) | async-done | bytes 2359328 | tf_op jit(solution)/shard_map/cond/branch_1_fun/all_to_all | solution.py:264
  38.9 42.1 %conditional.1 = (bf16[128,3072]{1,0:T(8,128)(2,1)}, f32[192,128]{1,0:T(8,128)}, bf16[192,3072]{1,0:T(8,128)(2,1)}, bf16[4,128,3072]{2,1,0:T(8,128)(2,1)}) conditional(s32[]{:T(128)} %convert_element_type.18, () %tuple.37, (bf16[1,128,3072]{2,1,0:T(8,128)(2,1)}, bf16[4,96,3072]{2,1,0:T(8,128)(2,1)S(1)}, bf16[128,3072]{1,0:T(8,128)(2,1)S(1)}, ...), branch_computations={%region_2.0_spmd, %region_3.0_spmd} | conditional | flops 453240832 | bytes 28365094 | solution.py:57
  38.9 4.6 %all-to-all-start.2 = ((bf16[4,128,3072]{2,1,0:T(8,128)(2,1)}), bf16[4,128,3072]{2,1,0:T(8,128)(2,1)}, u32[]{:S(2)}, u32[]{:S(2)}) async-start(bf16[4,128,3072]{2,1,0:T(8,128)(2,1)} %get-tuple-element.61), calls=%async_computation.2 | async-start | bytes 6291456 | tf_op jit(solution)/shard_map/cond/branch_1_fun/cond/branch_1_fun/all_to_all | solution.py:256
  43.5 37.4 %conditional = (bf16[128,3072]{1,0:T(8,128)(2,1)}, f32[192,128]{1,0:T(8,128)}, bf16[192,3072]{1,0:T(8,128)(2,1)}) conditional(s32[]{:T(128)} %convert_element_type.17, () %tuple.34, (bf16[1,128,3072]{2,1,0:T(8,128)(2,1)}, bf16[4,96,3072]{2,1,0:T(8,128)(2,1)S(1)}, bf16[128,3072]{1,0:T(8,128)(2,1)S(1)}) %tuple.35), branch_computations={%region_4.0_spmd, %region_5.0_spmd} | conditional | flops 453240832 | bytes 18927788 | solution.py:57
  43.5 1.9 %first_products.1 = f32[400,128]{1,0:T(8,128)S(1)} custom-call(bf16[4,96,3072]{2,1,0:T(8,128)(2,1)S(1)} %get-tuple-element.49.weights_ref, bf16[128,3072]{1,0:T(8,128)(2,1)} %bitcast.16, bf16[128,3072]{1,0:T(8,128)(2,1)S(1)} %get-tuple-element.51.cotangent_ref), custom_call_target="tpu_custom_call" | custom-call | flops 301989888 | bytes 5242880 | tf_op jit(solution)/shard_map/cond/branch_1_fun/cond/branch_1_fun/cond/branch_1_fun/first_products/pallas_call | solution.py:74
  45.5 0.0 copy-start.2
  45.5 2.1 %collective-permute-start = (f32[400,128]{1,0:T(8,128)S(1)}, f32[400,128]{1,0:T(8,128)S(1)}, u32[]{:S(2)}, u32[]{:S(2)}) collective-permute-start(f32[400,128]{1,0:T(8,128)S(1)} %first_products.1), channel_id=1, source_target_pairs={{0,1},{1,0},{2,3},{3,2},{4,5},{5,4},{6,7},{7,6},{8,9},{9,8},{10,11... | collective-permute-start | bytes 614408 | tf_op jit(solution)/shard_map/cond/branch_1_fun/cond/branch_1_fun/cond/branch_1_fun/ppermute | solution.py:48
  47.5 1.4 %collective-permute-done = f32[400,128]{1,0:T(8,128)S(1)} collective-permute-done((f32[400,128]{1,0:T(8,128)S(1)}, f32[400,128]{1,0:T(8,128)S(1)}, u32[]{:S(2)}, u32[]{:S(2)}) %collective-permute-start) | collective-permute-done | bytes 204832 | tf_op jit(solution)/shard_map/cond/branch_1_fun/cond/branch_1_fun/cond/branch_1_fun/ppermute | solution.py:48
  49.0 3.4 %collective-permute-start.1 = (bf16[400,128]{1,0:T(8,128)(2,1)S(1)}, bf16[400,128]{1,0:T(8,128)(2,1)S(1)}, u32[]{:S(2)}, u32[]{:S(2)}) collective-permute-start(bf16[400,128]{1,0:T(8,128)(2,1)S(1)} %add_convert_fusion), channel_id=1, source_target_pairs={{0,2},{1,3},{2,0},{3,1},{4,6},{5,7},{6,4},{7,5},{8,10},{9,11},{10,... | collective-permute-start | bytes 307208 | tf_op jit(solution)/shard_map/cond/branch_1_fun/cond/branch_1_fun/cond/branch_1_fun/ppermute | solution.py:48
  52.4 3.4 %collective-permute-done.1 = bf16[400,128]{1,0:T(8,128)(2,1)S(1)} collective-permute-done((bf16[400,128]{1,0:T(8,128)(2,1)S(1)}, bf16[400,128]{1,0:T(8,128)(2,1)S(1)}, u32[]{:S(2)}, u32[]{:S(2)}) %collective-permute-start.1) | collective-permute-done | bytes 102432 | tf_op jit(solution)/shard_map/cond/branch_1_fun/cond/branch_1_fun/cond/branch_1_fun/ppermute | solution.py:48
  55.8 0.0 copy-done.2
  55.8 1.4 %forward_output.1 = (bf16[128,3072]{1,0:T(8,128)(2,1)S(1)}, f32[192,128]{1,0:T(8,128)}, bf16[192,3072]{1,0:T(8,128)(2,1)}) custom-call(f32[400,128]{1,0:T(8,128)S(1)} %convert_add_fusion.parts_ref, bf16[4,96,3072]{2,1,0:T(8,128)(2,1)S(1)} %get-tuple-element.49.weights_ref, bf16[128,3072]{1,0:T(8,128)(2,1)S(1)} %bitcast.17), custom_call_target="tpu_custom_call" | custom-call | flops 150994944 | bytes 5242880 | tf_op jit(solution)/shard_map/cond/branch_1_fun/cond/branch_1_fun/cond/branch_1_fun/forward_output/pallas_call | solution.py:74
  57.3 4.9 %collective-permute-start.2 = (bf16[128,3072]{1,0:T(8,128)(2,1)S(1)}, bf16[128,3072]{1,0:T(8,128)(2,1)}, u32[]{:S(2)}, u32[]{:S(2)}) collective-permute-start(bf16[128,3072]{1,0:T(8,128)(2,1)S(1)} %get-tuple-element.52), channel_id=1, source_target_pairs={{0,16},{16,32},{32,48},{48,64},{64,80},{80,96},{96,112},{112,128},... | collective-permute-start | bytes 2359304 | tf_op jit(solution)/shard_map/cond/branch_1_fun/cond/branch_1_fun/cond/branch_1_fun/ppermute | solution.py:25
  62.2 18.7 %collective-permute-done.2 = bf16[128,3072]{1,0:T(8,128)(2,1)} collective-permute-done((bf16[128,3072]{1,0:T(8,128)(2,1)S(1)}, bf16[128,3072]{1,0:T(8,128)(2,1)}, u32[]{:S(2)}, u32[]{:S(2)}) %collective-permute-start.2) | collective-permute-done | bytes 786464 | tf_op jit(solution)/shard_map/cond/branch_1_fun/cond/branch_1_fun/cond/branch_1_fun/ppermute | solution.py:25
  80.9 0.0 all-to-all-done.2
  80.9 0.0 collective-permute-done.4
  80.9 0.0 collective-permute-done.5
  80.9 0.0 collective-permute-done.6
  80.9 13.6 %conditional.6 = ((bf16[128,3072]{1,0:T(8,128)(2,1)S(1)}, bf16[4,48,3200]{2,1,0:T(8,128)(2,1)})) conditional(s32[]{:T(128)} %convert_element_type.20, () %tuple.53, (bf16[192,3072]{1,0:T(8,128)(2,1)}, bf16[128,3072]{1,0:T(8,128)(2,1)}, bf16[128,3072]{1,0:T(8,128)(2,1)}, bf16[128,3072]{1,0:T(8,128)(2,1)}, f32[192,128]{1,0:T(8,128)}, ...), branch_computations={%region_6.0_spmd, %region_7.0_spmd} | conditional | flops 452984832 | bytes 14323748 | solution.py:57
  80.9 0.0 copy-start.1
  81.0 2.2 %second_products.1 = (bf16[208,128]{1,0:T(8,128)(2,1)S(1)}, bf16[128,3072]{1,0:T(8,128)(2,1)S(1)}) custom-call(bf16[192,3072]{1,0:T(8,128)(2,1)} %get-tuple-element.74.up_hbm.up_ref, bf16[128,3072]{1,0:T(8,128)(2,1)} %get-tuple-element.75.first_ref, bf16[128,3072]{1,0:T(8,128)(2,1)} %get-tuple-element.76.second_ref, ...), custom_call_target="tpu_custom_call" | custom-call | flops 150994944 | bytes 5242880 | tf_op jit(solution)/shard_map/cond/branch_1_fun/second_products/pallas_call | solution.py:74
  83.2 8.1 %all_to_all.16.parts_ref = bf16[4,208,128]{2,1,0:T(8,128)(2,1)S(1)} all-to-all(bf16[4,208,128]{2,1,0:T(8,128)(2,1)S(1)} %broadcast_in_dim.39), channel_id=1, replica_groups=mesh['pipe'=32,'dp'=4,'mp'=4] {'mp'}, dimensions={0} | all-to-all | bytes 425984 | tf_op jit(solution)/shard_map/cond/branch_1_fun/all_to_all | solution.py:41
  91.3 0.0 copy-done.1
  91.3 3.3 %input_gradient.1 = (bf16[128,3072]{1,0:T(8,128)(2,1)S(1)}, bf16[4,48,3200]{2,1,0:T(8,128)(2,1)}) custom-call(bf16[4,208,128]{2,1,0:T(8,128)(2,1)S(1)} %all_to_all.16.parts_ref, f32[192,128]{1,0:T(8,128)} %get-tuple-element.79.grad_act_ref, bf16[192,3072]{1,0:T(8,128)(2,1)} %get-tuple-element.74.up_hbm.up_ref, ...), custom_call_target="tpu_custom_call" | custom-call | flops 301989888 | bytes 5242880 | tf_op jit(solution)/shard_map/cond/branch_1_fun/input_gradient/pallas_call | solution.py:74
  94.5 16.3 %collective-permute-start.7 = (bf16[128,3072]{1,0:T(8,128)(2,1)S(1)}, bf16[128,3072]{1,0:T(8,128)(2,1)S(1)}, u32[]{:S(2)}, u32[]{:S(2)}) collective-permute-start(bf16[128,3072]{1,0:T(8,128)(2,1)S(1)} %get-tuple-element.110), channel_id=1, source_target_pairs={{16,0},{32,16},{48,32},{64,48},{80,64},{96,80},{112,96},{128,112},... | collective-permute-start | bytes 2359304 | tf_op jit(solution)/shard_map/ppermute | solution.py:25
  110.8 24.6 %conditional.7 = (bf16[48,3072]{1,0:T(8,128)(2,1)}, bf16[1,48,3072]{2,1,0:T(8,128)(2,1)}, bf16[1,128,3072]{2,1,0:T(8,128)(2,1)}) conditional(s32[]{:T(128)} %convert_element_type.20, () %tuple.52, (bf16[4,48,3200]{2,1,0:T(8,128)(2,1)}, bf16[4,128,3072]{2,1,0:T(8,128)(2,1)}, bf16[128,3072]{1,0:T(8,128)(2,1)}) %tuple.57), branch_computations={%region_8.0_spmd, %region_9.0_spmd} | conditional | flops 150994944 | bytes 14172216 | solution.py:57
  110.8 4.7 %all-to-all-start.1 = ((bf16[4,48,3200]{2,1,0:T(8,128)(2,1)}), bf16[4,48,3200]{2,1,0:T(8,128)(2,1)S(1)}, u32[]{:S(2)}, u32[]{:S(2)}) async-start(bf16[4,48,3200]{2,1,0:T(8,128)(2,1)} %get-tuple-element.82), calls=%async_computation.1 | async-start | bytes 2457600 | tf_op jit(solution)/shard_map/cond/branch_1_fun/all_to_all | solution.py:288
  115.6 2.1 %held.1 = bf16[128,3072]{1,0:T(8,128)(2,1)} custom-call(bf16[128,3072]{1,0:T(8,128)(2,1)} %get-tuple-element.86.source_ref), custom_call_target="tpu_custom_call" | custom-call | bytes 5242880 | tf_op jit(solution)/shard_map/cond/branch_1_fun/held/pallas_call | solution.py:74
  117.6 14.5 %all-to-all-done.1.terms_ref = bf16[4,48,3200]{2,1,0:T(8,128)(2,1)S(1)} async-done(((bf16[4,48,3200]{2,1,0:T(8,128)(2,1)}), bf16[4,48,3200]{2,1,0:T(8,128)(2,1)S(1)}, u32[]{:S(2)}, u32[]{:S(2)}) %all-to-all-start.1) | async-done | bytes 1228832 | tf_op jit(solution)/shard_map/cond/branch_1_fun/all_to_all | solution.py:288
  132.1 3.3 %weight_gradients.1 = (bf16[48,3072]{1,0:T(8,128)(2,1)}, bf16[48,3072]{1,0:T(8,128)(2,1)}) custom-call(bf16[4,48,3200]{2,1,0:T(8,128)(2,1)S(1)} %all-to-all-done.1.terms_ref, bf16[4,128,3072]{2,1,0:T(8,128)(2,1)} %get-tuple-element.83.cotangents_ref), custom_call_target="tpu_custom_call" | custom-call | flops 150994944 | bytes 5242880 | tf_op jit(solution)/shard_map/cond/branch_1_fun/weight_gradients/pallas_call | solution.py:74
  135.4 0.0 collective-permute-done.7
  135.4 0.9 copy.48
  (3 shorter events, 0.1 us)
Async XLA Ops:
  0.6 80.3 %collective-permute-start.6 = (bf16[128,3072]{1,0:T(8,128)(2,1)}, bf16[128,3072]{1,0:T(8,128)(2,1)}, u32[]{:S(2)}, u32[]{:S(2)}) collective-permute-start(bf16[128,3072]{1,0:T(8,128)(2,1)} %bitcast.23), channel_id=1, source_target_pairs={{320,176},{336,160},{352,144},{368,128},{384,112},{400,96},{416,80... | collective-permute-start | bytes 2359304 | tf_op jit(solution)/shard_map/ppermute | solution.py:295
  2.3 1.1 copy-start.3
  5.1 27.3 %copy-start = (bf16[128,3072]{1,0:T(8,128)(2,1)S(1)}, bf16[128,3072]{1,0:T(8,128)(2,1)}, u32[]{:S(2)}) copy-start(bf16[128,3072]{1,0:T(8,128)(2,1)} %get-tuple-element.65) | copy-start | bytes 2359300 | tf_op jit(solution)/shard_map/cond
  5.1 33.7 %all-to-all-start.3 = ((bf16[4,96,3072]{2,1,0:T(8,128)(2,1)}), bf16[4,96,3072]{2,1,0:T(8,128)(2,1)S(1)}, u32[]{:S(2)}, u32[]{:S(2)}) async-start(bf16[4,96,3072]{2,1,0:T(8,128)(2,1)} %pad_maximum_fusion), calls=%async_computation.3 | async-start | bytes 4718592 | tf_op jit(solution)/shard_map/cond/branch_1_fun/all_to_all | solution.py:264
  9.7 22.7 %collective-permute-start.3 = (bf16[128,3072]{1,0:T(8,128)(2,1)}, bf16[128,3072]{1,0:T(8,128)(2,1)}, u32[]{:S(2)}, u32[]{:S(2)}) collective-permute-start(bf16[128,3072]{1,0:T(8,128)(2,1)} %get-tuple-element.67), channel_id=1, source_target_pairs={{0,16},{16,0},{32,48},{48,32},{192,208},{208,192},{256,272},{272,2... | collective-permute-start | bytes 2359304 | tf_op jit(solution)/shard_map/cond/branch_1_fun/ppermute | solution.py:265
  14.7 66.3 %collective-permute-start.4 = (bf16[128,3072]{1,0:T(8,128)(2,1)}, bf16[128,3072]{1,0:T(8,128)(2,1)}, u32[]{:S(2)}, u32[]{:S(2)}) collective-permute-start(bf16[128,3072]{1,0:T(8,128)(2,1)} %get-tuple-element.67), channel_id=1, source_target_pairs={{64,432},{80,416},{160,336},{176,320},{65,433},{81,417},{161,337},... | collective-permute-start | bytes 2359304 | tf_op jit(solution)/shard_map/cond/branch_1_fun/ppermute | solution.py:268
  34.5 46.5 %collective-permute-start.5 = (bf16[128,3072]{1,0:T(8,128)(2,1)}, bf16[128,3072]{1,0:T(8,128)(2,1)}, u32[]{:S(2)}, u32[]{:S(2)}) collective-permute-start(bf16[128,3072]{1,0:T(8,128)(2,1)} %collective-permute-done.3), channel_id=1, source_target_pairs={{16,496},{0,480},{48,464},{32,448},{208,304},{192,288},{272,240},{... | collective-permute-start | bytes 2359304 | tf_op jit(solution)/shard_map/cond/branch_1_fun/ppermute | solution.py:269
  38.9 42.0 %all-to-all-start.2 = ((bf16[4,128,3072]{2,1,0:T(8,128)(2,1)}), bf16[4,128,3072]{2,1,0:T(8,128)(2,1)}, u32[]{:S(2)}, u32[]{:S(2)}) async-start(bf16[4,128,3072]{2,1,0:T(8,128)(2,1)} %get-tuple-element.61), calls=%async_computation.2 | async-start | bytes 6291456 | tf_op jit(solution)/shard_map/cond/branch_1_fun/cond/branch_1_fun/all_to_all | solution.py:256
  45.5 10.4 %copy-start.2 = (bf16[1,128,3072]{2,1,0:T(8,128)(2,1)S(1)}, bf16[1,128,3072]{2,1,0:T(8,128)(2,1)}, u32[]{:S(2)}) copy-start(bf16[1,128,3072]{2,1,0:T(8,128)(2,1)} %get-tuple-element.50) | copy-start | bytes 2359300 | tf_op jit(solution)/shard_map/cond/branch_1_fun/cond/branch_1_fun/cond
  45.5 3.5 %collective-permute-start = (f32[400,128]{1,0:T(8,128)S(1)}, f32[400,128]{1,0:T(8,128)S(1)}, u32[]{:S(2)}, u32[]{:S(2)}) collective-permute-start(f32[400,128]{1,0:T(8,128)S(1)} %first_products.1), channel_id=1, source_target_pairs={{0,1},{1,0},{2,3},{3,2},{4,5},{5,4},{6,7},{7,6},{8,9},{9,8},{10,11... | collective-permute-start | bytes 614408 | tf_op jit(solution)/shard_map/cond/branch_1_fun/cond/branch_1_fun/cond/branch_1_fun/ppermute | solution.py:48
  49.0 6.8 %collective-permute-start.1 = (bf16[400,128]{1,0:T(8,128)(2,1)S(1)}, bf16[400,128]{1,0:T(8,128)(2,1)S(1)}, u32[]{:S(2)}, u32[]{:S(2)}) collective-permute-start(bf16[400,128]{1,0:T(8,128)(2,1)S(1)} %add_convert_fusion), channel_id=1, source_target_pairs={{0,2},{1,3},{2,0},{3,1},{4,6},{5,7},{6,4},{7,5},{8,10},{9,11},{10,... | collective-permute-start | bytes 307208 | tf_op jit(solution)/shard_map/cond/branch_1_fun/cond/branch_1_fun/cond/branch_1_fun/ppermute | solution.py:48
  57.3 23.6 %collective-permute-start.2 = (bf16[128,3072]{1,0:T(8,128)(2,1)S(1)}, bf16[128,3072]{1,0:T(8,128)(2,1)}, u32[]{:S(2)}, u32[]{:S(2)}) collective-permute-start(bf16[128,3072]{1,0:T(8,128)(2,1)S(1)} %get-tuple-element.52), channel_id=1, source_target_pairs={{0,16},{16,32},{32,48},{48,64},{64,80},{80,96},{96,112},{112,128},... | collective-permute-start | bytes 2359304 | tf_op jit(solution)/shard_map/cond/branch_1_fun/cond/branch_1_fun/cond/branch_1_fun/ppermute | solution.py:25
  80.9 10.3 %copy-start.1 = (bf16[128,3072]{1,0:T(8,128)(2,1)S(1)}, bf16[128,3072]{1,0:T(8,128)(2,1)}, u32[]{:S(2)}) copy-start(bf16[128,3072]{1,0:T(8,128)(2,1)} %get-tuple-element.81.cotangent_ref) | copy-start | bytes 2359300 | tf_op jit(solution)/shard_map/cond
  94.5 40.9 %collective-permute-start.7 = (bf16[128,3072]{1,0:T(8,128)(2,1)S(1)}, bf16[128,3072]{1,0:T(8,128)(2,1)S(1)}, u32[]{:S(2)}, u32[]{:S(2)}) collective-permute-start(bf16[128,3072]{1,0:T(8,128)(2,1)S(1)} %get-tuple-element.110), channel_id=1, source_target_pairs={{16,0},{32,16},{48,32},{64,48},{80,64},{96,80},{112,96},{128,112},... | collective-permute-start | bytes 2359304 | tf_op jit(solution)/shard_map/ppermute | solution.py:25
  110.8 21.3 %all-to-all-start.1 = ((bf16[4,48,3200]{2,1,0:T(8,128)(2,1)}), bf16[4,48,3200]{2,1,0:T(8,128)(2,1)S(1)}, u32[]{:S(2)}, u32[]{:S(2)}) async-start(bf16[4,48,3200]{2,1,0:T(8,128)(2,1)} %get-tuple-element.82), calls=%async_computation.1 | async-start | bytes 2457600 | tf_op jit(solution)/shard_map/cond/branch_1_fun/all_to_all | solution.py:288

commit v6 on v5

--- a/solution.py
+++ b/solution.py
@@ -112,25 +112,23 @@
     return jnp.broadcast_to(jnp.sum(squares.T, axis=0, keepdims=True), (EXTRA, squares.shape[0]))
 
 
-def first_kernel(weights_ref, input_ref, cotangent_ref, out_ref):
-    rank = (out_ref.shape[0] - EXTRA) // 2
-    product = squares = grad_act = 0.0
+def first_kernel(weights_ref, input_ref, out_ref):
+    rank = out_ref.shape[0] - EXTRA
+    product = squares = 0.0
     for tile in tiles(input_ref.shape[1]):
         inputs = input_ref[:, tile]
         product += dot(up_rows(weights_ref, tile), inputs, 1, 1)
-        grad_act += dot(down_rows(weights_ref, tile), cotangent_ref[:, tile], 1, 1)
         squares += squares_of(inputs)
     out_ref[:rank, :] = product.astype(out_ref.dtype)
-    out_ref[rank : 2 * rank, :] = grad_act.astype(out_ref.dtype)
-    out_ref[2 * rank :, :] = row_sums(squares).astype(out_ref.dtype)
-
-
-def first_products(weights, inputs, cotangent):
+    out_ref[rank:, :] = row_sums(squares).astype(out_ref.dtype)
+
+
+def first_products(weights, inputs):
     group, own_rank, features = weights.shape
     rank, rows = group * own_rank // 2, inputs.shape[0]
     return call(
-        first_kernel, "first_products", (weights, inputs, cotangent),
-        struct(2 * rank + EXTRA, rows, dtype=jnp.float32), [], 4 * rank * rows * features,
+        first_kernel, "first_products", (weights, inputs),
+        struct(rank + EXTRA, rows, dtype=jnp.float32), [], 2 * rank * rows * features,
     )
 
 
@@ -177,24 +175,27 @@
     )
 
 
-def output_kernel(parts_ref, weights_ref, input_ref, out_ref, grad_act_ref, up_ref):
-    rank = grad_act_ref.shape[0]
-    scale = lax.rsqrt(parts_ref[2 * rank : 2 * rank + 1, :] / D + epsilon)
+def output_kernel(parts_ref, weights_ref, input_ref, cotangent_ref, out_ref, product_ref, up_ref):
+    rank = product_ref.shape[0]
+    scale = lax.rsqrt(parts_ref[rank : rank + 1, :] / D + epsilon)
     act = gated(parts_ref[:rank, :] * scale)[0].astype(jnp.bfloat16)
-    grad_act_ref[...] = parts_ref[rank : 2 * rank, :]
+    product = 0.0
     for tile in tiles(input_ref.shape[1]):
-        out = input_ref[:, tile].astype(jnp.float32) + dot(act, down_rows(weights_ref, tile), 0, 0)
+        down = down_rows(weights_ref, tile)
+        out = input_ref[:, tile].astype(jnp.float32) + dot(act, down, 0, 0)
         out_ref[:, tile] = out.astype(out_ref.dtype)
+        product += dot(down, cotangent_ref[:, tile], 1, 1)
         up_ref[:, tile] = up_rows(weights_ref, tile)
-
-
-def forward_output(parts, weights, inputs):
+    product_ref[...] = product
+
+
+def forward_output(parts, weights, inputs, cotangent):
     group, own_rank, features = weights.shape
     rank, rows = group * own_rank // 2, inputs.shape[0]
     return call(
-        output_kernel, "forward_output", (parts, weights, inputs),
+        output_kernel, "forward_output", (parts, weights, inputs, cotangent),
         [struct(*inputs.shape), struct(rank, rows, dtype=jnp.float32), struct(rank, features)],
-        [], 2 * rank * rows * features,
+        [], 4 * rank * rows * features,
     )
 
 
@@ -247,9 +248,9 @@
 
 
 def forward(weights, forward_in, cotangent):
-    parts = summed(first_products(weights, forward_in, cotangent), "mp")
-    output, grad_act, up_full = forward_output(parts, weights, forward_in)
-    return shifted(output, "pipe", 1), grad_act, up_full
+    parts = summed(first_products(weights, forward_in), "mp")
+    output, product, up_full = forward_output(parts, weights, forward_in, cotangent)
+    return shifted(output, "pipe", 1), summed(product, "mp"), up_full
 
 
 def beside(weights, copies, forward_in, cotangent):

time: 137 us -> 139 us (1.015)
  starting transfers between devices: 50.8 us -> 56.5 us
  waiting for transfers between devices: 56.7 us -> 51.7 us
    ppermute x2, waiting for transfers between devices: 18.7 us -> 0.71 us  [shifted(): return lax.ppermute(block, axis, route)]
    ppermute x2 -> x4, waiting for transfers between devices: 4.83 us -> 17.9 us  [summed(): far = lax.ppermute(block, axis, [(i, i ^ distance) for i in range(size)])]
    ppermute x2 -> x4, starting transfers between devices: 5.45 us -> 9.74 us  [summed(): far = lax.ppermute(block, axis, [(i, i ^ distance) for i in range(size)])]
    ppermute x2, starting transfers between devices: 21.2 us -> 22.9 us  [shifted(): return lax.ppermute(block, axis, route)]
  transfers between devices with their start and end apart: 11 -> 13, of which waited for: 6 -> 8; matrix products, arithmetic and copies ran while one was open for 4% -> 4% of each run, Pallas kernels for 6% -> 6%
where the time goes in v6:
time: 139 us; the launch traced here: 138 us
  starting transfers between devices  56.5 us (41%)
  waiting for transfers between devices  51.7 us (37%)
  Pallas kernels  14.2 us (10%)
  blocking collectives  8.07 us (6%)
  local copies, waits for them, and re-layouts  4.23 us (3%)
  other arithmetic  2.28 us (2%)
    ppermute x2, starting transfers between devices, shifted(): return lax.ppermute(block, axis, route)  22.9 us
    ppermute x4, waiting for transfers between devices, summed(): far = lax.ppermute(block, axis, [(i, i ^ distance) for i in range(size)])  17.9 us
    ppermute x1, waiting for transfers between devices, ahead(): crossed = lax.ppermute(stash, 'pipe', [(i, i ^ 1) for i, _ in crossing])  16.2 us
    all_to_all x1, waiting for transfers between devices, last_terms(): terms = lax.all_to_all(terms, 'dp', split_axis=0, concat_axis=0, tiled=True)  14.5 us
    pallas_call x6, Pallas kernels, call(): pl.pallas_call(kernel, in_specs=[anywhere if i in fetched else in_vmem fo...  14.2 us
    ppermute x4, starting transfers between devices, summed(): far = lax.ppermute(block, axis, [(i, i ^ distance) for i in range(size)])  9.74 us
    all_to_all x1, blocking collectives, spread(): return lax.all_to_all(copies, axis, split_axis=0, concat_axis=0, tiled=True)  8.07 us
    ppermute x1, starting transfers between devices, ahead(): crossed = lax.ppermute(stash, 'pipe', [(i, i ^ 1) for i, _ in crossing])  4.92 us
  transfers between devices with their start and end apart: 13, of which 8 were waited for; matrix products, arithmetic and copies ran while one was open for 4% of the time, Pallas kernels for 6%

profile of v6, /device:TPU:288, one launch (start us, length us, event | category | flops | bytes accessed | tf_op | source)
XLA Modules:
  0.0 137.9 jit_solution(18429985081930959231)
XLA Ops:
  0.6 1.6 %collective-permute-start.8 = (bf16[128,3072]{1,0:T(8,128)(2,1)}, bf16[128,3072]{1,0:T(8,128)(2,1)}, u32[]{:S(2)}, u32[]{:S(2)}) collective-permute-start(bf16[128,3072]{1,0:T(8,128)(2,1)} %bitcast.23), channel_id=1, source_target_pairs={{320,176},{336,160},{352,144},{368,128},{384,112},{400,96},{416,80... | collective-permute-start | bytes 2359304 | tf_op jit(solution)/shard_map/ppermute | solution.py:296
  2.3 78.7 %conditional.5 = (bf16[128,3072]{1,0:T(8,128)(2,1)}, f32[192,128]{1,0:T(8,128)}, bf16[192,3072]{1,0:T(8,128)(2,1)}, bf16[4,128,3072]{2,1,0:T(8,128)(2,1)}, bf16[...) conditional(s32[]{:T(128)} %convert_element_type.29, () %tuple.54, (bf16[1,128,3072]{2,1,0:T(8,128)(2,1)}, ...), branch_computations={%region_0.0_spmd, %region_1.0_spmd} | conditional | flops 457959424 | bytes 60805816 | solution.py:57
  2.3 1.1 broadcast_in_dim.30
  3.4 0.0 copy-done.3
  3.4 0.1 broadcast_in_dim.36
  3.5 1.6 %pad_maximum_fusion = bf16[4,96,3072]{2,1,0:T(8,128)(2,1)} fusion(bf16[4,48,3072]{2,1,0:T(8,128)(2,1)S(1)} %broadcast_in_dim.36, bf16[4,48,3072]{2,1,0:T(8,128)(2,1)S(1)} %broadcast_in_dim.30), kind=kLoop, calls=%fused_computation.4 | loop fusion | flops 4718592 | bytes 4718592 | tf_op jit(solution)/shard_map/cond/branch_1_fun/concatenate | solution.py:265
  5.1 4.6 %all-to-all-start.3 = ((bf16[4,96,3072]{2,1,0:T(8,128)(2,1)}), bf16[4,96,3072]{2,1,0:T(8,128)(2,1)S(1)}, u32[]{:S(2)}, u32[]{:S(2)}) async-start(bf16[4,96,3072]{2,1,0:T(8,128)(2,1)} %pad_maximum_fusion), calls=%async_computation.3 | async-start | bytes 4718592 | tf_op jit(solution)/shard_map/cond/branch_1_fun/all_to_all | solution.py:265
  9.7 4.9 %collective-permute-start.5 = (bf16[128,3072]{1,0:T(8,128)(2,1)}, bf16[128,3072]{1,0:T(8,128)(2,1)}, u32[]{:S(2)}, u32[]{:S(2)}) collective-permute-start(bf16[128,3072]{1,0:T(8,128)(2,1)} %get-tuple-element.67), channel_id=1, source_target_pairs={{0,16},{16,0},{32,48},{48,32},{192,208},{208,192},{256,272},{272,2... | collective-permute-start | bytes 2359304 | tf_op jit(solution)/shard_map/cond/branch_1_fun/ppermute | solution.py:266
  14.7 1.6 %collective-permute-start.6 = (bf16[128,3072]{1,0:T(8,128)(2,1)}, bf16[128,3072]{1,0:T(8,128)(2,1)}, u32[]{:S(2)}, u32[]{:S(2)}) collective-permute-start(bf16[128,3072]{1,0:T(8,128)(2,1)} %get-tuple-element.67), channel_id=1, source_target_pairs={{64,432},{80,416},{160,336},{176,320},{65,433},{81,417},{161,337},... | collective-permute-start | bytes 2359304 | tf_op jit(solution)/shard_map/cond/branch_1_fun/ppermute | solution.py:269
  16.2 16.2 %collective-permute-done.5 = bf16[128,3072]{1,0:T(8,128)(2,1)} collective-permute-done((bf16[128,3072]{1,0:T(8,128)(2,1)}, bf16[128,3072]{1,0:T(8,128)(2,1)}, u32[]{:S(2)}, u32[]{:S(2)}) %collective-permute-start.5) | collective-permute-done | bytes 786464 | tf_op jit(solution)/shard_map/cond/branch_1_fun/ppermute | solution.py:266
  32.4 0.0 copy-done
  32.4 2.1 %broadcast_in_dim.38 = bf16[4,128,3072]{2,1,0:T(8,128)(2,1)} broadcast(bf16[128,3072]{1,0:T(8,128)(2,1)S(1)} %copy-done), dimensions={1,2} | broadcast | bytes 3932160 | tf_op jit(solution)/shard_map/cond/branch_1_fun/broadcast_in_dim | solution.py:267
  34.5 2.0 %collective-permute-start.7 = (bf16[128,3072]{1,0:T(8,128)(2,1)}, bf16[128,3072]{1,0:T(8,128)(2,1)}, u32[]{:S(2)}, u32[]{:S(2)}) collective-permute-start(bf16[128,3072]{1,0:T(8,128)(2,1)} %collective-permute-done.5), channel_id=1, source_target_pairs={{16,496},{0,480},{48,464},{32,448},{208,304},{192,288},{272,240},{... | collective-permute-start | bytes 2359304 | tf_op jit(solution)/shard_map/cond/branch_1_fun/ppermute | solution.py:270
  36.5 2.4 %all-to-all-done.3 = bf16[4,96,3072]{2,1,0:T(8,128)(2,1)S(1)} async-done(((bf16[4,96,3072]{2,1,0:T(8,128)(2,1)}), bf16[4,96,3072]{2,1,0:T(8,128)(2,1)S(1)}, u32[]{:S(2)}, u32[]{:S(2)}) %all-to-all-start.3) | async-done | bytes 2359328 | tf_op jit(solution)/shard_map/cond/branch_1_fun/all_to_all | solution.py:265
  38.9 42.1 %conditional.1 = (bf16[128,3072]{1,0:T(8,128)(2,1)}, f32[192,128]{1,0:T(8,128)}, bf16[192,3072]{1,0:T(8,128)(2,1)}, bf16[4,128,3072]{2,1,0:T(8,128)(2,1)}) conditional(s32[]{:T(128)} %convert_element_type.27, () %tuple.37, (bf16[1,128,3072]{2,1,0:T(8,128)(2,1)}, bf16[4,96,3072]{2,1,0:T(8,128)(2,1)S(1)}, bf16[128,3072]{1,0:T(8,128)(2,1)S(1)}, ...), branch_computations={%region_2.0_spmd, %region_3.0_spmd} | conditional | flops 453240832 | bytes 28365174 | solution.py:57
  38.9 4.6 %all-to-all-start.2 = ((bf16[4,128,3072]{2,1,0:T(8,128)(2,1)}), bf16[4,128,3072]{2,1,0:T(8,128)(2,1)}, u32[]{:S(2)}, u32[]{:S(2)}) async-start(bf16[4,128,3072]{2,1,0:T(8,128)(2,1)} %get-tuple-element.61), calls=%async_computation.2 | async-start | bytes 6291456 | tf_op jit(solution)/shard_map/cond/branch_1_fun/cond/branch_1_fun/all_to_all | solution.py:257
  43.5 37.5 %conditional = (bf16[128,3072]{1,0:T(8,128)(2,1)}, f32[192,128]{1,0:T(8,128)}, bf16[192,3072]{1,0:T(8,128)(2,1)}) conditional(s32[]{:T(128)} %convert_element_type.26, () %tuple.34, (bf16[1,128,3072]{2,1,0:T(8,128)(2,1)}, bf16[4,96,3072]{2,1,0:T(8,128)(2,1)S(1)}, bf16[128,3072]{1,0:T(8,128)(2,1)S(1)}) %tuple.35), branch_computations={%region_4.0_spmd, %region_5.0_spmd} | conditional | flops 453240832 | bytes 18927868 | solution.py:57
  43.5 0.0 copy-start.2
  43.5 1.7 %first_products.1 = f32[208,128]{1,0:T(8,128)S(1)} custom-call(bf16[4,96,3072]{2,1,0:T(8,128)(2,1)S(1)} %get-tuple-element.49.weights_ref, bf16[128,3072]{1,0:T(8,128)(2,1)} %bitcast.16), custom_call_target="tpu_custom_call" | custom-call | flops 150994944 | bytes 5242880 | tf_op jit(solution)/shard_map/cond/branch_1_fun/cond/branch_1_fun/cond/branch_1_fun/first_products/pallas_call | solution.py:74
  45.2 1.9 %collective-permute-start = (f32[208,128]{1,0:T(8,128)S(1)}, f32[208,128]{1,0:T(8,128)S(1)}, u32[]{:S(2)}, u32[]{:S(2)}) collective-permute-start(f32[208,128]{1,0:T(8,128)S(1)} %first_products.1), channel_id=1, source_target_pairs={{0,1},{1,0},{2,3},{3,2},{4,5},{5,4},{6,7},{7,6},{8,9},{9,8},{10,11... | collective-permute-start | bytes 319496 | tf_op jit(solution)/shard_map/cond/branch_1_fun/cond/branch_1_fun/cond/branch_1_fun/ppermute | solution.py:48
  47.2 1.3 collective-permute-done
  48.5 3.4 %collective-permute-start.1 = (bf16[208,128]{1,0:T(8,128)(2,1)S(1)}, bf16[208,128]{1,0:T(8,128)(2,1)S(1)}, u32[]{:S(2)}, u32[]{:S(2)}) collective-permute-start(bf16[208,128]{1,0:T(8,128)(2,1)S(1)} %add_convert_fusion), channel_id=1, source_target_pairs={{0,2},{1,3},{2,0},{3,1},{4,6},{5,7},{6,4},{7,5},{8,10},{9,11},{10,... | collective-permute-start | bytes 159752 | tf_op jit(solution)/shard_map/cond/branch_1_fun/cond/branch_1_fun/cond/branch_1_fun/ppermute | solution.py:48
  51.9 2.6 %collective-permute-done.1 = bf16[208,128]{1,0:T(8,128)(2,1)S(1)} collective-permute-done((bf16[208,128]{1,0:T(8,128)(2,1)S(1)}, bf16[208,128]{1,0:T(8,128)(2,1)S(1)}, u32[]{:S(2)}, u32[]{:S(2)}) %collective-permute-start.1) | collective-permute-done | bytes 53280 | tf_op jit(solution)/shard_map/cond/branch_1_fun/cond/branch_1_fun/cond/branch_1_fun/ppermute | solution.py:48
  54.5 1.7 %forward_output.1 = (bf16[128,3072]{1,0:T(8,128)(2,1)S(1)}, f32[192,128]{1,0:T(8,128)S(1)}, bf16[192,3072]{1,0:T(8,128)(2,1)}) custom-call(f32[208,128]{1,0:T(8,128)S(1)} %convert_add_fusion.parts_ref, bf16[4,96,3072]{2,1,0:T(8,128)(2,1)S(1)} %get-tuple-element.49.weights_ref, bf16[128,3072]{1,0:T(8,128)(2,1)S(1)} %bitcast.17, ...), custom_call_target="tpu_custom_call" | custom-call | flops 301989888 | bytes 5242880 | tf_op jit(solution)/shard_map/cond/branch_1_fun/cond/branch_1_fun/cond/branch_1_fun/forward_output/pallas_call | solution.py:74
  56.3 4.9 %collective-permute-start.2 = (bf16[128,3072]{1,0:T(8,128)(2,1)S(1)}, bf16[128,3072]{1,0:T(8,128)(2,1)}, u32[]{:S(2)}, u32[]{:S(2)}) collective-permute-start(bf16[128,3072]{1,0:T(8,128)(2,1)S(1)} %get-tuple-element.52), channel_id=1, source_target_pairs={{0,16},{16,32},{32,48},{48,64},{64,80},{80,96},{96,112},{112,128},... | collective-permute-start | bytes 2359304 | tf_op jit(solution)/shard_map/cond/branch_1_fun/cond/branch_1_fun/cond/branch_1_fun/ppermute | solution.py:25
  61.2 1.9 %collective-permute-start.3 = (f32[192,128]{1,0:T(8,128)S(1)}, f32[192,128]{1,0:T(8,128)S(1)}, u32[]{:S(2)}, u32[]{:S(2)}) collective-permute-start(f32[192,128]{1,0:T(8,128)S(1)} %get-tuple-element.53), channel_id=1, source_target_pairs={{0,1},{1,0},{2,3},{3,2},{4,5},{5,4},{6,7},{7,6},{8,9},{9,8},{10,11... | collective-permute-start | bytes 294920 | tf_op jit(solution)/shard_map/cond/branch_1_fun/cond/branch_1_fun/cond/branch_1_fun/ppermute | solution.py:48
  63.1 1.3 collective-permute-done.3
  64.4 2.5 %collective-permute-start.4 = (bf16[192,128]{1,0:T(8,128)(2,1)S(1)}, bf16[192,128]{1,0:T(8,128)(2,1)S(1)}, u32[]{:S(2)}, u32[]{:S(2)}) collective-permute-start(bf16[192,128]{1,0:T(8,128)(2,1)S(1)} %add_convert_fusion.1), channel_id=1, source_target_pairs={{0,2},{1,3},{2,0},{3,1},{4,6},{5,7},{6,4},{7,5},{8,10},{9,11},{10,... | collective-permute-start | bytes 147464 | tf_op jit(solution)/shard_map/cond/branch_1_fun/cond/branch_1_fun/cond/branch_1_fun/ppermute | solution.py:48
  66.9 12.7 %collective-permute-done.4 = bf16[192,128]{1,0:T(8,128)(2,1)S(1)} collective-permute-done((bf16[192,128]{1,0:T(8,128)(2,1)S(1)}, bf16[192,128]{1,0:T(8,128)(2,1)S(1)}, u32[]{:S(2)}, u32[]{:S(2)}) %collective-permute-start.4) | collective-permute-done | bytes 49184 | tf_op jit(solution)/shard_map/cond/branch_1_fun/cond/branch_1_fun/cond/branch_1_fun/ppermute | solution.py:48
  79.7 0.7 convert_add_fusion.1
  80.3 0.7 collective-permute-done.2
  81.0 0.0 all-to-all-done.2
  81.0 0.0 collective-permute-done.6
  81.0 0.0 collective-permute-done.7
  81.0 0.0 collective-permute-done.8
  81.0 13.6 %conditional.6 = ((bf16[128,3072]{1,0:T(8,128)(2,1)S(1)}, bf16[4,48,3200]{2,1,0:T(8,128)(2,1)})) conditional(s32[]{:T(128)} %convert_element_type.29, () %tuple.53, (bf16[192,3072]{1,0:T(8,128)(2,1)}, bf16[128,3072]{1,0:T(8,128)(2,1)}, bf16[128,3072]{1,0:T(8,128)(2,1)}, bf16[128,3072]{1,0:T(8,128)(2,1)}, f32[192,128]{1,0:T(8,128)}, ...), branch_computations={%region_6.0_spmd, %region_7.0_spmd} | conditional | flops 452984832 | bytes 14323748 | solution.py:57
  81.0 0.0 copy-start.1
  81.1 2.2 %second_products.1 = (bf16[208,128]{1,0:T(8,128)(2,1)S(1)}, bf16[128,3072]{1,0:T(8,128)(2,1)S(1)}) custom-call(bf16[192,3072]{1,0:T(8,128)(2,1)} %get-tuple-element.74.up_hbm.up_ref, bf16[128,3072]{1,0:T(8,128)(2,1)} %get-tuple-element.75.first_ref, bf16[128,3072]{1,0:T(8,128)(2,1)} %get-tuple-element.76.second_ref, ...), custom_call_target="tpu_custom_call" | custom-call | flops 150994944 | bytes 5242880 | tf_op jit(solution)/shard_map/cond/branch_1_fun/second_products/pallas_call | solution.py:74
  83.3 8.1 %all_to_all.16.parts_ref = bf16[4,208,128]{2,1,0:T(8,128)(2,1)S(1)} all-to-all(bf16[4,208,128]{2,1,0:T(8,128)(2,1)S(1)} %broadcast_in_dim.39), channel_id=1, replica_groups=mesh['pipe'=32,'dp'=4,'mp'=4] {'mp'}, dimensions={0} | all-to-all | bytes 425984 | tf_op jit(solution)/shard_map/cond/branch_1_fun/all_to_all | solution.py:41
  91.4 3.2 %input_gradient.1 = (bf16[128,3072]{1,0:T(8,128)(2,1)S(1)}, bf16[4,48,3200]{2,1,0:T(8,128)(2,1)}) custom-call(bf16[4,208,128]{2,1,0:T(8,128)(2,1)S(1)} %all_to_all.16.parts_ref, f32[192,128]{1,0:T(8,128)} %get-tuple-element.79.grad_act_ref, bf16[192,3072]{1,0:T(8,128)(2,1)} %get-tuple-element.74.up_hbm.up_ref, ...), custom_call_target="tpu_custom_call" | custom-call | flops 301989888 | bytes 5242880 | tf_op jit(solution)/shard_map/cond/branch_1_fun/input_gradient/pallas_call | solution.py:74
  94.6 18.0 %collective-permute-start.9 = (bf16[128,3072]{1,0:T(8,128)(2,1)S(1)}, bf16[128,3072]{1,0:T(8,128)(2,1)S(1)}, u32[]{:S(2)}, u32[]{:S(2)}) collective-permute-start(bf16[128,3072]{1,0:T(8,128)(2,1)S(1)} %get-tuple-element.110), channel_id=1, source_target_pairs={{16,0},{32,16},{48,32},{64,48},{80,64},{96,80},{112,96},{128,112},... | collective-permute-start | bytes 2359304 | tf_op jit(solution)/shard_map/ppermute | solution.py:25
  112.6 24.3 %conditional.7 = (bf16[48,3072]{1,0:T(8,128)(2,1)}, bf16[1,48,3072]{2,1,0:T(8,128)(2,1)}, bf16[1,128,3072]{2,1,0:T(8,128)(2,1)}) conditional(s32[]{:T(128)} %convert_element_type.29, () %tuple.52, (bf16[4,48,3200]{2,1,0:T(8,128)(2,1)}, bf16[4,128,3072]{2,1,0:T(8,128)(2,1)}, bf16[128,3072]{1,0:T(8,128)(2,1)}) %tuple.57), branch_computations={%region_8.0_spmd, %region_9.0_spmd} | conditional | flops 150994944 | bytes 14172216 | solution.py:57
  112.6 4.5 %all-to-all-start.1 = ((bf16[4,48,3200]{2,1,0:T(8,128)(2,1)}), bf16[4,48,3200]{2,1,0:T(8,128)(2,1)S(1)}, u32[]{:S(2)}, u32[]{:S(2)}) async-start(bf16[4,48,3200]{2,1,0:T(8,128)(2,1)} %get-tuple-element.82), calls=%async_computation.1 | async-start | bytes 2457600 | tf_op jit(solution)/shard_map/cond/branch_1_fun/all_to_all | solution.py:289
  117.1 2.1 %held.1 = bf16[128,3072]{1,0:T(8,128)(2,1)} custom-call(bf16[128,3072]{1,0:T(8,128)(2,1)} %get-tuple-element.86.source_ref), custom_call_target="tpu_custom_call" | custom-call | bytes 5242880 | tf_op jit(solution)/shard_map/cond/branch_1_fun/held/pallas_call | solution.py:74
  119.2 14.5 %all-to-all-done.1.terms_ref = bf16[4,48,3200]{2,1,0:T(8,128)(2,1)S(1)} async-done(((bf16[4,48,3200]{2,1,0:T(8,128)(2,1)}), bf16[4,48,3200]{2,1,0:T(8,128)(2,1)S(1)}, u32[]{:S(2)}, u32[]{:S(2)}) %all-to-all-start.1) | async-done | bytes 1228832 | tf_op jit(solution)/shard_map/cond/branch_1_fun/all_to_all | solution.py:289
  133.7 3.3 %weight_gradients.1 = (bf16[48,3072]{1,0:T(8,128)(2,1)}, bf16[48,3072]{1,0:T(8,128)(2,1)}) custom-call(bf16[4,48,3200]{2,1,0:T(8,128)(2,1)S(1)} %all-to-all-done.1.terms_ref, bf16[4,128,3072]{2,1,0:T(8,128)(2,1)} %get-tuple-element.83.cotangents_ref), custom_call_target="tpu_custom_call" | custom-call | flops 150994944 | bytes 5242880 | tf_op jit(solution)/shard_map/cond/branch_1_fun/weight_gradients/pallas_call | solution.py:74
  137.0 0.0 collective-permute-done.9
  137.0 0.9 copy.48
  (8 shorter events, 0.1 us)
Async XLA Ops:
  0.6 80.4 %collective-permute-start.8 = (bf16[128,3072]{1,0:T(8,128)(2,1)}, bf16[128,3072]{1,0:T(8,128)(2,1)}, u32[]{:S(2)}, u32[]{:S(2)}) collective-permute-start(bf16[128,3072]{1,0:T(8,128)(2,1)} %bitcast.23), channel_id=1, source_target_pairs={{320,176},{336,160},{352,144},{368,128},{384,112},{400,96},{416,80... | collective-permute-start | bytes 2359304 | tf_op jit(solution)/shard_map/ppermute | solution.py:296
  2.3 1.1 copy-start.3
  5.1 27.3 %copy-start = (bf16[128,3072]{1,0:T(8,128)(2,1)S(1)}, bf16[128,3072]{1,0:T(8,128)(2,1)}, u32[]{:S(2)}) copy-start(bf16[128,3072]{1,0:T(8,128)(2,1)} %get-tuple-element.65) | copy-start | bytes 2359300 | tf_op jit(solution)/shard_map/cond
  5.1 33.7 %all-to-all-start.3 = ((bf16[4,96,3072]{2,1,0:T(8,128)(2,1)}), bf16[4,96,3072]{2,1,0:T(8,128)(2,1)S(1)}, u32[]{:S(2)}, u32[]{:S(2)}) async-start(bf16[4,96,3072]{2,1,0:T(8,128)(2,1)} %pad_maximum_fusion), calls=%async_computation.3 | async-start | bytes 4718592 | tf_op jit(solution)/shard_map/cond/branch_1_fun/all_to_all | solution.py:265
  9.7 22.7 %collective-permute-start.5 = (bf16[128,3072]{1,0:T(8,128)(2,1)}, bf16[128,3072]{1,0:T(8,128)(2,1)}, u32[]{:S(2)}, u32[]{:S(2)}) collective-permute-start(bf16[128,3072]{1,0:T(8,128)(2,1)} %get-tuple-element.67), channel_id=1, source_target_pairs={{0,16},{16,0},{32,48},{48,32},{192,208},{208,192},{256,272},{272,2... | collective-permute-start | bytes 2359304 | tf_op jit(solution)/shard_map/cond/branch_1_fun/ppermute | solution.py:266
  14.7 66.4 %collective-permute-start.6 = (bf16[128,3072]{1,0:T(8,128)(2,1)}, bf16[128,3072]{1,0:T(8,128)(2,1)}, u32[]{:S(2)}, u32[]{:S(2)}) collective-permute-start(bf16[128,3072]{1,0:T(8,128)(2,1)} %get-tuple-element.67), channel_id=1, source_target_pairs={{64,432},{80,416},{160,336},{176,320},{65,433},{81,417},{161,337},... | collective-permute-start | bytes 2359304 | tf_op jit(solution)/shard_map/cond/branch_1_fun/ppermute | solution.py:269
  34.5 46.5 %collective-permute-start.7 = (bf16[128,3072]{1,0:T(8,128)(2,1)}, bf16[128,3072]{1,0:T(8,128)(2,1)}, u32[]{:S(2)}, u32[]{:S(2)}) collective-permute-start(bf16[128,3072]{1,0:T(8,128)(2,1)} %collective-permute-done.5), channel_id=1, source_target_pairs={{16,496},{0,480},{48,464},{32,448},{208,304},{192,288},{272,240},{... | collective-permute-start | bytes 2359304 | tf_op jit(solution)/shard_map/cond/branch_1_fun/ppermute | solution.py:270
  38.9 42.1 %all-to-all-start.2 = ((bf16[4,128,3072]{2,1,0:T(8,128)(2,1)}), bf16[4,128,3072]{2,1,0:T(8,128)(2,1)}, u32[]{:S(2)}, u32[]{:S(2)}) async-start(bf16[4,128,3072]{2,1,0:T(8,128)(2,1)} %get-tuple-element.61), calls=%async_computation.2 | async-start | bytes 6291456 | tf_op jit(solution)/shard_map/cond/branch_1_fun/cond/branch_1_fun/all_to_all | solution.py:257
  43.5 11.0 %copy-start.2 = (bf16[1,128,3072]{2,1,0:T(8,128)(2,1)S(1)}, bf16[1,128,3072]{2,1,0:T(8,128)(2,1)}, u32[]{:S(2)}) copy-start(bf16[1,128,3072]{2,1,0:T(8,128)(2,1)} %get-tuple-element.50) | copy-start | bytes 2359300 | tf_op jit(solution)/shard_map/cond/branch_1_fun/cond/branch_1_fun/cond
  45.2 3.2 %collective-permute-start = (f32[208,128]{1,0:T(8,128)S(1)}, f32[208,128]{1,0:T(8,128)S(1)}, u32[]{:S(2)}, u32[]{:S(2)}) collective-permute-start(f32[208,128]{1,0:T(8,128)S(1)} %first_products.1), channel_id=1, source_target_pairs={{0,1},{1,0},{2,3},{3,2},{4,5},{5,4},{6,7},{7,6},{8,9},{9,8},{10,11... | collective-permute-start | bytes 319496 | tf_op jit(solution)/shard_map/cond/branch_1_fun/cond/branch_1_fun/cond/branch_1_fun/ppermute | solution.py:48
  48.5 6.0 %collective-permute-start.1 = (bf16[208,128]{1,0:T(8,128)(2,1)S(1)}, bf16[208,128]{1,0:T(8,128)(2,1)S(1)}, u32[]{:S(2)}, u32[]{:S(2)}) collective-permute-start(bf16[208,128]{1,0:T(8,128)(2,1)S(1)} %add_convert_fusion), channel_id=1, source_target_pairs={{0,2},{1,3},{2,0},{3,1},{4,6},{5,7},{6,4},{7,5},{8,10},{9,11},{10,... | collective-permute-start | bytes 159752 | tf_op jit(solution)/shard_map/cond/branch_1_fun/cond/branch_1_fun/cond/branch_1_fun/ppermute | solution.py:48
  56.3 24.7 %collective-permute-start.2 = (bf16[128,3072]{1,0:T(8,128)(2,1)S(1)}, bf16[128,3072]{1,0:T(8,128)(2,1)}, u32[]{:S(2)}, u32[]{:S(2)}) collective-permute-start(bf16[128,3072]{1,0:T(8,128)(2,1)S(1)} %get-tuple-element.52), channel_id=1, source_target_pairs={{0,16},{16,32},{32,48},{48,64},{64,80},{80,96},{96,112},{112,128},... | collective-permute-start | bytes 2359304 | tf_op jit(solution)/shard_map/cond/branch_1_fun/cond/branch_1_fun/cond/branch_1_fun/ppermute | solution.py:25
  61.2 3.2 %collective-permute-start.3 = (f32[192,128]{1,0:T(8,128)S(1)}, f32[192,128]{1,0:T(8,128)S(1)}, u32[]{:S(2)}, u32[]{:S(2)}) collective-permute-start(f32[192,128]{1,0:T(8,128)S(1)} %get-tuple-element.53), channel_id=1, source_target_pairs={{0,1},{1,0},{2,3},{3,2},{4,5},{5,4},{6,7},{7,6},{8,9},{9,8},{10,11... | collective-permute-start | bytes 294920 | tf_op jit(solution)/shard_map/cond/branch_1_fun/cond/branch_1_fun/cond/branch_1_fun/ppermute | solution.py:48
  64.4 15.2 %collective-permute-start.4 = (bf16[192,128]{1,0:T(8,128)(2,1)S(1)}, bf16[192,128]{1,0:T(8,128)(2,1)S(1)}, u32[]{:S(2)}, u32[]{:S(2)}) collective-permute-start(bf16[192,128]{1,0:T(8,128)(2,1)S(1)} %add_convert_fusion.1), channel_id=1, source_target_pairs={{0,2},{1,3},{2,0},{3,1},{4,6},{5,7},{6,4},{7,5},{8,10},{9,11},{10,... | collective-permute-start | bytes 147464 | tf_op jit(solution)/shard_map/cond/branch_1_fun/cond/branch_1_fun/cond/branch_1_fun/ppermute | solution.py:48
  81.0 10.3 %copy-start.1 = (bf16[128,3072]{1,0:T(8,128)(2,1)S(1)}, bf16[128,3072]{1,0:T(8,128)(2,1)}, u32[]{:S(2)}) copy-start(bf16[128,3072]{1,0:T(8,128)(2,1)} %get-tuple-element.81.cotangent_ref) | copy-start | bytes 2359300 | tf_op jit(solution)/shard_map/cond
  94.6 42.4 %collective-permute-start.9 = (bf16[128,3072]{1,0:T(8,128)(2,1)S(1)}, bf16[128,3072]{1,0:T(8,128)(2,1)S(1)}, u32[]{:S(2)}, u32[]{:S(2)}) collective-permute-start(bf16[128,3072]{1,0:T(8,128)(2,1)S(1)} %get-tuple-element.110), channel_id=1, source_target_pairs={{16,0},{32,16},{48,32},{64,48},{80,64},{96,80},{112,96},{128,112},... | collective-permute-start | bytes 2359304 | tf_op jit(solution)/shard_map/ppermute | solution.py:25
  112.6 21.1 %all-to-all-start.1 = ((bf16[4,48,3200]{2,1,0:T(8,128)(2,1)}), bf16[4,48,3200]{2,1,0:T(8,128)(2,1)S(1)}, u32[]{:S(2)}, u32[]{:S(2)}) async-start(bf16[4,48,3200]{2,1,0:T(8,128)(2,1)} %get-tuple-element.82), calls=%async_computation.1 | async-start | bytes 2457600 | tf_op jit(solution)/shard_map/cond/branch_1_fun/all_to_all | solution.py:289
